TPU v7x, 32 devices: a whole 2x2x4 slice. The times are simulated.
32 devices in a mesh: shard: 8 (over z, x), tensor: 4 (over y, core).
Axes of the slice: x: 2, y: 2, z: 4, core: 2. Of those that a mesh axis runs over, the one named last changes fastest.
Arguments:
- hidden_acts: bfloat16 [2, 2048, 10944], P(None, 'shard', 'tensor'), may hold values from -18 to 18
- out_grads: bfloat16 [2, 2048, 1024], P(None, 'shard'), may hold values from -18 to 18
- sample_idx: int32 [2, 1024], P(None, 'shard'), may hold values from 0 to 255
- grad_weight: bfloat16 [1024, 10944], P('shard', 'tensor'), may hold values from -112 to 112
- momentum: float32 [1024, 10944], P('shard', 'tensor'), may hold values from -6 to 6
- weight: float32 [1024, 10944], P('shard', 'tensor'), may hold values from -6 to 6
Outputs:
- new_momentum: float32 [1024, 10944], P('shard', 'tensor')
- new_weight: float32 [1024, 10944], P('shard', 'tensor')
All inputs are finite; a program needn't handle non-finite values.
Results may differ from a plain program's by a relative error of at most 0.0085.
Values may be sent and summed in bfloat16 or wider, within the bound.
No kernel may reach another device: no remote copies, remote signals or barrier semaphores. Data moves between devices by JAX's collectives and lax.ppermute only.
A program may use at most 128 MiB of HBM per device.

v0:
```python
import jax
import jax.numpy as jnp
from jax import lax
from jax.sharding import PartitionSpec as P

DOUT = 1024
FF = 10944
ABLK = 1368
NS_STEPS = 2


DAMPING = 0.1
CLIP_LEVEL = 0.5
MOMENTUM_RATE = 0.9
LEARN_RATE = 0.5


def spread(value, axis, source):
    kept = jnp.where(lax.axis_index(axis) == source, value, 0).astype(value.dtype)
    return lax.psum(kept, axis)


def round_bf16(value):
    return lax.optimization_barrier(value.astype(jnp.bfloat16)).astype(jnp.float32)


def block_moments(rows, width, scale):
    stacked = rows.reshape(rows.shape[0], rows.shape[1] // width, width)
    moments = jnp.einsum("nkb,nkc->kbc", stacked, stacked, preferred_element_type=jnp.float32)
    return round_bf16(moments * scale)


def newton_inverse(stat):
    width = stat.shape[0]
    shift = DAMPING * jnp.trace(stat) / width
    damped = stat + shift * jnp.eye(width, dtype=jnp.float32)
    normed = (damped / jnp.sqrt(jnp.sum(damped * damped))).astype(jnp.bfloat16)
    iterate = jnp.eye(width, dtype=jnp.bfloat16)
    for step in range(NS_STEPS):
        product = jnp.dot(normed, iterate, preferred_element_type=jnp.float32).astype(jnp.bfloat16)
        twice = 2.0 * iterate.astype(jnp.float32)
        iterate = (twice - jnp.dot(iterate, product, preferred_element_type=jnp.float32)).astype(
            jnp.bfloat16
        )
    return iterate


def empty_inverse(stat):
    return jnp.zeros(stat.shape, jnp.bfloat16)


def per_device(hidden_acts, out_grads, sample_idx, grad_weight, momentum, weight):
    groups = lax.axis_size("shard")
    my_group = lax.axis_index("shard")
    batches, picks = sample_idx.shape
    scale = 1.0 / (batches * picks * groups)
    select = jax.vmap(lambda tokens, where: jnp.take(tokens, where, axis=0))
    picked_acts = select(hidden_acts, sample_idx).reshape(batches * picks, -1)
    picked_grads = select(out_grads, sample_idx).reshape(batches * picks, -1)
    act_part = block_moments(picked_acts, ABLK, scale)
    grad_part = block_moments(picked_grads, DOUT, scale)
    act_blocks = act_part.shape[0]
    stride = groups // (act_blocks + 1)
    grad_owner = act_blocks * stride
    owns_act = my_group == 0
    block = 1
    owns_act = jnp.logical_or(owns_act, my_group == block * stride)
    act_stat, grad_stat = (
        lax.psum(act_part.astype(jnp.bfloat16), "shard").astype(jnp.float32),
        lax.psum(grad_part.astype(jnp.bfloat16), "shard").astype(jnp.float32),
    )
    act_stat = round_bf16(act_stat)
    grad_block = round_bf16(grad_stat[0])
    chosen = act_stat[0]
    block = 1
    chosen = jnp.where(my_group == block * stride, act_stat[block], chosen)
    act_own = lax.cond(owns_act, newton_inverse, empty_inverse, chosen)
    grad_own = lax.cond(my_group == grad_owner, newton_inverse, empty_inverse, grad_block)
    act_inverse = jnp.stack(
        [spread(act_own, "shard", block * stride) for block in range(act_blocks)]
    )
    grad_inverse = spread(grad_own, "shard", grad_owner)
    my_rows = grad_weight.shape[0]
    first_row = my_group * my_rows
    inverse_rows = lax.dynamic_slice_in_dim(grad_inverse, first_row, my_rows, 0)
    start_total = jnp.zeros(grad_weight.shape, jnp.float32)
    piece = lax.all_gather(grad_weight, "shard", axis=0, tiled=True)
    factor_part = lax.slice_in_dim(inverse_rows, 0, piece.shape[0], axis=1)
    left = start_total + jnp.dot(factor_part, piece, preferred_element_type=jnp.float32)
    left = left.astype(jnp.bfloat16)
    hidden_width = left.shape[1]
    left_blocks = left.reshape(my_rows, act_blocks, ABLK)
    update = jnp.einsum(
        "rkb,kbc->rkc", left_blocks, act_inverse, preferred_element_type=jnp.float32
    )
    update = update.reshape(my_rows, hidden_width)
    local_align = jnp.sum(update * grad_weight.astype(jnp.float32))
    alignment = lax.psum(local_align, ("shard", "tensor"))
    ratio = jnp.minimum(1.0, CLIP_LEVEL / jnp.sqrt(alignment / (DOUT * FF)))
    new_momentum = MOMENTUM_RATE * momentum + ratio * update
    new_weight = weight - LEARN_RATE * new_momentum
    return (new_momentum, new_weight)


def solution(mesh):
    in_specs = (
        P(None, "shard", "tensor"),
        P(None, "shard", None),
        P(None, "shard"),
        P("shard", "tensor"),
        P("shard", "tensor"),
        P("shard", "tensor"),
    )
    out_specs = (P("shard", "tensor"), P("shard", "tensor"))
    return jax.shard_map(
        per_device, mesh=mesh, in_specs=in_specs, out_specs=out_specs, check_vma=False
    )
```

profile of v0, /device:TPU:0, one launch (start us, length us, event | category | flops | bytes accessed | tf_op | source)
XLA Modules:
  0.0 809.9 jit_solution(5922410722755919697)
XLA Ops:
  9.4 4.5 copy.14
  13.9 4.8 gather_fusion
  18.7 1.5 copy.15
  20.2 7.3 multiply_convert_fusion
  27.5 2.8 gather_fusion.1
  30.5 2.1 fusion.23
  33.5 311.3 %all-reduce.7.cloned.1.call-done = (bf16[1024,1024]{1,0:T(8,128)(2,1)}, bf16[2,1368,1368]{2,1,0:T(8,128)(2,1)}) async-done(((bf16[1024,1024]{1,0:T(8,128)(2,1)}, bf16[2,1368,1368]{2,1,0:T(8,128)(2,1)}), (bf16[1024,1024]{1,0:T(8,128)(2,1)}, bf16[2,1368,1368]{2,1,0:T(8,128)(2,1)})) %all-reduce.7.cloned.1.call-update) | async-done | bytes 9582864 | tf_op jit(solution)/shard_map/psum | solution.py:70
  344.8 10.0 %convert_element_type.98 = f32[2,1368,1368]{2,1,0:T(8,128)} convert(bf16[2,1368,1368]{2,1,0:T(8,128)(2,1)} %get-tuple-element.27) | non-fusion elementwise | flops 3742848 | bytes 22457088 | tf_op jit(solution)/shard_map/convert_element_type | solution.py:24
  354.8 2.5 convert_element_type.103
  357.3 65.4 %conditional.2 = (bf16[1368,1368]{0,1:T(8,128)(2,1)}) conditional(s32[]{:T(128)} %convert_element_type.96, () %tuple.21, (pred[]{:T(512)}, f32[2,1368,1368]{2,1,0:T(8,128)}) %tuple.22), branch_computations={%region_1.2_spmd, %region_2.5_spmd} | conditional | flops 20533264384 | bytes 67371312 | solution.py:77
  357.3 9.3 %fusion = (f32[]{:T(128)}, f32[1,1368,1368]{2,1,0:T(8,128)}) fusion(f32[2,1368,1368]{2,1,0:T(8,128)} %get-tuple-element.19, pred[]{:T(512)} %get-tuple-element.18), kind=kLoop, calls=%fused_computation.6 | loop fusion | flops 7485695 | bytes 22457092 | tf_op jit(solution)/shard_map/cond/branch_1_fun/jit(trace)/reduce_sum | solution.py:35
  367.2 5.8 multiply_reduce_fusion
  373.6 5.7 divide_convert_fusion
  379.4 17.6 %fusion.4 = bf16[1368,1368]{1,0:T(8,128)(2,1)} fusion(bf16[1368,1368]{1,0:T(8,128)(2,1)} %divide_convert_fusion), kind=kOutput, calls=%fused_computation.15 | convolution fusion | flops 10257275904 | bytes 7485696 | tf_op jit(solution)/shard_map/cond/branch_1_fun/dot_general | solution.py:42
  396.9 19.4 %fusion.5 = bf16[1368,1368]{1,0:T(8,128)(2,1)} fusion(bf16[1368,1368]{1,0:T(8,128)(2,1)} %fusion.4, bf16[1368,1368]{1,0:T(8,128)(2,1)} %divide_convert_fusion), kind=kOutput, calls=%fused_computation.16 | convolution fusion | flops 10249789440 | bytes 11228544 | tf_op jit(solution)/shard_map/cond/branch_1_fun/dot_general | solution.py:42
  416.3 6.2 copy.22
  422.7 4.9 conditional.3
  429.0 5.6 select_bitcast_fusion.1
  434.7 3.0 all-gather.2.cloned.1.call-done
  437.7 313.4 %all-reduce.5.cloned.1.call-done = (bf16[1024,1024]{1,0:T(8,128)(2,1)}, bf16[1,1368,1368]{1,2,0:T(8,128)(2,1)}, bf16[1,1368,1368]{1,2,0:T(8,128)(2,1)}) async-done(((bf16[1024,1024]{1,0:T(8,128)(2,1)}, bf16[1,1368,1368]{1,2,0:T(8,128)(2,1)}, bf16[1,1368,1368]{1,2,0:T(8,128)(2,1)}), (bf16[1024,1024]{1,0:T(8,128)(2,1)}, bf16[1,1368,1368]{1,2,0:T(8,128)(2,1)}, ...) | async-done | bytes 9582864 | tf_op jit(solution)/shard_map/psum | solution.py:20
  751.0 4.4 convolution_convert_fusion.1
  756.0 2.5 fusion.18
  759.5 39.3 %psum.47 = f32[]{:T(128)} all-reduce(f32[]{:T(128)} %fusion.24), channel_id=1, replica_groups=mesh['shard'=8,'tensor'=4] {'shard','tensor'}, use_global_device_ids=true, to_apply=%region_14.15 | all-reduce | flops 1 | bytes 8 | tf_op jit(solution)/shard_map/psum | solution.py:98
  799.5 3.6 multiply_subtract_fusion
  (25 shorter events, 6.5 us)
Async XLA Ops:
  7.2 20.3 %copy-start = (bf16[2,256,1024]{2,1,0:T(8,128)(2,1)S(1)}, bf16[2,256,1024]{2,1,0:T(8,128)(2,1)}, u32[]{:S(2)}) copy-start(bf16[2,256,1024]{2,1,0:T(8,128)(2,1)} %param.11) | copy-start | bytes 3145732
  7.2 337.6 %all-reduce.7.cloned.1.call-start = ((), (), s32[]{:S(2)}) async-start(), calls=%async_computation.2 | async-start | bytes 19603456 | tf_op jit(solution)/shard_map/psum | solution.py:70
  32.7 405.0 %all-gather.2.cloned.1.call-start = ((), (), s32[]{:S(2)}) async-start(), calls=%async_computation | async-start | bytes 6303744 | tf_op jit(solution)/shard_map/all_gather | solution.py:87
  33.4 717.6 %all-reduce.5.cloned.1.call-start = ((), (), s32[]{:S(2)}) async-start(), calls=%async_computation.1 | async-start | bytes 19603456 | tf_op jit(solution)/shard_map/psum | solution.py:20
  344.8 10.0 %copy-start.3 = (bf16[1024,1024]{1,0:T(8,128)(2,1)S(1)}, bf16[1024,1024]{1,0:T(8,128)(2,1)}, u32[]{:S(2)}) copy-start(bf16[1024,1024]{1,0:T(8,128)(2,1)} %get-tuple-element.26) | copy-start | bytes 6291460
  751.0 4.4 copy-start.5
  751.0 5.0 copy-start.6
  756.0 2.5 copy-start.2
  758.5 44.6 %copy-start.1 = (bf16[2,256,1024]{2,1,0:T(8,128)(2,1)S(1)}, bf16[2,256,1024]{2,1,0:T(8,128)(2,1)}, u32[]{:S(2)}) copy-start(bf16[2,256,1024]{2,1,0:T(8,128)(2,1)} %param.11) | copy-start | bytes 3145732
Sparse Core Ops, SparseCore 0:
  32.8 311.9 all-reduce.6
  347.0 90.5 all-gather.1
  442.9 308.0 all-reduce.4
where the time goes:
time: 820 us; the launch traced here: 810 us
  waiting for transfers between devices  628 us (77%)
  matrix products  53.2 us (6%)
  other arithmetic  47.2 us (6%)
  blocking collectives  39.3 us (5%)
  local copies, waits for them, and re-layouts  20.9 us (3%)
  between operations  14.8 us (2%)
    psum x1, waiting for transfers between devices, spread(): return lax.psum(kept, axis)  313 us
    psum x1, waiting for transfers between devices, per_device(): lax.psum(grad_part.astype(jnp.bfloat16), 'shard').astype(jnp.float32)  311 us
    psum x1, blocking collectives, per_device(): alignment = lax.psum(local_align, ('shard', 'tensor'))  39.3 us
    dot_general x2, matrix products, newton_inverse(): jnp.dot(iterate, product, preferred_element_type=jnp.float32)  37 us
  transfers between devices with their start and end apart: 3, of which 3 were waited for; matrix products, arithmetic and copies ran while one was open for 10% of the time, Pallas kernels for 0%

commit v1 on v0

v1 whole, which is shorter than its diff:
```python
import jax
import jax.numpy as jnp
from jax import lax
from jax.sharding import PartitionSpec as P

DOUT = 1024
FF = 10944
ABLK = 1368

DAMPING = 0.1
CLIP_LEVEL = 0.5
MOMENTUM_RATE = 0.9
LEARN_RATE = 0.5

AXES = ("shard", "tensor")


def permute(value, shards, tensors, target):
    pairs = []
    for s in range(shards):
        for t in range(tensors):
            to_s, to_t = target(s, t)
            pairs.append((s * tensors + t, to_s * tensors + to_t))
    return lax.ppermute(value, AXES, pairs)


def pick(tokens, where):
    hot = (where[:, None] == lax.broadcasted_iota(jnp.int32, (where.shape[0], tokens.shape[0]), 1))
    return jnp.dot(hot.astype(jnp.bfloat16), tokens, preferred_element_type=jnp.float32).astype(
        jnp.bfloat16
    )


def pick_transposed(tokens_t, where):
    hot = (where[None, :] == lax.broadcasted_iota(jnp.int32, (tokens_t.shape[1], where.shape[0]), 0))
    return jnp.dot(tokens_t, hot.astype(jnp.bfloat16), preferred_element_type=jnp.float32).astype(
        jnp.bfloat16
    )


def damping_terms(gram):
    width = gram.shape[0]
    trace = jnp.trace(gram)
    shift = DAMPING * trace / width
    total = jnp.sum(gram * gram) + 2.0 * shift * trace + width * shift * shift
    scale = 1.0 / jnp.sqrt(total)
    return scale, shift * scale


def dot_f32(a, b):
    return jnp.dot(a, b, preferred_element_type=jnp.float32)


def per_device(hidden_acts, out_grads, sample_idx, grad_weight, momentum, weight):
    n = lax.axis_size("shard")
    nt = lax.axis_size("tensor")
    batches, picks = sample_idx.shape
    rows, hidden = grad_weight.shape
    blocks = hidden // ABLK
    high = 2 * blocks
    m = n // high
    me = lax.axis_index("shard")
    col = lax.axis_index("tensor")
    core = col % 2
    hi = me // m
    lo = me % m

    def split(s, t):
        return s // m, s % m, t // 2, t % 2

    def send(value, f):
        def target(s, t):
            a, b, y, c = f(*split(s, t))
            return a * m + b, y * 2 + c

        return permute(value, n, nt, target)

    def over_lo(value, d):
        return send(value, lambda h, l, y, c: (h, l ^ d, y, c))

    def over_core(value):
        return send(value, lambda h, l, y, c: (h, l, y, c ^ 1))

    grad_t = grad_weight.T.reshape(blocks, ABLK, rows)
    home = lambda k: (lambda h, l, y, c: (2 * c + ((h ^ k) & 1), l, y, h >> 1))
    w_own = [
        send(lax.dynamic_index_in_dim(grad_t, (hi ^ k) & 1, 0, keepdims=False), home(k))
        for k in range(2)
    ]

    q_rows = batches * picks // nt
    flat_idx = sample_idx.reshape(-1)
    my_idx = lax.dynamic_slice_in_dim(flat_idx, col * q_rows, q_rows, 0)
    my_tokens = lax.dynamic_index_in_dim(
        out_grads, col * q_rows // picks, 0, keepdims=False
    )
    q = pick(my_tokens, my_idx)
    q = [q] + [
        send(q, lambda h, l, y, c, d=d: (h ^ d, l, y, c)) for d in range(1, high)
    ]
    q = jnp.concatenate(q, axis=0)

    acts_t = jnp.swapaxes(hidden_acts, 1, 2)
    picked = jnp.stack([pick_transposed(acts_t[i], sample_idx[i]) for i in range(batches)])
    picked = jnp.swapaxes(picked.reshape(batches, blocks, ABLK, picks), 0, 1)
    picked = picked.reshape(blocks * batches, ABLK, picks)
    spread = lambda k: (lambda h, l, y, c: (blocks * c + ((h ^ k) >> 1), l, y, (h ^ k) & 1))
    z_own = [
        send(lax.dynamic_index_in_dim(picked, hi ^ k, 0, keepdims=False), spread(k))
        for k in range(high)
    ]

    w_lo = w_own + [over_lo(w, d) for d in range(1, m) for w in w_own]
    w_all = w_lo + [over_core(w) for w in w_lo]

    q = jnp.concatenate([q] + [over_lo(q, d) for d in range(1, m)], axis=0)
    for step in range(1, nt // 2):
        pass
    others = [q]
    for d in range(1, nt // 2):
        others.append(send(q, lambda h, l, y, c, d=d: (h, l, y ^ d, c)))
    q = jnp.concatenate(others, axis=0)
    q = jnp.concatenate([q, over_core(q)], axis=0)

    z_lo = z_own + [over_lo(z, d) for d in range(1, m) for z in z_own]
    z_all = jnp.concatenate(z_lo + [over_core(z) for z in z_lo], axis=1)

    count = batches * picks * n
    g_gram = lax.dot_general(
        q, q, (((0,), (0,)), ((), ())), preferred_element_type=jnp.float32
    ) * (1.0 / count)
    g_scale, g_shift = damping_terms(g_gram)
    first = (2 * core + (hi & 1)) * m + lo
    mine = jnp.concatenate(
        [lax.dynamic_slice_in_dim(g_gram, (first ^ (k * m)) * rows, rows, 1) for k in range(2)],
        axis=1,
    )
    place = jnp.concatenate([(first ^ (k * m)) * rows + jnp.arange(rows) for k in range(2)])
    eye = (lax.broadcasted_iota(jnp.int32, (DOUT, 2 * rows), 0) == place[None, :])
    g_damped = g_gram * g_scale + g_shift * jnp.eye(DOUT, dtype=jnp.float32)
    g_norm = g_damped.astype(jnp.bfloat16)
    y1 = mine * g_scale + jnp.where(eye, g_shift, 0.0)
    y2 = dot_f32(g_norm, y1.astype(jnp.bfloat16))
    y3 = dot_f32(g_norm, y2.astype(jnp.bfloat16))
    g_poly = (4.0 * y2 - 6.0 * y1 - y3).astype(jnp.bfloat16).reshape(n, rows, 2 * rows)
    g_poly = jnp.concatenate(
        [lax.dynamic_index_in_dim(g_poly, first ^ r, 0, keepdims=False) for r in
         [dq * 2 * m + k * m + d for dq in range(2) for d in range(m) for k in range(2)]],
        axis=0,
    )
    w_mine = jnp.concatenate(w_own, axis=1).astype(jnp.float32)
    left = 4.0 * w_mine + dot_f32(jnp.concatenate(w_all, axis=1), g_poly)
    left = left.astype(jnp.bfloat16)

    a_gram = lax.dot_general(
        z_all, z_all, (((1,), (1,)), ((), ())), preferred_element_type=jnp.float32
    ) * (1.0 / count)
    a_scale, a_shift = damping_terms(a_gram)
    a_norm = (a_gram * a_scale + a_shift * jnp.eye(ABLK, dtype=jnp.float32)).astype(jnp.bfloat16)
    left_f = left.astype(jnp.float32)
    t1 = 4.0 * left_f - dot_f32(a_norm, left)
    t2 = dot_f32(a_norm, t1.astype(jnp.bfloat16)) - 6.0 * left_f
    update = dot_f32(a_norm, t2.astype(jnp.bfloat16)) + 4.0 * left_f

    total = jnp.sum(update * w_mine).reshape(1, 1)
    sent = update.astype(jnp.bfloat16)
    back = [send(sent[:, k * rows : (k + 1) * rows], home(k)) for k in range(2)]
    total = total + over_core(total)
    for d in [2**i for i in range(10) if 2**i < nt // 2]:
        total = total + send(total, lambda h, l, y, c, d=d: (h, l, y ^ d, c))
    for d in [2**i for i in range(10) if 2**i < m]:
        total = total + over_lo(total, d)
    for d in [2**i for i in range(10) if 2**i < high]:
        total = total + send(total, lambda h, l, y, c, d=d: (h ^ d, l, y, c))
    ratio = jnp.minimum(1.0, CLIP_LEVEL / jnp.sqrt(total[0, 0] / (DOUT * FF)))

    odd = (hi & 1) == 1
    final = jnp.concatenate(
        [jnp.where(odd, back[1 - j], back[j]) for j in range(2)], axis=0
    ).astype(jnp.float32)
    new_momentum = MOMENTUM_RATE * momentum.T + ratio * final
    new_weight = weight.T - LEARN_RATE * new_momentum
    return (new_momentum.T, new_weight.T)


def solution(mesh):
    in_specs = (
        P(None, "shard", "tensor"),
        P(None, "shard", None),
        P(None, "shard"),
        P("shard", "tensor"),
        P("shard", "tensor"),
        P("shard", "tensor"),
    )
    out_specs = (P("shard", "tensor"), P("shard", "tensor"))
    return jax.shard_map(
        per_device, mesh=mesh, in_specs=in_specs, out_specs=out_specs, check_vma=False
    )
```

time: 820 us -> 231 us (0.28); the launches traced: 810 us -> 230 us
  waiting for transfers between devices: 628 us -> 70.5 us
  starting transfers between devices: 0.12 us -> 66.3 us
  other arithmetic: 47.2 us -> 3.53 us
  blocking collectives: 39.3 us -> 0 us
    psum x2 -> x0, waiting for transfers between devices: 625 us -> none  [the longest x1 313 us: spread(): return lax.psum(kept, axis)]
    ppermute x0 -> x37, waiting for transfers between devices: none -> 70.5 us  [permute(): return lax.ppermute(value, AXES, pairs)]
    ppermute x0 -> x37, starting transfers between devices: none -> 66.3 us  [permute(): return lax.ppermute(value, AXES, pairs)]
    psum x1 -> x0, blocking collectives: 39.3 us -> none  [per_device(): alignment = lax.psum(local_align, ('shard', 'tensor'))]
    convert_element_type x3 -> x0, other arithmetic: 18.2 us -> none  [the longest x2 12.5 us: round_bf16(): lax.optimization_barrier(value.astype(jnp.bfloat16)).astype(jnp.float32)]
    reduce_sum x3 -> x0, other arithmetic: 16.1 us -> none  [the longest x1 9.34 us: newton_inverse(): shift = DAMPING * jnp.trace(stat) / width]
    gather x4 -> x0, local copies, waits for them, and re-layouts: 9.35 us -> none  [per_device(): select = jax.vmap(lambda tokens, where: jnp.take(tokens, where, axis=0))]
    dot_general x6 -> x10, matrix products: 53.2 us -> 53.4 us  [the longest x5 25 us: dot_f32(): return jnp.dot(a, b, preferred_element_type=jnp.float32)]
  transfers between devices with their start and end apart: 3 -> 37, of which waited for: 3 -> 17; matrix products, arithmetic and copies ran while one was open for 10% -> 14% of each run, Pallas kernels for 0% -> 0%
where the time goes in v1:
time: 231 us; the launch traced here: 230 us
  waiting for transfers between devices  70.5 us (31%)
  starting transfers between devices  66.3 us (29%)
  matrix products  53.4 us (23%)
  local copies, waits for them, and re-layouts  23.4 us (10%)
  between operations  12.6 us (5%)
  other arithmetic  3.53 us (2%)
    ppermute x37, waiting for transfers between devices, permute(): return lax.ppermute(value, AXES, pairs)  70.5 us
    ppermute x37, starting transfers between devices, permute(): return lax.ppermute(value, AXES, pairs)  66.3 us
    dot_general x5, matrix products, dot_f32(): return jnp.dot(a, b, preferred_element_type=jnp.float32)  25 us
    unnamed x47, local copies, waits for them, and re-layouts  12 us
    dot_general x1, matrix products, per_device(): lax.dot_general(q, q, (((0,), (0,)), ((), ())), preferred_element_type=jn...  11.9 us
    dot_general x1, matrix products, per_device(): lax.dot_general(z_all, z_all, (((1,), (1,)), ((), ())), preferred_element...  11.8 us
  transfers between devices with their start and end apart: 37, of which 17 were waited for; matrix products, arithmetic and copies ran while one was open for 14% of the time, Pallas kernels for 0%

profile of v1, /device:TPU:0, one launch (start us, length us, event | category | flops | bytes accessed | tf_op | source)
XLA Modules:
  0.0 229.8 jit_solution(7283553415386080236)
XLA Ops:
  2.9 3.0 %collective-permute-start.24 = (bf16[64,1024]{1,0:T(8,128)(2,1)S(1)}, bf16[64,1024]{1,0:T(8,128)(2,1)S(1)}, u32[]{:S(2)}, u32[]{:S(2)}) collective-permute-start(bf16[64,1024]{1,0:T(8,128)(2,1)S(1)} %get-tuple-element.42), channel_id=1, source_target_pairs={{0,8},{1,9},{2,10},{3,11},{4,12},{5,13},{6,14},{7,15},{8,0},{9,1},... | collective-permute-start | bytes 393224 | tf_op jit(solution)/shard_map/ppermute | solution.py:24
  20.3 6.5 %collective-permute-start.1 = (bf16[1368,128]{1,0:T(8,128)(2,1)}, bf16[1368,128]{1,0:T(8,128)(2,1)S(1)}, u32[]{:S(2)}, u32[]{:S(2)}) collective-permute-start(bf16[1368,128]{1,0:T(8,128)(2,1)} %get-tuple-element.15), channel_id=1, source_target_pairs={{0,1},{1,17},{2,3},{3,19},{4,5},{5,21},{6,7},{7,23},{8,0},{9,16},{... | collective-permute-start | bytes 1050632 | tf_op jit(solution)/shard_map/ppermute | solution.py:24
  27.6 12.2 %collective-permute-start.2 = (bf16[1368,128]{1,0:T(8,128)(2,1)}, bf16[1368,128]{1,0:T(8,128)(2,1)S(1)}, u32[]{:S(2)}, u32[]{:S(2)}) collective-permute-start(bf16[1368,128]{1,0:T(8,128)(2,1)} %get-tuple-element.14), channel_id=1, source_target_pairs={{0,8},{1,24},{2,10},{3,26},{4,12},{5,28},{6,14},{7,30},{8,9},{9,25... | collective-permute-start | bytes 1050632 | tf_op jit(solution)/shard_map/ppermute | solution.py:24
  40.6 7.2 %collective-permute-start.3 = (bf16[1368,128]{1,0:T(8,128)(2,1)}, bf16[1368,128]{1,0:T(8,128)(2,1)S(1)}, u32[]{:S(2)}, u32[]{:S(2)}) collective-permute-start(bf16[1368,128]{1,0:T(8,128)(2,1)} %get-tuple-element.13), channel_id=1, source_target_pairs={{0,9},{1,25},{2,11},{3,27},{4,13},{5,29},{6,15},{7,31},{8,8},{9,24... | collective-permute-start | bytes 1050632 | tf_op jit(solution)/shard_map/ppermute | solution.py:24
  54.0 7.5 %collective-permute-done.2 = bf16[1368,128]{1,0:T(8,128)(2,1)S(1)} collective-permute-done((bf16[1368,128]{1,0:T(8,128)(2,1)}, bf16[1368,128]{1,0:T(8,128)(2,1)S(1)}, u32[]{:S(2)}, u32[]{:S(2)}) %collective-permute-start.2) | collective-permute-done | bytes 350240 | tf_op jit(solution)/shard_map/ppermute | solution.py:24
  61.6 3.4 %collective-permute-start.21 = (bf16[1368,128]{1,0:T(8,128)(2,1)}, bf16[1368,128]{1,0:T(8,128)(2,1)S(1)}, u32[]{:S(2)}, u32[]{:S(2)}) collective-permute-start(bf16[1368,128]{1,0:T(8,128)(2,1)} %collective-permute-done.17), channel_id=1, source_target_pairs={{0,1},{1,0},{2,3},{3,2},{4,5},{5,4},{6,7},{7,6},{8,9},{9,8},{10,11... | collective-permute-start | bytes 1050632 | tf_op jit(solution)/shard_map/ppermute | solution.py:24
  68.0 3.2 %collective-permute-done.18 = bf16[1368,128]{1,0:T(8,128)(2,1)S(1)} collective-permute-done((bf16[1368,128]{1,0:T(8,128)(2,1)}, bf16[1368,128]{1,0:T(8,128)(2,1)S(1)}, u32[]{:S(2)}, u32[]{:S(2)}) %collective-permute-start.18) | collective-permute-done | bytes 350240 | tf_op jit(solution)/shard_map/ppermute | solution.py:24
  72.8 6.0 %collective-permute-done.19 = bf16[1368,128]{1,0:T(8,128)(2,1)} collective-permute-done((bf16[1368,128]{1,0:T(8,128)(2,1)}, bf16[1368,128]{1,0:T(8,128)(2,1)}, u32[]{:S(2)}, u32[]{:S(2)}) %collective-permute-start.19) | collective-permute-done | bytes 350240 | tf_op jit(solution)/shard_map/ppermute | solution.py:24
  82.3 3.9 %collective-permute-done.4 = bf16[1368,128]{1,0:T(8,128)(2,1)S(1)} collective-permute-done((bf16[1368,128]{1,0:T(8,128)(2,1)S(1)}, bf16[1368,128]{1,0:T(8,128)(2,1)S(1)}, u32[]{:S(2)}, u32[]{:S(2)}) %collective-permute-start.4) | collective-permute-done | bytes 350240 | tf_op jit(solution)/shard_map/ppermute | solution.py:24
  86.3 7.4 %collective-permute-done.5 = bf16[1368,128]{1,0:T(8,128)(2,1)S(1)} collective-permute-done((bf16[1368,128]{1,0:T(8,128)(2,1)S(1)}, bf16[1368,128]{1,0:T(8,128)(2,1)S(1)}, u32[]{:S(2)}, u32[]{:S(2)}) %collective-permute-start.5) | collective-permute-done | bytes 350240 | tf_op jit(solution)/shard_map/ppermute | solution.py:24
  93.8 7.4 %collective-permute-done.6 = bf16[1368,128]{1,0:T(8,128)(2,1)S(1)} collective-permute-done((bf16[1368,128]{1,0:T(8,128)(2,1)S(1)}, bf16[1368,128]{1,0:T(8,128)(2,1)S(1)}, u32[]{:S(2)}, u32[]{:S(2)}) %collective-permute-start.6) | collective-permute-done | bytes 350240 | tf_op jit(solution)/shard_map/ppermute | solution.py:24
  101.3 7.0 %collective-permute-done.7 = bf16[1368,128]{1,0:T(8,128)(2,1)S(1)} collective-permute-done((bf16[1368,128]{1,0:T(8,128)(2,1)S(1)}, bf16[1368,128]{1,0:T(8,128)(2,1)S(1)}, u32[]{:S(2)}, u32[]{:S(2)}) %collective-permute-start.7) | collective-permute-done | bytes 350240 | tf_op jit(solution)/shard_map/ppermute | solution.py:24
  115.0 18.1 %collective-permute-done.28 = bf16[512,1024]{1,0:T(8,128)(2,1)S(1)} collective-permute-done((bf16[512,1024]{1,0:T(8,128)(2,1)S(1)}, bf16[512,1024]{1,0:T(8,128)(2,1)S(1)}, u32[]{:S(2)}, u32[]{:S(2)}) %collective-permute-start.28) | collective-permute-done | bytes 1048608 | tf_op jit(solution)/shard_map/ppermute | solution.py:24
  134.7 11.8 %multiply_reduce_fusion = (f32[]{:T(128)}, f32[]{:T(128)}, f32[1368,1368]{1,0:T(8,128)}) fusion(bf16[1368,2048]{1,0:T(8,128)(2,1)S(1)} %constant_dynamic-update-slice_fusion), kind=kOutput, calls=%fused_computation.3 | convolution fusion | flops 7676580864 | bytes 13089032 | tf_op jit(solution)/shard_map/dot_general | solution.py:155
  155.5 11.9 %multiply_reduce_fusion.1 = (f32[]{:T(128)}, f32[]{:T(128)}, f32[1024,1024]{0,1:T(8,128)}, f32[1024,1024]{0,1:T(8,128)}) fusion(bf16[2048,1024]{1,0:T(8,128)(2,1)} %constant_dynamic-update-slice_fusion.35), kind=kOutput, calls=%fused_computation.7 | convolution fusion | flops 4301258752 | bytes 12582920 | tf_op jit(solution)/shard_map/dot_general | solution.py:129
  172.7 3.3 %fusion.14 = f32[1024,256]{1,0:T(8,128)S(1)} fusion(f32[1024,128]{0,1:T(8,128)S(1)} %get-tuple-element.8, f32[1024,128]{0,1:T(8,128)S(1)} %get-tuple-element.7, f32[]{:T(128)S(6)} %mul.179, s32[256]{0:T(256)S(1)} %pad_add_fusion, f32[]{:T(128)S(6)} %sqrt.10, f32[1024,1024]{0,1:T(8,128)} %get-tuple-element.43, f32[]{:T(128)S(6)} %mul.176), kind=kOutput, calls=%fused_computation.41 | convolution fusion | flops 543686656 | bytes 6292492 | tf_op jit(solution)/shard_map/dot_general | solution.py:51
  176.3 3.2 %fusion.6 = bf16[1024,256]{0,1:T(8,128)(2,1)S(1)} fusion(f32[1024,256]{0,1:T(8,128)S(1)} %copy.12, f32[1024,128]{0,1:T(8,128)} %copy-done.3, f32[1024,128]{0,1:T(8,128)S(1)} %get-tuple-element.7, f32[1024,256]{1,0:T(8,128)S(1)} %fusion.14, f32[]{:T(128)S(6)} %mul.179, s32[256]{0:T(256)S(1)} %pad_add_fusion, f32[]{:T(128)S(6)} %sqrt.10, ...), kind=kOutput, calls=%fused_computation.30 | convolution fusion | flops 544997376 | bytes 7865356 | tf_op jit(solution)/shard_map/dot_general | solution.py:51
  183.6 4.5 %fusion.1 = bf16[1368,256]{1,0:T(8,128)(2,1)S(1)} fusion(bf16[1368,256]{1,0:T(8,128)(2,1)S(1)} %fusion, f32[1368,1368]{1,0:T(8,128)} %get-tuple-element.44, f32[]{:T(128)S(6)} %mul.164, f32[]{:T(128)S(6)} %mul.161), kind=kOutput, calls=%fused_computation.14 | convolution fusion | flops 968927040 | bytes 8886536 | tf_op jit(solution)/shard_map/dot_general | solution.py:51
  188.1 11.2 %fusion.34 = (bf16[1368,256]{1,0:T(8,128)(2,1)S(1)}, f32[]{:T(128)}) fusion(bf16[1368,128]{1,0:T(8,128)(2,1)} %collective-permute-done.17, bf16[1368,128]{1,0:T(8,128)(2,1)} %collective-permute-done.16, bf16[1368,256]{1,0:T(8,128)(2,1)} %copy-done.6, bf16[1368,256]{1,0:T(8,128)(2,1)S(1)} %fusion.1, f32[1368,1368]{1,0:T(8,128)} %get-tuple-element.44, ...), kind=kOutput, calls=%fused_computation.128 | convolution fusion | flops 1939955328 | bytes 10287372 | tf_op jit(solution)/shard_map/dot_general | solution.py:51
  203.2 2.9 %collective-permute-start.30 = (f32[1,1]{1,0:T(1,128)}, f32[1,1]{1,0:T(1,128)}, u32[]{:S(2)}, u32[]{:S(2)}) collective-permute-start(f32[1,1]{1,0:T(1,128)} %bitcast.34), channel_id=1, source_target_pairs={{0,1},{1,0},{2,3},{3,2},{4,5},{5,4},{6,7},{7,6},{8,9},{9,8},{10,11... | collective-permute-start | bytes 20 | tf_op jit(solution)/shard_map/ppermute | solution.py:24
  208.4 2.9 %collective-permute-start.31 = (f32[1,1]{1,0:T(1,128)}, f32[1,1]{1,0:T(1,128)}, u32[]{:S(2)}, u32[]{:S(2)}) collective-permute-start(f32[1,1]{1,0:T(1,128)} %add.165), channel_id=1, source_target_pairs={{0,2},{1,3},{2,0},{3,1},{4,6},{5,7},{6,4},{7,5},{8,10},{9,11},{10,... | collective-permute-start | bytes 20 | tf_op jit(solution)/shard_map/ppermute | solution.py:24
  212.6 2.9 %collective-permute-start.32 = (f32[1,1]{1,0:T(1,128)}, f32[1,1]{1,0:T(1,128)}, u32[]{:S(2)}, u32[]{:S(2)}) collective-permute-start(f32[1,1]{1,0:T(1,128)} %add.166), channel_id=1, source_target_pairs={{0,4},{1,5},{2,6},{3,7},{4,0},{5,1},{6,2},{7,3},{8,12},{9,13},{10,... | collective-permute-start | bytes 20 | tf_op jit(solution)/shard_map/ppermute | solution.py:24
  222.7 3.1 %collective-permute-done.34 = f32[1,1]{1,0:T(1,128)} collective-permute-done((f32[1,1]{1,0:T(1,128)}, f32[1,1]{1,0:T(1,128)}, u32[]{:S(2)}, u32[]{:S(2)}) %collective-permute-start.34) | collective-permute-done | bytes 36 | tf_op jit(solution)/shard_map/ppermute | solution.py:24
  226.5 3.2 %fusion.5 = (f32[128,2736]{0,1:T(8,128)}, f32[128,2736]{0,1:T(8,128)}) fusion(f32[128,2736]{0,1:T(8,128)S(1)} %copy-done.2, f32[128,2736]{0,1:T(8,128)} %param.10, f32[]{:T(128)} %bitcast.35, bf16[1368,128]{1,0:T(8,128)(2,1)S(1)} %get-tuple-element.20, bf16[1368,128]{1,0:T(8,128)(2,1)S(1)} %get-tuple-element.19), kind=kLoop, calls=%fused_computation.27 | loop fusion | flops 3151872 | bytes 6303748 | tf_op jit(solution)/shard_map/transpose | solution.py:183
  (126 shorter events, 63.5 us)
Async XLA Ops:
  8.5 19.1 %collective-permute-start.26 = (bf16[64,1024]{1,0:T(8,128)(2,1)S(1)}, bf16[64,1024]{1,0:T(8,128)(2,1)S(1)}, u32[]{:S(2)}, u32[]{:S(2)}) collective-permute-start(bf16[64,1024]{1,0:T(8,128)(2,1)S(1)} %get-tuple-element.42), channel_id=1, source_target_pairs={{0,24},{1,25},{2,26},{3,27},{4,28},{5,29},{6,30},{7,31},{8,16},{9,... | collective-permute-start | bytes 393224 | tf_op jit(solution)/shard_map/ppermute | solution.py:24
  9.6 40.9 %collective-permute-start.17 = (bf16[1368,128]{1,0:T(8,128)(2,1)S(1)}, bf16[1368,128]{1,0:T(8,128)(2,1)}, u32[]{:S(2)}, u32[]{:S(2)}) collective-permute-start(bf16[1368,128]{1,0:T(8,128)(2,1)S(1)} %get-tuple-element.23), channel_id=1, source_target_pairs={{0,8},{1,24},{2,10},{3,26},{4,12},{5,28},{6,14},{7,30},{8,0},{9,16... | collective-permute-start | bytes 1050632 | tf_op jit(solution)/shard_map/ppermute | solution.py:24
  10.6 30.0 %collective-permute-start.16 = (bf16[1368,128]{1,0:T(8,128)(2,1)S(1)}, bf16[1368,128]{1,0:T(8,128)(2,1)}, u32[]{:S(2)}, u32[]{:S(2)}) collective-permute-start(bf16[1368,128]{1,0:T(8,128)(2,1)S(1)} %get-tuple-element.24), channel_id=1, source_target_pairs={{0,0},{1,16},{2,2},{3,18},{4,4},{5,20},{6,6},{7,22},{8,8},{9,24},{... | collective-permute-start | bytes 1050632 | tf_op jit(solution)/shard_map/ppermute | solution.py:24
  17.8 31.1 %collective-permute-start = (bf16[1368,128]{1,0:T(8,128)(2,1)}, bf16[1368,128]{1,0:T(8,128)(2,1)S(1)}, u32[]{:S(2)}, u32[]{:S(2)}) collective-permute-start(bf16[1368,128]{1,0:T(8,128)(2,1)} %get-tuple-element.16), channel_id=1, source_target_pairs={{0,0},{1,16},{2,2},{3,18},{4,4},{5,20},{6,6},{7,22},{8,1},{9,17},{... | collective-permute-start | bytes 1050632 | tf_op jit(solution)/shard_map/ppermute | solution.py:24
  20.3 32.0 %collective-permute-start.1 = (bf16[1368,128]{1,0:T(8,128)(2,1)}, bf16[1368,128]{1,0:T(8,128)(2,1)S(1)}, u32[]{:S(2)}, u32[]{:S(2)}) collective-permute-start(bf16[1368,128]{1,0:T(8,128)(2,1)} %get-tuple-element.15), channel_id=1, source_target_pairs={{0,1},{1,17},{2,3},{3,19},{4,5},{5,21},{6,7},{7,23},{8,0},{9,16},{... | collective-permute-start | bytes 1050632 | tf_op jit(solution)/shard_map/ppermute | solution.py:24
  27.6 33.9 %collective-permute-start.2 = (bf16[1368,128]{1,0:T(8,128)(2,1)}, bf16[1368,128]{1,0:T(8,128)(2,1)S(1)}, u32[]{:S(2)}, u32[]{:S(2)}) collective-permute-start(bf16[1368,128]{1,0:T(8,128)(2,1)} %get-tuple-element.14), channel_id=1, source_target_pairs={{0,8},{1,24},{2,10},{3,26},{4,12},{5,28},{6,14},{7,30},{8,9},{9,25... | collective-permute-start | bytes 1050632 | tf_op jit(solution)/shard_map/ppermute | solution.py:24
  40.6 21.0 %collective-permute-start.3 = (bf16[1368,128]{1,0:T(8,128)(2,1)}, bf16[1368,128]{1,0:T(8,128)(2,1)S(1)}, u32[]{:S(2)}, u32[]{:S(2)}) collective-permute-start(bf16[1368,128]{1,0:T(8,128)(2,1)} %get-tuple-element.13), channel_id=1, source_target_pairs={{0,9},{1,25},{2,11},{3,27},{4,13},{5,29},{6,15},{7,31},{8,8},{9,24... | collective-permute-start | bytes 1050632 | tf_op jit(solution)/shard_map/ppermute | solution.py:24
  50.6 20.6 %collective-permute-start.18 = (bf16[1368,128]{1,0:T(8,128)(2,1)}, bf16[1368,128]{1,0:T(8,128)(2,1)S(1)}, u32[]{:S(2)}, u32[]{:S(2)}) collective-permute-start(bf16[1368,128]{1,0:T(8,128)(2,1)} %collective-permute-done.16), channel_id=1, source_target_pairs={{0,4},{1,5},{2,6},{3,7},{4,0},{5,1},{6,2},{7,3},{8,12},{9,13},{10,... | collective-permute-start | bytes 1050632 | tf_op jit(solution)/shard_map/ppermute | solution.py:24
  52.3 26.5 %collective-permute-start.19 = (bf16[1368,128]{1,0:T(8,128)(2,1)}, bf16[1368,128]{1,0:T(8,128)(2,1)}, u32[]{:S(2)}, u32[]{:S(2)}) collective-permute-start(bf16[1368,128]{1,0:T(8,128)(2,1)} %collective-permute-done.17), channel_id=1, source_target_pairs={{0,4},{1,5},{2,6},{3,7},{4,0},{5,1},{6,2},{7,3},{8,12},{9,13},{10,... | collective-permute-start | bytes 1050632 | tf_op jit(solution)/shard_map/ppermute | solution.py:24
  61.5 19.9 %collective-permute-start.20 = (bf16[1368,128]{1,0:T(8,128)(2,1)}, bf16[1368,128]{1,0:T(8,128)(2,1)S(1)}, u32[]{:S(2)}, u32[]{:S(2)}) collective-permute-start(bf16[1368,128]{1,0:T(8,128)(2,1)} %collective-permute-done.16), channel_id=1, source_target_pairs={{0,1},{1,0},{2,3},{3,2},{4,5},{5,4},{6,7},{7,6},{8,9},{9,8},{10,11... | collective-permute-start | bytes 1050632 | tf_op jit(solution)/shard_map/ppermute | solution.py:24
  61.6 20.5 %collective-permute-start.21 = (bf16[1368,128]{1,0:T(8,128)(2,1)}, bf16[1368,128]{1,0:T(8,128)(2,1)S(1)}, u32[]{:S(2)}, u32[]{:S(2)}) collective-permute-start(bf16[1368,128]{1,0:T(8,128)(2,1)} %collective-permute-done.17), channel_id=1, source_target_pairs={{0,1},{1,0},{2,3},{3,2},{4,5},{5,4},{6,7},{7,6},{8,9},{9,8},{10,11... | collective-permute-start | bytes 1050632 | tf_op jit(solution)/shard_map/ppermute | solution.py:24
  65.2 21.0 %collective-permute-start.4 = (bf16[1368,128]{1,0:T(8,128)(2,1)S(1)}, bf16[1368,128]{1,0:T(8,128)(2,1)S(1)}, u32[]{:S(2)}, u32[]{:S(2)}) collective-permute-start(bf16[1368,128]{1,0:T(8,128)(2,1)S(1)} %collective-permute-done), channel_id=1, source_target_pairs={{0,4},{1,5},{2,6},{3,7},{4,0},{5,1},{6,2},{7,3},{8,12},{9,13},{10,... | collective-permute-start | bytes 1050632 | tf_op jit(solution)/shard_map/ppermute | solution.py:24
  71.2 22.5 %collective-permute-start.5 = (bf16[1368,128]{1,0:T(8,128)(2,1)S(1)}, bf16[1368,128]{1,0:T(8,128)(2,1)S(1)}, u32[]{:S(2)}, u32[]{:S(2)}) collective-permute-start(bf16[1368,128]{1,0:T(8,128)(2,1)S(1)} %collective-permute-done.1), channel_id=1, source_target_pairs={{0,4},{1,5},{2,6},{3,7},{4,0},{5,1},{6,2},{7,3},{8,12},{9,13},{10,... | collective-permute-start | bytes 1050632 | tf_op jit(solution)/shard_map/ppermute | solution.py:24
  78.8 22.4 %collective-permute-start.6 = (bf16[1368,128]{1,0:T(8,128)(2,1)S(1)}, bf16[1368,128]{1,0:T(8,128)(2,1)S(1)}, u32[]{:S(2)}, u32[]{:S(2)}) collective-permute-start(bf16[1368,128]{1,0:T(8,128)(2,1)S(1)} %collective-permute-done.2), channel_id=1, source_target_pairs={{0,4},{1,5},{2,6},{3,7},{4,0},{5,1},{6,2},{7,3},{8,12},{9,13},{10,... | collective-permute-start | bytes 1050632 | tf_op jit(solution)/shard_map/ppermute | solution.py:24
  81.4 26.9 %collective-permute-start.7 = (bf16[1368,128]{1,0:T(8,128)(2,1)S(1)}, bf16[1368,128]{1,0:T(8,128)(2,1)S(1)}, u32[]{:S(2)}, u32[]{:S(2)}) collective-permute-start(bf16[1368,128]{1,0:T(8,128)(2,1)S(1)} %collective-permute-done.3), channel_id=1, source_target_pairs={{0,4},{1,5},{2,6},{3,7},{4,0},{5,1},{6,2},{7,3},{8,12},{9,13},{10,... | collective-permute-start | bytes 1050632 | tf_op jit(solution)/shard_map/ppermute | solution.py:24
  82.1 27.9 %collective-permute-start.8 = (bf16[1368,128]{1,0:T(8,128)(2,1)S(1)}, bf16[1368,128]{1,0:T(8,128)(2,1)S(1)}, u32[]{:S(2)}, u32[]{:S(2)}) collective-permute-start(bf16[1368,128]{1,0:T(8,128)(2,1)S(1)} %collective-permute-done), channel_id=1, source_target_pairs={{0,1},{1,0},{2,3},{3,2},{4,5},{5,4},{6,7},{7,6},{8,9},{9,8},{10,11... | collective-permute-start | bytes 1050632 | tf_op jit(solution)/shard_map/ppermute | solution.py:24
  86.2 24.0 %collective-permute-start.9 = (bf16[1368,128]{1,0:T(8,128)(2,1)S(1)}, bf16[1368,128]{1,0:T(8,128)(2,1)S(1)}, u32[]{:S(2)}, u32[]{:S(2)}) collective-permute-start(bf16[1368,128]{1,0:T(8,128)(2,1)S(1)} %collective-permute-done.1), channel_id=1, source_target_pairs={{0,1},{1,0},{2,3},{3,2},{4,5},{5,4},{6,7},{7,6},{8,9},{9,8},{10,11... | collective-permute-start | bytes 1050632 | tf_op jit(solution)/shard_map/ppermute | solution.py:24
  93.7 17.2 %collective-permute-start.10 = (bf16[1368,128]{1,0:T(8,128)(2,1)S(1)}, bf16[1368,128]{1,0:T(8,128)(2,1)S(1)}, u32[]{:S(2)}, u32[]{:S(2)}) collective-permute-start(bf16[1368,128]{1,0:T(8,128)(2,1)S(1)} %collective-permute-done.2), channel_id=1, source_target_pairs={{0,1},{1,0},{2,3},{3,2},{4,5},{5,4},{6,7},{7,6},{8,9},{9,8},{10,11... | collective-permute-start | bytes 1050632 | tf_op jit(solution)/shard_map/ppermute | solution.py:24
  108.3 24.8 %collective-permute-start.28 = (bf16[512,1024]{1,0:T(8,128)(2,1)S(1)}, bf16[512,1024]{1,0:T(8,128)(2,1)S(1)}, u32[]{:S(2)}, u32[]{:S(2)}) collective-permute-start(bf16[512,1024]{1,0:T(8,128)(2,1)S(1)} %get-tuple-element.27), channel_id=1, source_target_pairs={{0,2},{1,3},{2,0},{3,1},{4,6},{5,7},{6,4},{7,5},{8,10},{9,11},{10,... | collective-permute-start | bytes 3145736 | tf_op jit(solution)/shard_map/ppermute | solution.py:24
  110.0 40.5 %collective-permute-start.22 = (bf16[1368,128]{1,0:T(8,128)(2,1)S(1)}, bf16[1368,128]{1,0:T(8,128)(2,1)}, u32[]{:S(2)}, u32[]{:S(2)}) collective-permute-start(bf16[1368,128]{1,0:T(8,128)(2,1)S(1)} %collective-permute-done.18), channel_id=1, source_target_pairs={{0,1},{1,0},{2,3},{3,2},{4,5},{5,4},{6,7},{7,6},{8,9},{9,8},{10,11... | collective-permute-start | bytes 1050632 | tf_op jit(solution)/shard_map/ppermute | solution.py:24
  110.2 42.1 %collective-permute-start.23 = (bf16[1368,128]{1,0:T(8,128)(2,1)}, bf16[1368,128]{1,0:T(8,128)(2,1)}, u32[]{:S(2)}, u32[]{:S(2)}) collective-permute-start(bf16[1368,128]{1,0:T(8,128)(2,1)} %collective-permute-done.19), channel_id=1, source_target_pairs={{0,1},{1,0},{2,3},{3,2},{4,5},{5,4},{6,7},{7,6},{8,9},{9,8},{10,11... | collective-permute-start | bytes 1050632 | tf_op jit(solution)/shard_map/ppermute | solution.py:24
  134.7 19.3 %collective-permute-start.29 = (bf16[1024,1024]{1,0:T(8,128)(2,1)}, bf16[1024,1024]{1,0:T(8,128)(2,1)S(1)}, u32[]{:S(2)}, u32[]{:S(2)}) collective-permute-start(bf16[1024,1024]{1,0:T(8,128)(2,1)} %get-tuple-element.17), channel_id=1, source_target_pairs={{0,1},{1,0},{2,3},{3,2},{4,5},{5,4},{6,7},{7,6},{8,9},{9,8},{10,11... | collective-permute-start | bytes 6291464 | tf_op jit(solution)/shard_map/ppermute | solution.py:24
  200.0 26.3 %collective-permute-start.35 = (bf16[1368,128]{1,0:T(8,128)(2,1)}, bf16[1368,128]{1,0:T(8,128)(2,1)S(1)}, u32[]{:S(2)}, u32[]{:S(2)}) collective-permute-start(bf16[1368,128]{1,0:T(8,128)(2,1)} %get-tuple-element.21), channel_id=1, source_target_pairs={{0,8},{1,24},{2,10},{3,26},{4,12},{5,28},{6,14},{7,30},{8,0},{9,16... | collective-permute-start | bytes 1050632 | tf_op jit(solution)/shard_map/ppermute | solution.py:24
  202.5 23.9 %collective-permute-start.36 = (bf16[1368,128]{1,0:T(8,128)(2,1)S(1)}, bf16[1368,128]{1,0:T(8,128)(2,1)S(1)}, u32[]{:S(2)}, u32[]{:S(2)}) collective-permute-start(bf16[1368,128]{1,0:T(8,128)(2,1)S(1)} %get-tuple-element.22), channel_id=1, source_target_pairs={{0,0},{1,16},{2,2},{3,18},{4,4},{5,20},{6,6},{7,22},{8,8},{9,24},{... | collective-permute-start | bytes 1050632 | tf_op jit(solution)/shard_map/ppermute | solution.py:24
  (20 other events, 215.7 us)

commit v2 on v1

v2 whole, which is shorter than its diff:
```python
import functools

import jax
import jax.numpy as jnp
from jax import lax
from jax.experimental import pallas as pl
from jax.experimental.pallas import tpu as pltpu
from jax.sharding import PartitionSpec as P

DOUT = 1024
FF = 10944
ABLK = 1368

DAMPING = 0.1
CLIP_LEVEL = 0.5
MOMENTUM_RATE = 0.9
LEARN_RATE = 0.5

AXES = ("shard", "tensor")


def route(shards, tensors, target):
    pairs = []
    for s in range(shards):
        for t in range(tensors):
            to = target(s, t)
            if to is not None:
                pairs.append((s * tensors + t, to[0] * tensors + to[1]))
    return pairs


def pick(tokens, where):
    hot = (where[:, None] == lax.broadcasted_iota(jnp.int32, (where.shape[0], tokens.shape[0]), 1))
    return jnp.dot(hot.astype(jnp.bfloat16), tokens, preferred_element_type=jnp.float32).astype(
        jnp.bfloat16
    )


def pick_transposed(tokens_t, where):
    hot = (where[None, :] == lax.broadcasted_iota(jnp.int32, (tokens_t.shape[1], where.shape[0]), 0))
    return jnp.dot(tokens_t, hot.astype(jnp.bfloat16), preferred_element_type=jnp.float32).astype(
        jnp.bfloat16
    )


def row_tiles(width, limit):
    count = -(-width // limit)
    size = -(-width // (count * 16)) * 16
    return [(at, min(size, width - at)) for at in range(0, width, size)]


def dot_nt(a, b):
    return lax.dot_general(a, b, (((1,), (1,)), ((), ())), preferred_element_type=jnp.float32)


def dot_nn(a, b):
    return jnp.dot(a, b, preferred_element_type=jnp.float32)


def damping_terms(trace, squares, width):
    shift = DAMPING * trace / width
    norm = jnp.sqrt(squares + 2.0 * shift * trace + width * shift * shift)
    return 1.0 / norm, shift / norm


def lay_out(parts, wide):
    at = 0
    for part in parts:
        count, _, lanes = part.shape
        for i in range(count):
            wide[:, at : at + lanes] = part[i]
            at += lanes


def gram_kernel(*refs):
    *parts, out, wide = refs
    lay_out(parts, wide)
    for at, size in row_tiles(out.shape[0], 352):
        out[at : at + size, :] = dot_nt(wide[at : at + size, :], wide[...])


def factor_gram(wide, base, gram, scale):
    width = gram.shape[0]
    trace, squares = 0.0, 0.0
    for at, size in row_tiles(width, 352):
        tile = dot_nt(wide[at : at + size, :], wide[...])
        if base is not None:
            tile = tile + base[at : at + size, :]
        tile = tile * scale
        gram[at : at + size, :] = tile.astype(jnp.bfloat16)
        row = lax.broadcasted_iota(jnp.int32, tile.shape, 0) + at
        column = lax.broadcasted_iota(jnp.int32, tile.shape, 1)
        trace = trace + jnp.sum(jnp.where(row == column, tile, 0.0))
        squares = squares + jnp.sum(tile * tile)
    return trace, squares


def grad_kernel(scale, rows, high, m, where, q_mine, q_other, w_mine, w_other, left, wide, gram, poly, all_rows):
    width = gram.shape[0]
    half = w_mine.shape[1]
    lay_out([q_mine, q_other], wide)
    trace, squares = factor_gram(wide, None, gram, scale)
    norm, shift = damping_terms(trace, squares, width)
    rounds = half // rows
    at = lax.broadcasted_iota(jnp.int32, (width, width), 0)
    piece = at // rows
    arrival, other = piece % rounds, piece // rounds
    shard = ((arrival % high) ^ where[0]) * m + 2 * (arrival // high) + (other ^ where[1])
    place = shard * rows + at % rows
    hot = (place == lax.broadcasted_iota(jnp.int32, (width, width), 1)).astype(jnp.float32)
    hot = hot.astype(jnp.bfloat16)
    own = hot[:half]
    y1 = norm * dot_nn(own, gram[...]) + shift * own.astype(jnp.float32)
    y1_low = y1.astype(jnp.bfloat16)
    y2 = norm * dot_nn(y1_low, gram[...]) + shift * y1
    y2_low = y2.astype(jnp.bfloat16)
    y3 = norm * dot_nn(y2_low, gram[...]) + shift * y2
    total = (4.0 * y2 - 6.0 * y1 - y3).astype(jnp.bfloat16)
    poly[...] = dot_nt(total, hot).astype(jnp.bfloat16)
    all_rows[:, :half] = w_mine[...]
    all_rows[:, half:] = w_other[...]
    for at, size in row_tiles(left.shape[0], 352):
        mixed = dot_nt(all_rows[at : at + size, :], poly[...])
        mixed = mixed + 4.0 * w_mine[at : at + size, :].astype(jnp.float32)
        left[at : at + size, :] = mixed.astype(jnp.bfloat16)


def act_kernel(scale, parts, base, left, w_mine, *refs):
    *refs, update, inner, wide, gram, first, second = refs
    lay_out(refs, wide)
    width = gram.shape[0]
    trace, squares = factor_gram(wide, base, gram, scale)
    norm, shift = damping_terms(trace, squares, width)
    tiles = row_tiles(width, 352)
    for at, size in tiles:
        rows = left[at : at + size, :].astype(jnp.float32)
        step = norm * dot_nn(gram[at : at + size, :], left[...]) + shift * rows
        first[at : at + size, :] = 4.0 * rows - step
    second[...] = first[...].astype(jnp.bfloat16)
    total = 0.0
    for at, size in tiles:
        rows = left[at : at + size, :].astype(jnp.float32)
        step = norm * dot_nn(gram[at : at + size, :], second[...])
        first[at : at + size, :] = step + shift * first[at : at + size, :] - 6.0 * rows
    second[...] = first[...].astype(jnp.bfloat16)
    for at, size in tiles:
        rows = left[at : at + size, :].astype(jnp.float32)
        step = norm * dot_nn(gram[at : at + size, :], second[...])
        done = step + shift * first[at : at + size, :] + 4.0 * rows
        total = total + jnp.sum(done * w_mine[at : at + size, :].astype(jnp.float32))
        update[at : at + size, :] = done.astype(jnp.bfloat16)
    inner[...] = jnp.full(inner.shape, total, jnp.float32)


def call(kernel, out_shape, scratch, operands, flops, scalars=0):
    vmem = pl.BlockSpec(memory_space=pltpu.VMEM)
    smem = pl.BlockSpec(memory_space=pltpu.SMEM)
    moved = sum(x.size * x.dtype.itemsize for x in operands)
    return pl.pallas_call(
        kernel,
        out_shape=out_shape,
        in_specs=[smem] * scalars + [vmem] * (len(operands) - scalars),
        out_specs=jax.tree.map(lambda _: vmem, out_shape),
        scratch_shapes=[pltpu.VMEM(shape, dtype) for shape, dtype in scratch],
        compiler_params=pltpu.CompilerParams(vmem_limit_bytes=48 * 2**20),
        cost_estimate=pl.CostEstimate(flops=flops, bytes_accessed=moved, transcendentals=0),
    )(*operands)


def per_device(hidden_acts, out_grads, sample_idx, grad_weight, momentum, weight):
    n = lax.axis_size("shard")
    nt = lax.axis_size("tensor")
    batches, picks = sample_idx.shape
    rows, hidden = grad_weight.shape
    blocks = hidden // ABLK
    high = 2 * blocks
    m = n // high
    me = lax.axis_index("shard")
    col = lax.axis_index("tensor")
    core = col % 2
    hi = me // m
    lo = me % m

    def pairs_of(f):
        def target(s, t):
            to = f(s // m, s % m, t // 2, t % 2)
            return None if to is None else (to[0] * m + to[1], to[2] * 2 + to[3])

        return route(n, nt, target)

    def send(value, f, back=False):
        pairs = pairs_of(f)
        if back:
            pairs = [(to, source) for source, to in pairs]
        return lax.ppermute(value, AXES, pairs)

    def over_lo(value, d):
        return send(value, lambda h, l, y, c: (h, l ^ d, y, c))

    def over_core(value):
        return send(value, lambda h, l, y, c: (h, l, y, c ^ 1))

    def home(p):
        def target(h, l, y, c):
            j = h ^ (p % high)
            if l // 2 != p // high or j > 1:
                return None
            return (1 + j, c, y, l % 2)

        return target

    rounds = n // 2
    mine_j = hi - 1
    at_home = jnp.logical_and(jnp.logical_or(hi == 1, hi == 2), lo < 2)

    grad_t = grad_weight.T.reshape(blocks, ABLK, rows)
    w_own = [
        send(lax.dynamic_index_in_dim(grad_t, (hi ^ p) & 1, 0, keepdims=False), home(p))
        for p in range(rounds)
    ]

    acts_t = jnp.swapaxes(hidden_acts, 1, 2)
    tokens_t = lax.dynamic_index_in_dim(out_grads, col // 2, 0, keepdims=False).T
    my_idx = lax.dynamic_index_in_dim(sample_idx, col // 2, 0, keepdims=False)
    q = pick_transposed(tokens_t, my_idx)
    q = [
        send(q, lambda h, l, y, c, p=p: (1 + c, l, y, h & 1) if h >> 1 == p else None)
        for p in range(high // 2)
    ]
    q = jnp.stack(q)

    picked = jnp.stack([pick_transposed(acts_t[i], sample_idx[i]) for i in range(batches)])
    picked = picked.reshape(batches, blocks, ABLK, picks)
    z_own = [
        send(lax.dynamic_index_in_dim(picked, (hi ^ p) & 1, 1, keepdims=False), home(p))
        for p in range(rounds)
    ]

    q = jnp.concatenate([q] + [over_lo(q, d) for d in range(1, m)])
    q = jnp.concatenate(
        [q] + [send(q, lambda h, l, y, c, d=d: (h, l, y ^ d, c)) for d in range(1, nt // 2)]
    )
    q_other = over_core(q)

    w_mine = jnp.concatenate(w_own, axis=1)
    w_other = over_core(w_mine)

    bf16, f32 = jnp.bfloat16, jnp.float32
    count = batches * picks * n
    scale = 1.0 / count
    half = rounds * rows
    where = jnp.stack([mine_j & 1, core]).astype(jnp.int32)
    left = call(
        functools.partial(grad_kernel, scale, rows, high, m),
        jax.ShapeDtypeStruct((ABLK, half), bf16),
        [((DOUT, count), bf16), ((DOUT, DOUT), bf16), ((half, DOUT), bf16), ((ABLK, DOUT), bf16)],
        [where, q, q_other, w_mine, w_other],
        2 * DOUT * (DOUT * count + 4 * half * DOUT + ABLK * half),
        scalars=1,
    )

    cut = rounds // 2
    z_first = z_own[:cut] + [over_core(z) for z in z_own[:cut]]
    z_second = z_own[cut:] + [over_core(z) for z in z_own[cut:]]
    base = call(
        gram_kernel,
        jax.ShapeDtypeStruct((ABLK, ABLK), f32),
        [((ABLK, count // 2), bf16)],
        z_first,
        ABLK * ABLK * count,
    )

    update, inner = call(
        functools.partial(act_kernel, scale, len(z_second)),
        (jax.ShapeDtypeStruct((ABLK, half), bf16), jax.ShapeDtypeStruct((8, 128), f32)),
        [
            ((ABLK, count // 2), bf16),
            ((ABLK, ABLK), bf16),
            ((ABLK, half), f32),
            ((ABLK, half), bf16),
        ],
        [base, left, w_mine] + z_second,
        ABLK * ABLK * (count + 6 * half),
    )

    total = jnp.where(at_home, inner[:1, :1], 0.0)
    back = [
        send(update[:, p * rows : (p + 1) * rows], home(p), back=True) for p in range(rounds)
    ]
    total = total + over_core(total)
    for d in [2**i for i in range(10) if 2**i < nt // 2]:
        total = total + send(total, lambda h, l, y, c, d=d: (h, l, y ^ d, c))
    for d in [2**i for i in range(10) if 2**i < m]:
        total = total + over_lo(total, d)
    for d in [2**i for i in range(10) if 2**i < high]:
        total = total + send(total, lambda h, l, y, c, d=d: (h ^ d, l, y, c))
    ratio = jnp.minimum(1.0, CLIP_LEVEL / jnp.sqrt(total[0, 0] / (DOUT * FF)))

    even = sum(x.astype(jnp.float32) for x in back[0::2])
    odd = sum(x.astype(jnp.float32) for x in back[1::2])
    swap = (hi & 1) == 1
    final = jnp.concatenate([jnp.where(swap, odd, even), jnp.where(swap, even, odd)], axis=0)
    new_momentum = MOMENTUM_RATE * momentum.T + ratio * final
    new_weight = weight.T - LEARN_RATE * new_momentum
    return (new_momentum.T, new_weight.T)


def solution(mesh):
    in_specs = (
        P(None, "shard", "tensor"),
        P(None, "shard", None),
        P(None, "shard"),
        P("shard", "tensor"),
        P("shard", "tensor"),
        P("shard", "tensor"),
    )
    out_specs = (P("shard", "tensor"), P("shard", "tensor"))
    return jax.shard_map(
        per_device, mesh=mesh, in_specs=in_specs, out_specs=out_specs, check_vma=False
    )
```

time: 231 us -> 178 us (0.77)
  matrix products: 53.4 us -> 1.41 us
  waiting for transfers between devices: 70.5 us -> 31.3 us
  Pallas kernels: 0 us -> 39 us
  starting transfers between devices: 66.3 us -> 91 us
  local copies, waits for them, and re-layouts: 23.4 us -> 4.7 us
  between operations: 12.6 us -> 4.84 us
    dot_general x8 -> x0, matrix products: 49.7 us -> none  [the longest x5 25 us: dot_f32(): return jnp.dot(a, b, preferred_element_type=jnp.float32)]
    ppermute x37 -> x27, waiting for transfers between devices: 70.5 us -> 31.3 us  [send(): return lax.ppermute(value, AXES, pairs)]
    pallas_call x0 -> x3, Pallas kernels: none -> 39 us  [call(): pl.pallas_call(kernel, out_shape=out_shape, in_specs=[smem] * scalars + [...]
    ppermute x37 -> x27, starting transfers between devices: 66.3 us -> 91 us  [send(): return lax.ppermute(value, AXES, pairs)]
    unnamed x47 -> x23, local copies, waits for them, and re-layouts: 12 us -> 2.18 us
    concatenate x5 -> x1, local copies, waits for them, and re-layouts: 4.96 us -> 0.09 us  [per_device(): w_mine = jnp.concatenate(w_own, axis=1)]
    dot_general x2 -> x3, matrix products: 3.75 us -> 1.41 us  [pick_transposed(): jnp.dot(tokens_t, hot.astype(jnp.bfloat16), preferred_element_type=jnp.fl...]
  transfers between devices with their start and end apart: 37 -> 27, of which waited for: 17 -> 11; matrix products, arithmetic and copies ran while one was open for 14% -> 3% of each run, Pallas kernels for 0% -> 13%
where the time goes in v2:
time: 178 us; the launch traced here: 177 us
  starting transfers between devices  91 us (51%)
  Pallas kernels  39 us (22%)
  waiting for transfers between devices  31.3 us (18%)
  other arithmetic  5.02 us (3%)
  between operations  4.84 us (3%)
  local copies, waits for them, and re-layouts  4.7 us (3%)
    ppermute x27, starting transfers between devices, send(): return lax.ppermute(value, AXES, pairs)  91 us
    pallas_call x3, Pallas kernels, call(): pl.pallas_call(kernel, out_shape=out_shape, in_specs=[smem] * scalars + [...  39 us
    ppermute x27, waiting for transfers between devices, send(): return lax.ppermute(value, AXES, pairs)  31.3 us
  transfers between devices with their start and end apart: 27, of which 11 were waited for; matrix products, arithmetic and copies ran while one was open for 3% of the time, Pallas kernels for 13%

profile of v2, /device:TPU:0, one launch (start us, length us, event | category | flops | bytes accessed | tf_op | source)
XLA Modules:
  0.0 177.4 jit_solution(12827674973467973928)
XLA Ops:
  2.3 4.9 %collective-permute-start.4 = (bf16[1024,128]{1,0:T(8,128)(2,1)S(1)}, bf16[1024,128]{1,0:T(8,128)(2,1)S(1)}, u32[]{:S(2)}, u32[]{:S(2)}) collective-permute-start(bf16[1024,128]{1,0:T(8,128)(2,1)S(1)} %convolution_convert_fusion.2), channel_id=1, source_target_pairs={{0,8},{1,16},{2,10},{3,18},{4,12},{5,20},{6,14},{7,22},{8,9},{9,17... | collective-permute-start | bytes 786440 | tf_op jit(solution)/shard_map/ppermute | solution.py:195
  7.9 5.6 %collective-permute-done.4 = bf16[1024,128]{1,0:T(8,128)(2,1)S(1)} collective-permute-done((bf16[1024,128]{1,0:T(8,128)(2,1)S(1)}, bf16[1024,128]{1,0:T(8,128)(2,1)S(1)}, u32[]{:S(2)}, u32[]{:S(2)}) %collective-permute-start.4) | collective-permute-done | bytes 262176 | tf_op jit(solution)/shard_map/ppermute | solution.py:195
  13.6 1.6 collective-permute-start.6
  15.2 6.8 %collective-permute-start.9 = (bf16[1368,128]{1,0:T(8,128)(2,1)S(1)}, bf16[1368,128]{1,0:T(8,128)(2,1)S(1)}, u32[]{:S(2)}, u32[]{:S(2)}) collective-permute-start(bf16[1368,128]{1,0:T(8,128)(2,1)S(1)} %get-tuple-element.21), channel_id=1, source_target_pairs={{0,8},{1,12},{2,10},{3,14},{4,9},{5,13},{6,11},{7,15},{8,16},{9,20... | collective-permute-start | bytes 1050632 | tf_op jit(solution)/shard_map/ppermute | solution.py:195
  24.8 3.2 %collective-permute-done.6 = bf16[2,1024,128]{2,1,0:T(8,128)(2,1)S(1)} collective-permute-done((bf16[2,1024,128]{2,1,0:T(8,128)(2,1)S(1)}, bf16[2,1024,128]{2,1,0:T(8,128)(2,1)S(1)}, u32[]{:S(2)}, u32[]{:S(2)}) %collective-permute-start.6) | collective-permute-done | bytes 524320 | tf_op jit(solution)/shard_map/ppermute | solution.py:195
  28.1 1.6 collective-permute-start.7
  31.9 17.5 %collective-permute-start = (bf16[2,1368,128]{2,1,0:T(8,128)(2,1)S(1)}, bf16[2,1368,128]{2,1,0:T(8,128)(2,1)S(1)}, u32[]{:S(2)}, u32[]{:S(2)}) collective-permute-start(bf16[2,1368,128]{2,1,0:T(8,128)(2,1)S(1)} %get-tuple-element.15), channel_id=1, source_target_pairs={{0,8},{1,12},{2,10},{3,14},{4,9},{5,13},{6,11},{7,15},{8,16},{9,20... | collective-permute-start | bytes 2101256 | tf_op jit(solution)/shard_map/ppermute | solution.py:195
  49.5 3.4 %collective-permute-done.7 = bf16[4,1024,128]{2,1,0:T(8,128)(2,1)S(1)} collective-permute-done((bf16[4,1024,128]{2,1,0:T(8,128)(2,1)S(1)}, bf16[4,1024,128]{2,1,0:T(8,128)(2,1)S(1)}, u32[]{:S(2)}, u32[]{:S(2)}) %collective-permute-start.7) | collective-permute-done | bytes 1048608 | tf_op jit(solution)/shard_map/ppermute | solution.py:195
  52.9 8.9 %collective-permute-start.1 = (bf16[2,1368,128]{2,1,0:T(8,128)(2,1)S(1)}, bf16[2,1368,128]{2,1,0:T(8,128)(2,1)}, u32[]{:S(2)}, u32[]{:S(2)}) collective-permute-start(bf16[2,1368,128]{2,1,0:T(8,128)(2,1)S(1)} %get-tuple-element.16), channel_id=1, source_target_pairs={{0,16},{1,20},{2,18},{3,22},{4,17},{5,21},{6,19},{7,23},{8,8},{9,1... | collective-permute-start | bytes 2101256 | tf_op jit(solution)/shard_map/ppermute | solution.py:195
  61.8 1.6 pad_maximum_fusion.q_mine
  63.4 1.7 collective-permute-start.8
  65.2 1.5 collective-permute-start.14
  67.0 1.5 collective-permute-start.15
  68.5 10.6 %collective-permute-done.1.refs_1_ = bf16[2,1368,128]{2,1,0:T(8,128)(2,1)} collective-permute-done((bf16[2,1368,128]{2,1,0:T(8,128)(2,1)S(1)}, bf16[2,1368,128]{2,1,0:T(8,128)(2,1)}, u32[]{:S(2)}, u32[]{:S(2)}) %collective-permute-start.1) | collective-permute-done | bytes 700448 | tf_op jit(solution)/shard_map/ppermute | solution.py:195
  81.2 2.3 %collective-permute-done.2.refs_2_ = bf16[2,1368,128]{2,1,0:T(8,128)(2,1)} collective-permute-done((bf16[2,1368,128]{2,1,0:T(8,128)(2,1)S(1)}, bf16[2,1368,128]{2,1,0:T(8,128)(2,1)}, u32[]{:S(2)}, u32[]{:S(2)}) %collective-permute-start.2) | collective-permute-done | bytes 700448 | tf_op jit(solution)/shard_map/ppermute | solution.py:195
  84.6 9.2 %shard_map.77.base = f32[1368,1368]{1,0:T(8,128)} custom-call(bf16[2,1368,128]{2,1,0:T(8,128)(2,1)S(1)} %collective-permute-done.refs_0_, bf16[2,1368,128]{2,1,0:T(8,128)(2,1)} %collective-permute-done.1.refs_1_, bf16[2,1368,128]{2,1,0:T(8,128)(2,1)} %collective-permute-done.2.refs_2_, bf16[2,1368,128]{2,1,0:T(8,128)(2,1)} %collective-permute-done.3.refs_3_), custom_call_target="tpu_custom_call" | custom-call | flops 3832676352 | bytes 2801664 | tf_op jit(solution)/shard_map/pallas_call | solution.py:159
  93.8 13.6 %shard_map.78.left = bf16[1368,512]{1,0:T(8,128)(2,1)S(1)} custom-call(s32[2]{0:T(128)S(1)} %pad_add_fusion.where, bf16[8,1024,128]{2,1,0:T(8,128)(2,1)} %pad_maximum_fusion.q_mine, bf16[8,1024,128]{2,1,0:T(8,128)(2,1)} %collective-permute-done.8.q_other, bf16[1368,512]{1,0:T(8,128)(2,1)S(1)} %constant_dynamic-update-slice_fusion.w_mine, ...), custom_call_target="tpu_custom_call" | custom-call | flops 10024386560 | bytes 6995976 | tf_op jit(solution)/shard_map/pallas_call | solution.py:159
  107.4 16.2 %shard_map.79 = (bf16[1368,512]{1,0:T(8,128)(2,1)S(1)}, f32[8,128]{1,0:T(8,128)S(1)}) custom-call(f32[1368,1368]{1,0:T(8,128)} %shard_map.77.base, bf16[1368,512]{1,0:T(8,128)(2,1)S(1)} %shard_map.78.left, bf16[1368,512]{1,0:T(8,128)(2,1)} %copy-done.1, bf16[2,1368,128]{2,1,0:T(8,128)(2,1)} %collective-permute-done.14.refs_0_, ...), custom_call_target="tpu_custom_call" | custom-call | flops 9581690880 | bytes 13089024 | tf_op jit(solution)/shard_map/pallas_call | solution.py:159
  131.6 1.9 %collective-permute-start.19 = (f32[1,1]{1,0:T(1,128)}, f32[1,1]{1,0:T(1,128)}, u32[]{:S(2)}, u32[]{:S(2)}) collective-permute-start(f32[1,1]{1,0:T(1,128)} %add.65), channel_id=1, source_target_pairs={{0,2},{1,3},{2,0},{3,1},{4,6},{5,7},{6,4},{7,5},{8,10},{9,11},{10,... | collective-permute-start | bytes 20 | tf_op jit(solution)/shard_map/ppermute | solution.py:195
  133.5 1.7 collective-permute-done.19
  137.2 2.2 %collective-permute-done.20 = f32[1,1]{1,0:T(1,128)} collective-permute-done((f32[1,1]{1,0:T(1,128)}, f32[1,1]{1,0:T(1,128)}, u32[]{:S(2)}, u32[]{:S(2)}) %collective-permute-start.20) | collective-permute-done | bytes 36 | tf_op jit(solution)/shard_map/ppermute | solution.py:195
  140.0 27.8 %collective-permute-start.21 = (f32[1,1]{1,0:T(1,128)}, f32[1,1]{1,0:T(1,128)}, u32[]{:S(2)}, u32[]{:S(2)}) collective-permute-start(f32[1,1]{1,0:T(1,128)} %add.67), channel_id=1, source_target_pairs={{0,8},{1,9},{2,10},{3,11},{4,12},{5,13},{6,14},{7,15},{8,0},{9,1},... | collective-permute-start | bytes 20 | tf_op jit(solution)/shard_map/ppermute | solution.py:195
  168.6 3.2 %collective-permute-start.22 = (f32[1,1]{1,0:T(1,128)}, f32[1,1]{1,0:T(1,128)}, u32[]{:S(2)}, u32[]{:S(2)}) collective-permute-start(f32[1,1]{1,0:T(1,128)} %add.68), channel_id=1, source_target_pairs={{0,16},{1,17},{2,18},{3,19},{4,20},{5,21},{6,22},{7,23},{8,24},{9,... | collective-permute-start | bytes 20 | tf_op jit(solution)/shard_map/ppermute | solution.py:195
  175.5 1.9 %fusion.1 = (f32[128,2736]{0,1:T(8,128)}, f32[128,2736]{0,1:T(8,128)}) fusion(f32[128,2736]{0,1:T(8,128)S(1)} %copy-done.8, f32[1368,128]{1,0:T(8,128)S(1)} %get-tuple-element.9, f32[1368,128]{1,0:T(8,128)S(1)} %get-tuple-element.8, f32[]{:T(128)} %bitcast.30, f32[128,2736]{0,1:T(8,128)S(1)} %copy-done.9), kind=kLoop, calls=%fused_computation.16 | loop fusion | flops 2101248 | bytes 7004164 | tf_op jit(solution)/shard_map/transpose | solution.py:305
  (71 shorter events, 22.2 us)
Async XLA Ops:
  2.3 11.3 %collective-permute-start.4 = (bf16[1024,128]{1,0:T(8,128)(2,1)S(1)}, bf16[1024,128]{1,0:T(8,128)(2,1)S(1)}, u32[]{:S(2)}, u32[]{:S(2)}) collective-permute-start(bf16[1024,128]{1,0:T(8,128)(2,1)S(1)} %convolution_convert_fusion.2), channel_id=1, source_target_pairs={{0,8},{1,16},{2,10},{3,18},{4,12},{5,20},{6,14},{7,22},{8,9},{9,17... | collective-permute-start | bytes 786440 | tf_op jit(solution)/shard_map/ppermute | solution.py:195
  7.2 6.3 %collective-permute-start.5 = (bf16[1024,128]{1,0:T(8,128)(2,1)S(1)}, bf16[1024,128]{1,0:T(8,128)(2,1)S(1)}, u32[]{:S(2)}, u32[]{:S(2)}) collective-permute-start(bf16[1024,128]{1,0:T(8,128)(2,1)S(1)} %convolution_convert_fusion.2), channel_id=1, source_target_pairs={{16,8},{17,16},{18,10},{19,18},{20,12},{21,20},{22,14},{23,22},{24... | collective-permute-start | bytes 786440 | tf_op jit(solution)/shard_map/ppermute | solution.py:195
  13.6 14.4 %collective-permute-start.6 = (bf16[2,1024,128]{2,1,0:T(8,128)(2,1)S(1)}, bf16[2,1024,128]{2,1,0:T(8,128)(2,1)S(1)}, u32[]{:S(2)}, u32[]{:S(2)}) collective-permute-start(bf16[2,1024,128]{2,1,0:T(8,128)(2,1)S(1)} %pad_maximum_fusion.2), channel_id=1, source_target_pairs={{0,4},{1,5},{2,6},{3,7},{4,0},{5,1},{6,2},{7,3},{8,12},{9,13},{10,... | collective-permute-start | bytes 1572872 | tf_op jit(solution)/shard_map/ppermute | solution.py:195
  15.2 16.7 %collective-permute-start.9 = (bf16[1368,128]{1,0:T(8,128)(2,1)S(1)}, bf16[1368,128]{1,0:T(8,128)(2,1)S(1)}, u32[]{:S(2)}, u32[]{:S(2)}) collective-permute-start(bf16[1368,128]{1,0:T(8,128)(2,1)S(1)} %get-tuple-element.21), channel_id=1, source_target_pairs={{0,8},{1,12},{2,10},{3,14},{4,9},{5,13},{6,11},{7,15},{8,16},{9,20... | collective-permute-start | bytes 1050632 | tf_op jit(solution)/shard_map/ppermute | solution.py:195
  22.1 41.3 %collective-permute-start.10 = (bf16[1368,128]{1,0:T(8,128)(2,1)S(1)}, bf16[1368,128]{1,0:T(8,128)(2,1)S(1)}, u32[]{:S(2)}, u32[]{:S(2)}) collective-permute-start(bf16[1368,128]{1,0:T(8,128)(2,1)S(1)} %get-tuple-element.20), channel_id=1, source_target_pairs={{0,16},{1,20},{2,18},{3,22},{4,17},{5,21},{6,19},{7,23},{8,8},{9,1... | collective-permute-start | bytes 1050632 | tf_op jit(solution)/shard_map/ppermute | solution.py:195
  23.4 41.8 %collective-permute-start.11 = (bf16[1368,128]{1,0:T(8,128)(2,1)S(1)}, bf16[1368,128]{1,0:T(8,128)(2,1)S(1)}, u32[]{:S(2)}, u32[]{:S(2)}) collective-permute-start(bf16[1368,128]{1,0:T(8,128)(2,1)S(1)} %get-tuple-element.19), channel_id=1, source_target_pairs={{16,8},{17,12},{18,10},{19,14},{20,9},{21,13},{22,11},{23,15},{24,... | collective-permute-start | bytes 1050632 | tf_op jit(solution)/shard_map/ppermute | solution.py:195
  24.1 42.7 %collective-permute-start.12 = (bf16[1368,128]{1,0:T(8,128)(2,1)S(1)}, bf16[1368,128]{1,0:T(8,128)(2,1)S(1)}, u32[]{:S(2)}, u32[]{:S(2)}) collective-permute-start(bf16[1368,128]{1,0:T(8,128)(2,1)S(1)} %get-tuple-element.18), channel_id=1, source_target_pairs={{16,16},{17,20},{18,18},{19,22},{20,17},{21,21},{22,19},{23,23},{2... | collective-permute-start | bytes 1050632 | tf_op jit(solution)/shard_map/ppermute | solution.py:195
  28.1 24.8 %collective-permute-start.7 = (bf16[4,1024,128]{2,1,0:T(8,128)(2,1)S(1)}, bf16[4,1024,128]{2,1,0:T(8,128)(2,1)S(1)}, u32[]{:S(2)}, u32[]{:S(2)}) collective-permute-start(bf16[4,1024,128]{2,1,0:T(8,128)(2,1)S(1)} %pad_maximum_fusion.1), channel_id=1, source_target_pairs={{0,2},{1,3},{2,0},{3,1},{4,6},{5,7},{6,4},{7,5},{8,10},{9,11},{10,... | collective-permute-start | bytes 3145736 | tf_op jit(solution)/shard_map/ppermute | solution.py:195
  31.9 35.1 %collective-permute-start = (bf16[2,1368,128]{2,1,0:T(8,128)(2,1)S(1)}, bf16[2,1368,128]{2,1,0:T(8,128)(2,1)S(1)}, u32[]{:S(2)}, u32[]{:S(2)}) collective-permute-start(bf16[2,1368,128]{2,1,0:T(8,128)(2,1)S(1)} %get-tuple-element.15), channel_id=1, source_target_pairs={{0,8},{1,12},{2,10},{3,14},{4,9},{5,13},{6,11},{7,15},{8,16},{9,20... | collective-permute-start | bytes 2101256 | tf_op jit(solution)/shard_map/ppermute | solution.py:195
  52.9 26.2 %collective-permute-start.1 = (bf16[2,1368,128]{2,1,0:T(8,128)(2,1)S(1)}, bf16[2,1368,128]{2,1,0:T(8,128)(2,1)}, u32[]{:S(2)}, u32[]{:S(2)}) collective-permute-start(bf16[2,1368,128]{2,1,0:T(8,128)(2,1)S(1)} %get-tuple-element.16), channel_id=1, source_target_pairs={{0,16},{1,20},{2,18},{3,22},{4,17},{5,21},{6,19},{7,23},{8,8},{9,1... | collective-permute-start | bytes 2101256 | tf_op jit(solution)/shard_map/ppermute | solution.py:195
  63.4 30.4 %collective-permute-start.8 = (bf16[8,1024,128]{2,1,0:T(8,128)(2,1)}, bf16[8,1024,128]{2,1,0:T(8,128)(2,1)}, u32[]{:S(2)}, u32[]{:S(2)}) collective-permute-start(bf16[8,1024,128]{2,1,0:T(8,128)(2,1)} %pad_maximum_fusion.q_mine), channel_id=1, source_target_pairs={{0,1},{1,0},{2,3},{3,2},{4,5},{5,4},{6,7},{7,6},{8,9},{9,8},{10,11... | collective-permute-start | bytes 6291464 | tf_op jit(solution)/shard_map/ppermute | solution.py:195
  65.2 15.4 %collective-permute-start.14 = (bf16[2,1368,128]{2,1,0:T(8,128)(2,1)S(1)}, bf16[2,1368,128]{2,1,0:T(8,128)(2,1)}, u32[]{:S(2)}, u32[]{:S(2)}) collective-permute-start(bf16[2,1368,128]{2,1,0:T(8,128)(2,1)S(1)} %get-tuple-element.17), channel_id=1, source_target_pairs={{16,8},{17,12},{18,10},{19,14},{20,9},{21,13},{22,11},{23,15},{24,... | collective-permute-start | bytes 2101256 | tf_op jit(solution)/shard_map/ppermute | solution.py:195
  66.9 26.9 %collective-permute-start.13 = (bf16[1368,512]{1,0:T(8,128)(2,1)S(1)}, bf16[1368,512]{1,0:T(8,128)(2,1)}, u32[]{:S(2)}, u32[]{:S(2)}) collective-permute-start(bf16[1368,512]{1,0:T(8,128)(2,1)S(1)} %constant_dynamic-update-slice_fusion.w_mine), channel_id=1, source_target_pairs={{0,1},{1,0},{2,3},{3,2},{4,5},{5,4},{6,7},{7,6},{8,9},{9,8},{10,11... | collective-permute-start | bytes 4202504 | tf_op jit(solution)/shard_map/ppermute | solution.py:195
  67.0 13.7 %collective-permute-start.15 = (bf16[2,1368,128]{2,1,0:T(8,128)(2,1)}, bf16[2,1368,128]{2,1,0:T(8,128)(2,1)}, u32[]{:S(2)}, u32[]{:S(2)}) collective-permute-start(bf16[2,1368,128]{2,1,0:T(8,128)(2,1)} %get-tuple-element.14), channel_id=1, source_target_pairs={{16,16},{17,20},{18,18},{19,22},{20,17},{21,21},{22,19},{23,23},{2... | collective-permute-start | bytes 2101256 | tf_op jit(solution)/shard_map/ppermute | solution.py:195
  79.1 4.4 %collective-permute-start.2 = (bf16[2,1368,128]{2,1,0:T(8,128)(2,1)S(1)}, bf16[2,1368,128]{2,1,0:T(8,128)(2,1)}, u32[]{:S(2)}, u32[]{:S(2)}) collective-permute-start(bf16[2,1368,128]{2,1,0:T(8,128)(2,1)S(1)} %collective-permute-done.refs_0_), channel_id=1, source_target_pairs={{0,1},{1,0},{2,3},{3,2},{4,5},{5,4},{6,7},{7,6},{8,9},{9,8},{10,11... | collective-permute-start | bytes 2101256 | tf_op jit(solution)/shard_map/ppermute | solution.py:195
  80.6 4.0 %collective-permute-start.3 = (bf16[2,1368,128]{2,1,0:T(8,128)(2,1)}, bf16[2,1368,128]{2,1,0:T(8,128)(2,1)}, u32[]{:S(2)}, u32[]{:S(2)}) collective-permute-start(bf16[2,1368,128]{2,1,0:T(8,128)(2,1)} %collective-permute-done.1.refs_1_), channel_id=1, source_target_pairs={{0,1},{1,0},{2,3},{3,2},{4,5},{5,4},{6,7},{7,6},{8,9},{9,8},{10,11... | collective-permute-start | bytes 2101256 | tf_op jit(solution)/shard_map/ppermute | solution.py:195
  80.7 26.7 %collective-permute-start.16 = (bf16[2,1368,128]{2,1,0:T(8,128)(2,1)}, bf16[2,1368,128]{2,1,0:T(8,128)(2,1)S(1)}, u32[]{:S(2)}, u32[]{:S(2)}) collective-permute-start(bf16[2,1368,128]{2,1,0:T(8,128)(2,1)} %collective-permute-done.14.refs_0_), channel_id=1, source_target_pairs={{0,1},{1,0},{2,3},{3,2},{4,5},{5,4},{6,7},{7,6},{8,9},{9,8},{10,11... | collective-permute-start | bytes 2101256 | tf_op jit(solution)/shard_map/ppermute | solution.py:195
  83.5 24.0 %collective-permute-start.17 = (bf16[2,1368,128]{2,1,0:T(8,128)(2,1)}, bf16[2,1368,128]{2,1,0:T(8,128)(2,1)S(1)}, u32[]{:S(2)}, u32[]{:S(2)}) collective-permute-start(bf16[2,1368,128]{2,1,0:T(8,128)(2,1)} %collective-permute-done.15.refs_1_), channel_id=1, source_target_pairs={{0,1},{1,0},{2,3},{3,2},{4,5},{5,4},{6,7},{7,6},{8,9},{9,8},{10,11... | collective-permute-start | bytes 2101256 | tf_op jit(solution)/shard_map/ppermute | solution.py:195
  124.7 49.1 %collective-permute-start.23 = (bf16[1368,128]{1,0:T(8,128)(2,1)}, bf16[1368,128]{1,0:T(8,128)(2,1)S(1)}, u32[]{:S(2)}, u32[]{:S(2)}) collective-permute-start(bf16[1368,128]{1,0:T(8,128)(2,1)} %get-tuple-element.13), channel_id=1, source_target_pairs={{16,0},{20,1},{18,2},{22,3},{17,4},{21,5},{19,6},{23,7},{8,8},{12,... | collective-permute-start | bytes 1050632 | tf_op jit(solution)/shard_map/ppermute | solution.py:195
  126.0 47.8 %collective-permute-start.24 = (bf16[1368,128]{1,0:T(8,128)(2,1)S(1)}, bf16[1368,128]{1,0:T(8,128)(2,1)S(1)}, u32[]{:S(2)}, u32[]{:S(2)}) collective-permute-start(bf16[1368,128]{1,0:T(8,128)(2,1)S(1)} %get-tuple-element.12), channel_id=1, source_target_pairs={{16,16},{20,17},{18,18},{22,19},{17,20},{21,21},{19,22},{23,23},{8... | collective-permute-start | bytes 1050632 | tf_op jit(solution)/shard_map/ppermute | solution.py:195
  126.6 47.1 %collective-permute-start.25 = (bf16[1368,128]{1,0:T(8,128)(2,1)S(1)}, bf16[1368,128]{1,0:T(8,128)(2,1)S(1)}, u32[]{:S(2)}, u32[]{:S(2)}) collective-permute-start(bf16[1368,128]{1,0:T(8,128)(2,1)S(1)} %get-tuple-element.10), channel_id=1, source_target_pairs={{8,0},{12,1},{10,2},{14,3},{9,4},{13,5},{11,6},{15,7},{16,8},{20,9... | collective-permute-start | bytes 1050632 | tf_op jit(solution)/shard_map/ppermute | solution.py:195
  127.9 45.8 %collective-permute-start.26 = (bf16[1368,128]{1,0:T(8,128)(2,1)S(1)}, bf16[1368,128]{1,0:T(8,128)(2,1)S(1)}, u32[]{:S(2)}, u32[]{:S(2)}) collective-permute-start(bf16[1368,128]{1,0:T(8,128)(2,1)S(1)} %get-tuple-element.11), channel_id=1, source_target_pairs={{8,16},{12,17},{10,18},{14,19},{9,20},{13,21},{11,22},{15,23},{16,... | collective-permute-start | bytes 1050632 | tf_op jit(solution)/shard_map/ppermute | solution.py:195
  140.0 27.9 %collective-permute-start.21 = (f32[1,1]{1,0:T(1,128)}, f32[1,1]{1,0:T(1,128)}, u32[]{:S(2)}, u32[]{:S(2)}) collective-permute-start(f32[1,1]{1,0:T(1,128)} %add.67), channel_id=1, source_target_pairs={{0,8},{1,9},{2,10},{3,11},{4,12},{5,13},{6,14},{7,15},{8,0},{9,1},... | collective-permute-start | bytes 20 | tf_op jit(solution)/shard_map/ppermute | solution.py:195
  168.6 4.5 %collective-permute-start.22 = (f32[1,1]{1,0:T(1,128)}, f32[1,1]{1,0:T(1,128)}, u32[]{:S(2)}, u32[]{:S(2)}) collective-permute-start(f32[1,1]{1,0:T(1,128)} %add.68), channel_id=1, source_target_pairs={{0,16},{1,17},{2,18},{3,19},{4,20},{5,21},{6,22},{7,23},{8,24},{9,... | collective-permute-start | bytes 20 | tf_op jit(solution)/shard_map/ppermute | solution.py:195
  (13 other events, 147.3 us)

commit v3 on v2

--- a/solution.py
+++ b/solution.py
@@ -17,6 +17,12 @@
 LEARN_RATE = 0.5
 
 AXES = ("shard", "tensor")
+VMEM_MIB = 32
+ORDER = (0, 2, 3, 1)
+
+
+def mirrored(position, j):
+    return position + j * (len(ORDER) - 1 - 2 * position)
 
 
 def route(shards, tensors, target):
@@ -27,13 +33,6 @@
             if to is not None:
                 pairs.append((s * tensors + t, to[0] * tensors + to[1]))
     return pairs
-
-
-def pick(tokens, where):
-    hot = (where[:, None] == lax.broadcasted_iota(jnp.int32, (where.shape[0], tokens.shape[0]), 1))
-    return jnp.dot(hot.astype(jnp.bfloat16), tokens, preferred_element_type=jnp.float32).astype(
-        jnp.bfloat16
-    )
 
 
 def pick_transposed(tokens_t, where):
@@ -95,17 +94,39 @@
     return trace, squares
 
 
-def grad_kernel(scale, rows, high, m, where, q_mine, q_other, w_mine, w_other, left, wide, gram, poly, all_rows):
+def pick_kernel(upper, index, tokens, outer, inside):
+    batches, _, count = tokens.shape
+    picks = index.shape[1]
+    for i in range(batches):
+        row = lax.broadcasted_iota(jnp.int32, (count, picks), 0)
+        hot = (row == index[i : i + 1, :]).astype(jnp.float32).astype(jnp.bfloat16)
+        chosen = dot_nn(tokens[i], hot)
+        for block in range(2):
+            part = chosen[block * ABLK : (block + 1) * ABLK].astype(jnp.bfloat16)
+
+            @pl.when(upper[0] == block)
+            def _():
+                outer[i] = part
+
+            @pl.when(upper[0] != block)
+            def _():
+                inside[i] = part
+
+
+def grad_kernel(scale, rows, high, m, where, *refs):
+    *q_parts, w_mine, w_other, left, wide, gram, poly, all_rows = refs
     width = gram.shape[0]
     half = w_mine.shape[1]
-    lay_out([q_mine, q_other], wide)
+    lay_out(q_parts, wide)
     trace, squares = factor_gram(wide, None, gram, scale)
     norm, shift = damping_terms(trace, squares, width)
     rounds = half // rows
     at = lax.broadcasted_iota(jnp.int32, (width, width), 0)
     piece = at // rows
     arrival, other = piece % rounds, piece // rounds
-    shard = ((arrival % high) ^ where[0]) * m + 2 * (arrival // high) + (other ^ where[1])
+    turn = arrival % high
+    position = sum(jnp.where(turn == i, ORDER[i], 0) for i in range(high))
+    shard = mirrored(position, where[0]) * m + 2 * (arrival // high) + (other ^ where[1])
     place = shard * rows + at % rows
     hot = (place == lax.broadcasted_iota(jnp.int32, (width, width), 1)).astype(jnp.float32)
     hot = hot.astype(jnp.bfloat16)
@@ -162,7 +183,7 @@
         in_specs=[smem] * scalars + [vmem] * (len(operands) - scalars),
         out_specs=jax.tree.map(lambda _: vmem, out_shape),
         scratch_shapes=[pltpu.VMEM(shape, dtype) for shape, dtype in scratch],
-        compiler_params=pltpu.CompilerParams(vmem_limit_bytes=48 * 2**20),
+        compiler_params=pltpu.CompilerParams(vmem_limit_bytes=VMEM_MIB * 2**20),
         cost_estimate=pl.CostEstimate(flops=flops, bytes_accessed=moved, transcendentals=0),
     )(*operands)
 
@@ -202,50 +223,61 @@
 
     def home(p):
         def target(h, l, y, c):
-            j = h ^ (p % high)
-            if l // 2 != p // high or j > 1:
+            j = 0 if h == ORDER[p % high] else 1
+            if l // 2 != p // high or h != mirrored(ORDER[p % high], j):
                 return None
             return (1 + j, c, y, l % 2)
 
         return target
+
+    def outer_round(p):
+        return p % high in (0, high - 1)
+
+    upper = hi >= high // 2
+
+    def after(value, others):
+        return lax.optimization_barrier((value, others))[0]
 
     rounds = n // 2
     mine_j = hi - 1
     at_home = jnp.logical_and(jnp.logical_or(hi == 1, hi == 2), lo < 2)
 
-    grad_t = grad_weight.T.reshape(blocks, ABLK, rows)
-    w_own = [
-        send(lax.dynamic_index_in_dim(grad_t, (hi ^ p) & 1, 0, keepdims=False), home(p))
-        for p in range(rounds)
-    ]
-
-    acts_t = jnp.swapaxes(hidden_acts, 1, 2)
     tokens_t = lax.dynamic_index_in_dim(out_grads, col // 2, 0, keepdims=False).T
     my_idx = lax.dynamic_index_in_dim(sample_idx, col // 2, 0, keepdims=False)
     q = pick_transposed(tokens_t, my_idx)
-    q = [
-        send(q, lambda h, l, y, c, p=p: (1 + c, l, y, h & 1) if h >> 1 == p else None)
-        for p in range(high // 2)
-    ]
-    q = jnp.stack(q)
-
-    picked = jnp.stack([pick_transposed(acts_t[i], sample_idx[i]) for i in range(batches)])
-    picked = picked.reshape(batches, blocks, ABLK, picks)
-    z_own = [
-        send(lax.dynamic_index_in_dim(picked, (hi ^ p) & 1, 1, keepdims=False), home(p))
-        for p in range(rounds)
-    ]
-
-    q = jnp.concatenate([q] + [over_lo(q, d) for d in range(1, m)])
-    q = jnp.concatenate(
-        [q] + [send(q, lambda h, l, y, c, d=d: (h, l, y ^ d, c)) for d in range(1, nt // 2)]
-    )
-    q_other = over_core(q)
-
+    q_own = [send(q, home(p)) for p in range(rounds)]
+    q_same = jnp.stack(q_own)
+    q_parts = [q_same, over_core(q_same)]
+
+    bf16, f32 = jnp.bfloat16, jnp.float32
+    outer, inside = call(
+        pick_kernel,
+        (jax.ShapeDtypeStruct((batches, ABLK, picks), bf16),) * 2,
+        [],
+        [upper.astype(jnp.int32).reshape(1), sample_idx, jnp.swapaxes(hidden_acts, 1, 2)],
+        2 * batches * picks * hidden * hidden_acts.shape[1],
+        scalars=1,
+    )
+    late = [p for p in range(rounds) if p % high == 2]
+    early = [p for p in range(rounds) if p % high != 2]
+    outer, inside = after((outer, inside), q_own)
+    z_early = [send(outer if outer_round(p) else inside, home(p)) for p in early]
+
+    grad_t = after(grad_weight.T, z_early)
+    first = jnp.where(upper, ABLK, 0)
+    w_outer = lax.dynamic_slice_in_dim(grad_t, first, ABLK, 0)
+    w_inside = lax.dynamic_slice_in_dim(grad_t, ABLK - first, ABLK, 0)
+    w_own = [send(w_outer if outer_round(p) else w_inside, home(p)) for p in range(rounds)]
     w_mine = jnp.concatenate(w_own, axis=1)
     w_other = over_core(w_mine)
 
-    bf16, f32 = jnp.bfloat16, jnp.float32
+    inside = after(inside, w_own)
+    z_late = [send(inside, home(p)) for p in late]
+
+    for d in range(1, nt // 2):
+        q_far = send(q_same, lambda h, l, y, c, d=d: (h, l, y ^ d, c))
+        q_parts += [q_far, over_core(after(q_far, w_own))]
+
     count = batches * picks * n
     scale = 1.0 / count
     half = rounds * rows
@@ -254,52 +286,47 @@
         functools.partial(grad_kernel, scale, rows, high, m),
         jax.ShapeDtypeStruct((ABLK, half), bf16),
         [((DOUT, count), bf16), ((DOUT, DOUT), bf16), ((half, DOUT), bf16), ((ABLK, DOUT), bf16)],
-        [where, q, q_other, w_mine, w_other],
+        [where, *q_parts, w_mine, w_other],
         2 * DOUT * (DOUT * count + 4 * half * DOUT + ABLK * half),
         scalars=1,
     )
 
-    cut = rounds // 2
-    z_first = z_own[:cut] + [over_core(z) for z in z_own[:cut]]
-    z_second = z_own[cut:] + [over_core(z) for z in z_own[cut:]]
+    z_first = z_early + [over_core(z) for z in z_early]
+    z_second = z_late + [over_core(z) for z in z_late]
     base = call(
         gram_kernel,
         jax.ShapeDtypeStruct((ABLK, ABLK), f32),
-        [((ABLK, count // 2), bf16)],
+        [((ABLK, count * len(early) // rounds), bf16)],
         z_first,
-        ABLK * ABLK * count,
+        2 * ABLK * ABLK * count * len(early) // rounds,
     )
 
     update, inner = call(
         functools.partial(act_kernel, scale, len(z_second)),
         (jax.ShapeDtypeStruct((ABLK, half), bf16), jax.ShapeDtypeStruct((8, 128), f32)),
         [
-            ((ABLK, count // 2), bf16),
+            ((ABLK, count * len(late) // rounds), bf16),
             ((ABLK, ABLK), bf16),
             ((ABLK, half), f32),
             ((ABLK, half), bf16),
         ],
         [base, left, w_mine] + z_second,
-        ABLK * ABLK * (count + 6 * half),
-    )
-
-    total = jnp.where(at_home, inner[:1, :1], 0.0)
+        2 * ABLK * ABLK * (count * len(late) // rounds + 3 * half),
+    )
+
     back = [
         send(update[:, p * rows : (p + 1) * rows], home(p), back=True) for p in range(rounds)
     ]
-    total = total + over_core(total)
-    for d in [2**i for i in range(10) if 2**i < nt // 2]:
-        total = total + send(total, lambda h, l, y, c, d=d: (h, l, y ^ d, c))
-    for d in [2**i for i in range(10) if 2**i < m]:
-        total = total + over_lo(total, d)
-    for d in [2**i for i in range(10) if 2**i < high]:
-        total = total + send(total, lambda h, l, y, c, d=d: (h ^ d, l, y, c))
+    mine = jnp.where(at_home, inner[:1], 0.0)
+    heard = lax.all_to_all(jnp.broadcast_to(mine[None], (n * nt, 1, 128)), AXES, 0, 0)
+    total = jnp.sum(heard, axis=0)
     ratio = jnp.minimum(1.0, CLIP_LEVEL / jnp.sqrt(total[0, 0] / (DOUT * FF)))
 
-    even = sum(x.astype(jnp.float32) for x in back[0::2])
-    odd = sum(x.astype(jnp.float32) for x in back[1::2])
-    swap = (hi & 1) == 1
-    final = jnp.concatenate([jnp.where(swap, odd, even), jnp.where(swap, even, odd)], axis=0)
+    got_outer = sum(x.astype(f32) for p, x in enumerate(back) if outer_round(p))
+    got_inside = sum(x.astype(f32) for p, x in enumerate(back) if not outer_round(p))
+    final = jnp.concatenate(
+        [jnp.where(upper, got_inside, got_outer), jnp.where(upper, got_outer, got_inside)], axis=0
+    )
     new_momentum = MOMENTUM_RATE * momentum.T + ratio * final
     new_weight = weight.T - LEARN_RATE * new_momentum
     return (new_momentum.T, new_weight.T)

time: 178 us -> 151 us (0.85)
  starting transfers between devices: 91 us -> 61.2 us
  blocking collectives: 0 us -> 20.9 us
  waiting for transfers between devices: 31.3 us -> 15.9 us
  local copies, waits for them, and re-layouts: 4.7 us -> 11.7 us
  between operations: 4.84 us -> 1.11 us
  Pallas kernels: 39 us -> 36.1 us
    ppermute x27 -> x24, starting transfers between devices: 91 us -> 61.2 us  [send(): return lax.ppermute(value, AXES, pairs)]
    all_to_all x0 -> x1, blocking collectives: none -> 20.9 us  [per_device(): lax.all_to_all(jnp.broadcast_to(mine[None], (n * nt, 1, 128)), AXES, 0, 0)]
    ppermute x27 -> x24, waiting for transfers between devices: 31.3 us -> 15.9 us  [send(): return lax.ppermute(value, AXES, pairs)]
    unnamed x23 -> x33, local copies, waits for them, and re-layouts: 2.18 us -> 9.85 us
    pallas_call x3 -> x4, Pallas kernels: 39 us -> 36.1 us  [call(): pl.pallas_call(kernel, out_shape=out_shape, in_specs=[smem] * scalars + [...]
  transfers between devices with their start and end apart: 27 -> 24, of which waited for: 11 -> 3; matrix products, arithmetic and copies ran while one was open for 3% -> 1% of each run, Pallas kernels for 13% -> 16%
where the time goes in v3:
time: 151 us
  starting transfers between devices  61.2 us (41%)
  Pallas kernels  36.1 us (24%)
  blocking collectives  20.9 us (14%)
  waiting for transfers between devices  15.9 us (11%)
  local copies, waits for them, and re-layouts  11.7 us (8%)
  other arithmetic  3.39 us (2%)
    ppermute x24, starting transfers between devices, send(): return lax.ppermute(value, AXES, pairs)  61.2 us
    pallas_call x4, Pallas kernels, call(): pl.pallas_call(kernel, out_shape=out_shape, in_specs=[smem] * scalars + [...  36.1 us
    all_to_all x1, blocking collectives, per_device(): lax.all_to_all(jnp.broadcast_to(mine[None], (n * nt, 1, 128)), AXES, 0, 0)  20.9 us
    ppermute x24, waiting for transfers between devices, send(): return lax.ppermute(value, AXES, pairs)  15.9 us
    unnamed x33, local copies, waits for them, and re-layouts  9.85 us
  transfers between devices with their start and end apart: 24, of which 3 were waited for; matrix products, arithmetic and copies ran while one was open for 1% of the time, Pallas kernels for 16%

profile of v3, /device:TPU:0, one launch (start us, length us, event | category | flops | bytes accessed | tf_op | source)
XLA Modules:
  0.0 150.7 jit_solution(5408878846820350900)
XLA Ops:
  2.9 6.0 %collective-permute-start.2 = (bf16[1024,128]{1,0:T(8,128)(2,1)S(1)}, bf16[1024,128]{1,0:T(8,128)(2,1)S(1)}, u32[]{:S(2)}, u32[]{:S(2)}) collective-permute-start(bf16[1024,128]{1,0:T(8,128)(2,1)S(1)} %convolution_convert_fusion), channel_id=1, source_target_pairs={{0,16},{1,20},{2,18},{3,22},{4,17},{5,21},{6,19},{7,23},{24,8},{25... | collective-permute-start | bytes 786440 | tf_op jit(solution)/shard_map/ppermute | solution.py:216
  8.9 1.4 collective-permute-start.1
  10.3 3.1 %collective-permute-start = (bf16[1024,128]{1,0:T(8,128)(2,1)S(1)}, bf16[1024,128]{1,0:T(8,128)(2,1)}, u32[]{:S(2)}, u32[]{:S(2)}) collective-permute-start(bf16[1024,128]{1,0:T(8,128)(2,1)S(1)} %convolution_convert_fusion), channel_id=1, source_target_pairs={{0,8},{1,12},{2,10},{3,14},{4,9},{5,13},{6,11},{7,15},{24,16},{25,... | collective-permute-start | bytes 786440 | tf_op jit(solution)/shard_map/ppermute | solution.py:216
  13.4 1.8 %copy-done.1 = bf16[2,256,2736]{1,2,0:T(8,128)(2,1)S(1)} copy-done((bf16[2,256,2736]{1,2,0:T(8,128)(2,1)S(1)}, bf16[2,256,2736]{1,2,0:T(8,128)(2,1)}, u32[]{:S(2)}) %copy-start.1) | copy-done | bytes 2801688
  15.8 2.8 %shard_map.77 = (bf16[2,1368,128]{2,1,0:T(8,128)(2,1)S(1)}, bf16[2,1368,128]{2,1,0:T(8,128)(2,1)}) custom-call(s32[1]{0:T(128)} %bitcast.1.upper, s32[2,128]{1,0:T(2,128)S(1)} %copy-done.2, bf16[2,2736,256]{2,1,0:T(8,128)(2,1)S(1)} %bitcast.34), custom_call_target="tpu_custom_call" | custom-call | flops 358612992 | bytes 2802692 | tf_op jit(solution)/shard_map/pallas_call | solution.py:180
  19.6 1.5 %collective-permute-start.6 = (bf16[2,1368,128]{2,1,0:T(8,128)(2,1)S(1)}, bf16[2,1368,128]{2,1,0:T(8,128)(2,1)}, u32[]{:S(2)}, u32[]{:S(2)}) collective-permute-start(bf16[2,1368,128]{2,1,0:T(8,128)(2,1)S(1)} %get-tuple-element.13), channel_id=1, source_target_pairs={{8,8},{9,12},{10,10},{11,14},{12,9},{13,13},{14,11},{15,15},{16,16... | collective-permute-start | bytes 2101256 | tf_op jit(solution)/shard_map/ppermute | solution.py:216
  21.1 5.9 %collective-permute-start.4 = (bf16[2,1368,128]{2,1,0:T(8,128)(2,1)S(1)}, bf16[2,1368,128]{2,1,0:T(8,128)(2,1)S(1)}, u32[]{:S(2)}, u32[]{:S(2)}) collective-permute-start(bf16[2,1368,128]{2,1,0:T(8,128)(2,1)S(1)} %get-tuple-element.13), channel_id=1, source_target_pairs={{0,8},{1,12},{2,10},{3,14},{4,9},{5,13},{6,11},{7,15},{24,16},{25,... | collective-permute-start | bytes 2101256 | tf_op jit(solution)/shard_map/ppermute | solution.py:216
  27.0 1.6 %collective-permute-start.5 = (bf16[2,1368,128]{2,1,0:T(8,128)(2,1)}, bf16[2,1368,128]{2,1,0:T(8,128)(2,1)}, u32[]{:S(2)}, u32[]{:S(2)}) collective-permute-start(bf16[2,1368,128]{2,1,0:T(8,128)(2,1)} %get-tuple-element.17), channel_id=1, source_target_pairs={{8,16},{9,20},{10,18},{11,22},{12,17},{13,21},{14,19},{15,23},{16,... | collective-permute-start | bytes 2101256 | tf_op jit(solution)/shard_map/ppermute | solution.py:216
  28.6 11.5 %collective-permute-done.4.refs_0_ = bf16[2,1368,128]{2,1,0:T(8,128)(2,1)S(1)} collective-permute-done((bf16[2,1368,128]{2,1,0:T(8,128)(2,1)S(1)}, bf16[2,1368,128]{2,1,0:T(8,128)(2,1)S(1)}, u32[]{:S(2)}, u32[]{:S(2)}) %collective-permute-start.4) | collective-permute-done | bytes 700448 | tf_op jit(solution)/shard_map/ppermute | solution.py:216
  40.1 6.0 %collective-permute-start.12 = (bf16[1368,128]{1,0:T(8,128)(2,1)S(1)}, bf16[1368,128]{1,0:T(8,128)(2,1)S(1)}, u32[]{:S(2)}, u32[]{:S(2)}) collective-permute-start(bf16[1368,128]{1,0:T(8,128)(2,1)S(1)} %get-tuple-element.29), channel_id=1, source_target_pairs={{0,8},{1,12},{2,10},{3,14},{4,9},{5,13},{6,11},{7,15},{24,16},{25,... | collective-permute-start | bytes 1050632 | tf_op jit(solution)/shard_map/ppermute | solution.py:216
  48.1 1.6 %collective-permute-start.11 = (bf16[4,1024,128]{2,1,0:T(8,128)(2,1)S(1)}, bf16[4,1024,128]{2,1,0:T(8,128)(2,1)}, u32[]{:S(2)}, u32[]{:S(2)}) collective-permute-start(bf16[4,1024,128]{2,1,0:T(8,128)(2,1)S(1)} %pad_maximum_fusion.refs_0_), channel_id=1, source_target_pairs={{0,2},{1,3},{2,0},{3,1},{4,6},{5,7},{6,4},{7,5},{8,10},{9,11},{10,... | collective-permute-start | bytes 3145736 | tf_op jit(solution)/shard_map/ppermute | solution.py:216
  49.7 4.0 %collective-permute-start.14 = (bf16[1368,128]{1,0:T(8,128)(2,1)S(1)}, bf16[1368,128]{1,0:T(8,128)(2,1)S(1)}, u32[]{:S(2)}, u32[]{:S(2)}) collective-permute-start(bf16[1368,128]{1,0:T(8,128)(2,1)S(1)} %get-tuple-element.28), channel_id=1, source_target_pairs={{0,16},{1,20},{2,18},{3,22},{4,17},{5,21},{6,19},{7,23},{24,8},{25... | collective-permute-start | bytes 1050632 | tf_op jit(solution)/shard_map/ppermute | solution.py:216
  54.3 9.8 %collective-permute-start.9 = (bf16[2,1368,128]{2,1,0:T(8,128)(2,1)}, bf16[2,1368,128]{2,1,0:T(8,128)(2,1)S(1)}, u32[]{:S(2)}, u32[]{:S(2)}) collective-permute-start(bf16[2,1368,128]{2,1,0:T(8,128)(2,1)} %collective-permute-done.6.refs_2_), channel_id=1, source_target_pairs={{0,1},{1,0},{2,3},{3,2},{4,5},{5,4},{6,7},{7,6},{8,9},{9,8},{10,11... | collective-permute-start | bytes 2101256 | tf_op jit(solution)/shard_map/ppermute | solution.py:216
  64.6 3.2 %collective-permute-start.17 = (bf16[1368,512]{1,0:T(8,128)(2,1)S(1)}, bf16[1368,512]{1,0:T(8,128)(2,1)}, u32[]{:S(2)}, u32[]{:S(2)}) collective-permute-start(bf16[1368,512]{1,0:T(8,128)(2,1)S(1)} %constant_dynamic-update-slice_fusion.refs_4_.w_mine), channel_id=1, source_target_pairs={{0,1},{1,0},{2,3},{3,2},{4,5},{5,4},{6,7},{7,6},{8,9},{9,8},{10,11... | collective-permute-start | bytes 4202504 | tf_op jit(solution)/shard_map/ppermute | solution.py:216
  68.0 6.1 %collective-permute-start.10 = (bf16[4,1024,128]{2,1,0:T(8,128)(2,1)S(1)}, bf16[4,1024,128]{2,1,0:T(8,128)(2,1)}, u32[]{:S(2)}, u32[]{:S(2)}) collective-permute-start(bf16[4,1024,128]{2,1,0:T(8,128)(2,1)S(1)} %pad_maximum_fusion.refs_0_), channel_id=1, source_target_pairs={{0,1},{1,0},{2,3},{3,2},{4,5},{5,4},{6,7},{7,6},{8,9},{9,8},{10,11... | collective-permute-start | bytes 3145736 | tf_op jit(solution)/shard_map/ppermute | solution.py:216
  76.0 4.8 %collective-permute-start.18 = (bf16[2,1368,128]{2,1,0:T(8,128)(2,1)}, bf16[2,1368,128]{2,1,0:T(8,128)(2,1)}, u32[]{:S(2)}, u32[]{:S(2)}) collective-permute-start(bf16[2,1368,128]{2,1,0:T(8,128)(2,1)} %get-tuple-element.17), channel_id=1, source_target_pairs={{0,16},{1,20},{2,18},{3,22},{4,17},{5,21},{6,19},{7,23},{24,8},{25... | collective-permute-start | bytes 2101256 | tf_op jit(solution)/shard_map/ppermute | solution.py:216
  84.2 8.4 %shard_map.78.base = f32[1368,1368]{1,0:T(8,128)S(1)} custom-call(bf16[2,1368,128]{2,1,0:T(8,128)(2,1)S(1)} %copy-done.5, bf16[2,1368,128]{2,1,0:T(8,128)(2,1)} %collective-permute-done.5.refs_1_, bf16[2,1368,128]{2,1,0:T(8,128)(2,1)} %collective-permute-done.6.refs_2_, bf16[2,1368,128]{2,1,0:T(8,128)(2,1)S(1)} %copy-done.9, ...), custom_call_target="tpu_custom_call" | custom-call | flops 5749014528 | bytes 4202496 | tf_op jit(solution)/shard_map/pallas_call | solution.py:180
  92.6 3.5 %collective-permute-done.18.refs_0_ = bf16[2,1368,128]{2,1,0:T(8,128)(2,1)} collective-permute-done((bf16[2,1368,128]{2,1,0:T(8,128)(2,1)}, bf16[2,1368,128]{2,1,0:T(8,128)(2,1)}, u32[]{:S(2)}, u32[]{:S(2)}) %collective-permute-start.18) | collective-permute-done | bytes 700448 | tf_op jit(solution)/shard_map/ppermute | solution.py:216
  96.0 13.3 %shard_map.79.left = bf16[1368,512]{1,0:T(8,128)(2,1)S(1)} custom-call(s32[2]{0:T(128)S(1)} %pad_add_fusion.where, bf16[4,1024,128]{2,1,0:T(8,128)(2,1)S(1)} %pad_maximum_fusion.refs_0_, bf16[4,1024,128]{2,1,0:T(8,128)(2,1)} %collective-permute-done.10.refs_1_, bf16[4,1024,128]{2,1,0:T(8,128)(2,1)} %collective-permute-done.11.refs_2_, ...), custom_call_target="tpu_custom_call" | custom-call | flops 10024386560 | bytes 6995976 | tf_op jit(solution)/shard_map/pallas_call | solution.py:180
  109.4 11.7 %shard_map.80 = (bf16[1368,512]{1,0:T(8,128)(2,1)S(1)}, f32[8,128]{1,0:T(8,128)S(1)}) custom-call(f32[1368,1368]{1,0:T(8,128)S(1)} %shard_map.78.base, bf16[1368,512]{1,0:T(8,128)(2,1)S(1)} %shard_map.79.left, bf16[1368,512]{1,0:T(8,128)(2,1)S(1)} %constant_dynamic-update-slice_fusion.refs_4_.w_mine, bf16[2,1368,128]{2,1,0:T(8,128)(2,1)} %collective-permute-done.18.refs_0_, ...), custom_call_target="tpu_custom_call" | custom-call | flops 7665352704 | bytes 11688192 | tf_op jit(solution)/shard_map/pallas_call | solution.py:180
  122.0 1.3 collective-permute-start.22
  124.0 1.3 collective-permute-start.21
  126.0 20.9 %all_to_all.5 = f32[32,1,128]{2,1,0:T(1,128)S(1)} all-to-all(f32[32,1,128]{2,1,0:T(1,128)S(1)} %broadcast_in_dim.15), channel_id=1, replica_groups=mesh['shard'=8,'tensor'=4] {'shard','tensor'}, dimensions={0} | all-to-all | bytes 32768 | tf_op jit(solution)/shard_map/all_to_all | solution.py:321
  148.8 1.9 %fusion.1 = (f32[128,2736]{0,1:T(8,128)}, f32[128,2736]{0,1:T(8,128)}) fusion(f32[128,2736]{0,1:T(8,128)S(1)} %copy-done.10, f32[1368,128]{1,0:T(8,128)S(1)} %get-tuple-element.23, f32[1368,128]{1,0:T(8,128)S(1)} %get-tuple-element.22, f32[]{:T(128)} %bitcast.15, f32[128,2736]{0,1:T(8,128)S(1)} %copy-done.11), kind=kLoop, calls=%fused_computation.3 | loop fusion | flops 2101248 | bytes 7004164 | tf_op jit(solution)/shard_map/transpose | solution.py:332
  (74 shorter events, 16.4 us)
Async XLA Ops:
  2.2 16.3 %collective-permute-start.3 = (bf16[1024,128]{1,0:T(8,128)(2,1)S(1)}, bf16[1024,128]{1,0:T(8,128)(2,1)S(1)}, u32[]{:S(2)}, u32[]{:S(2)}) collective-permute-start(bf16[1024,128]{1,0:T(8,128)(2,1)S(1)} %convolution_convert_fusion), channel_id=1, source_target_pairs={{8,8},{9,12},{10,10},{11,14},{12,9},{13,13},{14,11},{15,15},{16,16... | collective-permute-start | bytes 786440 | tf_op jit(solution)/shard_map/ppermute | solution.py:216
  2.9 15.7 %collective-permute-start.2 = (bf16[1024,128]{1,0:T(8,128)(2,1)S(1)}, bf16[1024,128]{1,0:T(8,128)(2,1)S(1)}, u32[]{:S(2)}, u32[]{:S(2)}) collective-permute-start(bf16[1024,128]{1,0:T(8,128)(2,1)S(1)} %convolution_convert_fusion), channel_id=1, source_target_pairs={{0,16},{1,20},{2,18},{3,22},{4,17},{5,21},{6,19},{7,23},{24,8},{25... | collective-permute-start | bytes 786440 | tf_op jit(solution)/shard_map/ppermute | solution.py:216
  8.9 9.7 %collective-permute-start.1 = (bf16[1024,128]{1,0:T(8,128)(2,1)S(1)}, bf16[1024,128]{1,0:T(8,128)(2,1)}, u32[]{:S(2)}, u32[]{:S(2)}) collective-permute-start(bf16[1024,128]{1,0:T(8,128)(2,1)S(1)} %convolution_convert_fusion), channel_id=1, source_target_pairs={{8,16},{9,20},{10,18},{11,22},{12,17},{13,21},{14,19},{15,23},{16,... | collective-permute-start | bytes 786440 | tf_op jit(solution)/shard_map/ppermute | solution.py:216
  10.3 9.3 %collective-permute-start = (bf16[1024,128]{1,0:T(8,128)(2,1)S(1)}, bf16[1024,128]{1,0:T(8,128)(2,1)}, u32[]{:S(2)}, u32[]{:S(2)}) collective-permute-start(bf16[1024,128]{1,0:T(8,128)(2,1)S(1)} %convolution_convert_fusion), channel_id=1, source_target_pairs={{0,8},{1,12},{2,10},{3,14},{4,9},{5,13},{6,11},{7,15},{24,16},{25,... | collective-permute-start | bytes 786440 | tf_op jit(solution)/shard_map/ppermute | solution.py:216
  19.6 9.0 %collective-permute-start.6 = (bf16[2,1368,128]{2,1,0:T(8,128)(2,1)S(1)}, bf16[2,1368,128]{2,1,0:T(8,128)(2,1)}, u32[]{:S(2)}, u32[]{:S(2)}) collective-permute-start(bf16[2,1368,128]{2,1,0:T(8,128)(2,1)S(1)} %get-tuple-element.13), channel_id=1, source_target_pairs={{8,8},{9,12},{10,10},{11,14},{12,9},{13,13},{14,11},{15,15},{16,16... | collective-permute-start | bytes 2101256 | tf_op jit(solution)/shard_map/ppermute | solution.py:216
  21.1 19.0 %collective-permute-start.4 = (bf16[2,1368,128]{2,1,0:T(8,128)(2,1)S(1)}, bf16[2,1368,128]{2,1,0:T(8,128)(2,1)S(1)}, u32[]{:S(2)}, u32[]{:S(2)}) collective-permute-start(bf16[2,1368,128]{2,1,0:T(8,128)(2,1)S(1)} %get-tuple-element.13), channel_id=1, source_target_pairs={{0,8},{1,12},{2,10},{3,14},{4,9},{5,13},{6,11},{7,15},{24,16},{25,... | collective-permute-start | bytes 2101256 | tf_op jit(solution)/shard_map/ppermute | solution.py:216
  27.0 13.0 %collective-permute-start.5 = (bf16[2,1368,128]{2,1,0:T(8,128)(2,1)}, bf16[2,1368,128]{2,1,0:T(8,128)(2,1)}, u32[]{:S(2)}, u32[]{:S(2)}) collective-permute-start(bf16[2,1368,128]{2,1,0:T(8,128)(2,1)} %get-tuple-element.17), channel_id=1, source_target_pairs={{8,16},{9,20},{10,18},{11,22},{12,17},{13,21},{14,19},{15,23},{16,... | collective-permute-start | bytes 2101256 | tf_op jit(solution)/shard_map/ppermute | solution.py:216
  40.1 14.2 %collective-permute-start.12 = (bf16[1368,128]{1,0:T(8,128)(2,1)S(1)}, bf16[1368,128]{1,0:T(8,128)(2,1)S(1)}, u32[]{:S(2)}, u32[]{:S(2)}) collective-permute-start(bf16[1368,128]{1,0:T(8,128)(2,1)S(1)} %get-tuple-element.29), channel_id=1, source_target_pairs={{0,8},{1,12},{2,10},{3,14},{4,9},{5,13},{6,11},{7,15},{24,16},{25,... | collective-permute-start | bytes 1050632 | tf_op jit(solution)/shard_map/ppermute | solution.py:216
  46.1 18.1 %collective-permute-start.13 = (bf16[1368,128]{1,0:T(8,128)(2,1)S(1)}, bf16[1368,128]{1,0:T(8,128)(2,1)S(1)}, u32[]{:S(2)}, u32[]{:S(2)}) collective-permute-start(bf16[1368,128]{1,0:T(8,128)(2,1)S(1)} %get-tuple-element.28), channel_id=1, source_target_pairs={{8,16},{9,20},{10,18},{11,22},{12,17},{13,21},{14,19},{15,23},{16,... | collective-permute-start | bytes 1050632 | tf_op jit(solution)/shard_map/ppermute | solution.py:216
  48.1 19.9 %collective-permute-start.11 = (bf16[4,1024,128]{2,1,0:T(8,128)(2,1)S(1)}, bf16[4,1024,128]{2,1,0:T(8,128)(2,1)}, u32[]{:S(2)}, u32[]{:S(2)}) collective-permute-start(bf16[4,1024,128]{2,1,0:T(8,128)(2,1)S(1)} %pad_maximum_fusion.refs_0_), channel_id=1, source_target_pairs={{0,2},{1,3},{2,0},{3,1},{4,6},{5,7},{6,4},{7,5},{8,10},{9,11},{10,... | collective-permute-start | bytes 3145736 | tf_op jit(solution)/shard_map/ppermute | solution.py:216
  49.7 14.8 %collective-permute-start.14 = (bf16[1368,128]{1,0:T(8,128)(2,1)S(1)}, bf16[1368,128]{1,0:T(8,128)(2,1)S(1)}, u32[]{:S(2)}, u32[]{:S(2)}) collective-permute-start(bf16[1368,128]{1,0:T(8,128)(2,1)S(1)} %get-tuple-element.28), channel_id=1, source_target_pairs={{0,16},{1,20},{2,18},{3,22},{4,17},{5,21},{6,19},{7,23},{24,8},{25... | collective-permute-start | bytes 1050632 | tf_op jit(solution)/shard_map/ppermute | solution.py:216
  53.6 10.9 %collective-permute-start.15 = (bf16[1368,128]{1,0:T(8,128)(2,1)S(1)}, bf16[1368,128]{1,0:T(8,128)(2,1)S(1)}, u32[]{:S(2)}, u32[]{:S(2)}) collective-permute-start(bf16[1368,128]{1,0:T(8,128)(2,1)S(1)} %get-tuple-element.29), channel_id=1, source_target_pairs={{8,8},{9,12},{10,10},{11,14},{12,9},{13,13},{14,11},{15,15},{16,16... | collective-permute-start | bytes 1050632 | tf_op jit(solution)/shard_map/ppermute | solution.py:216
  54.3 19.8 %collective-permute-start.9 = (bf16[2,1368,128]{2,1,0:T(8,128)(2,1)}, bf16[2,1368,128]{2,1,0:T(8,128)(2,1)S(1)}, u32[]{:S(2)}, u32[]{:S(2)}) collective-permute-start(bf16[2,1368,128]{2,1,0:T(8,128)(2,1)} %collective-permute-done.6.refs_2_), channel_id=1, source_target_pairs={{0,1},{1,0},{2,3},{3,2},{4,5},{5,4},{6,7},{7,6},{8,9},{9,8},{10,11... | collective-permute-start | bytes 2101256 | tf_op jit(solution)/shard_map/ppermute | solution.py:216
  64.3 10.8 %collective-permute-start.7 = (bf16[2,1368,128]{2,1,0:T(8,128)(2,1)S(1)}, bf16[2,1368,128]{2,1,0:T(8,128)(2,1)S(1)}, u32[]{:S(2)}, u32[]{:S(2)}) collective-permute-start(bf16[2,1368,128]{2,1,0:T(8,128)(2,1)S(1)} %copy-done.4), channel_id=1, source_target_pairs={{0,1},{1,0},{2,3},{3,2},{4,5},{5,4},{6,7},{7,6},{8,9},{9,8},{10,11... | collective-permute-start | bytes 2101256 | tf_op jit(solution)/shard_map/ppermute | solution.py:216
  64.6 31.4 %collective-permute-start.17 = (bf16[1368,512]{1,0:T(8,128)(2,1)S(1)}, bf16[1368,512]{1,0:T(8,128)(2,1)}, u32[]{:S(2)}, u32[]{:S(2)}) collective-permute-start(bf16[1368,512]{1,0:T(8,128)(2,1)S(1)} %constant_dynamic-update-slice_fusion.refs_4_.w_mine), channel_id=1, source_target_pairs={{0,1},{1,0},{2,3},{3,2},{4,5},{5,4},{6,7},{7,6},{8,9},{9,8},{10,11... | collective-permute-start | bytes 4202504 | tf_op jit(solution)/shard_map/ppermute | solution.py:216
  67.9 13.0 %collective-permute-start.8 = (bf16[2,1368,128]{2,1,0:T(8,128)(2,1)}, bf16[2,1368,128]{2,1,0:T(8,128)(2,1)}, u32[]{:S(2)}, u32[]{:S(2)}) collective-permute-start(bf16[2,1368,128]{2,1,0:T(8,128)(2,1)} %collective-permute-done.5.refs_1_), channel_id=1, source_target_pairs={{0,1},{1,0},{2,3},{3,2},{4,5},{5,4},{6,7},{7,6},{8,9},{9,8},{10,11... | collective-permute-start | bytes 2101256 | tf_op jit(solution)/shard_map/ppermute | solution.py:216
  68.0 28.1 %collective-permute-start.10 = (bf16[4,1024,128]{2,1,0:T(8,128)(2,1)S(1)}, bf16[4,1024,128]{2,1,0:T(8,128)(2,1)}, u32[]{:S(2)}, u32[]{:S(2)}) collective-permute-start(bf16[4,1024,128]{2,1,0:T(8,128)(2,1)S(1)} %pad_maximum_fusion.refs_0_), channel_id=1, source_target_pairs={{0,1},{1,0},{2,3},{3,2},{4,5},{5,4},{6,7},{7,6},{8,9},{9,8},{10,11... | collective-permute-start | bytes 3145736 | tf_op jit(solution)/shard_map/ppermute | solution.py:216
  75.0 21.0 %collective-permute-start.16 = (bf16[4,1024,128]{2,1,0:T(8,128)(2,1)}, bf16[4,1024,128]{2,1,0:T(8,128)(2,1)}, u32[]{:S(2)}, u32[]{:S(2)}) collective-permute-start(bf16[4,1024,128]{2,1,0:T(8,128)(2,1)} %collective-permute-done.11.refs_2_), channel_id=1, source_target_pairs={{0,1},{1,0},{2,3},{3,2},{4,5},{5,4},{6,7},{7,6},{8,9},{9,8},{10,11... | collective-permute-start | bytes 3145736 | tf_op jit(solution)/shard_map/ppermute | solution.py:216
  76.0 20.0 %collective-permute-start.18 = (bf16[2,1368,128]{2,1,0:T(8,128)(2,1)}, bf16[2,1368,128]{2,1,0:T(8,128)(2,1)}, u32[]{:S(2)}, u32[]{:S(2)}) collective-permute-start(bf16[2,1368,128]{2,1,0:T(8,128)(2,1)} %get-tuple-element.17), channel_id=1, source_target_pairs={{0,16},{1,20},{2,18},{3,22},{4,17},{5,21},{6,19},{7,23},{24,8},{25... | collective-permute-start | bytes 2101256 | tf_op jit(solution)/shard_map/ppermute | solution.py:216
  96.0 13.3 %collective-permute-start.19 = (bf16[2,1368,128]{2,1,0:T(8,128)(2,1)}, bf16[2,1368,128]{2,1,0:T(8,128)(2,1)S(1)}, u32[]{:S(2)}, u32[]{:S(2)}) collective-permute-start(bf16[2,1368,128]{2,1,0:T(8,128)(2,1)} %collective-permute-done.18.refs_0_), channel_id=1, source_target_pairs={{0,1},{1,0},{2,3},{3,2},{4,5},{5,4},{6,7},{7,6},{8,9},{9,8},{10,11... | collective-permute-start | bytes 2101256 | tf_op jit(solution)/shard_map/ppermute | solution.py:216
  122.0 25.1 %collective-permute-start.22 = (bf16[1368,128]{1,0:T(8,128)(2,1)}, bf16[1368,128]{1,0:T(8,128)(2,1)S(1)}, u32[]{:S(2)}, u32[]{:S(2)}) collective-permute-start(bf16[1368,128]{1,0:T(8,128)(2,1)} %get-tuple-element.24), channel_id=1, source_target_pairs={{8,0},{12,1},{10,2},{14,3},{9,4},{13,5},{11,6},{15,7},{16,24},{20,... | collective-permute-start | bytes 1050632 | tf_op jit(solution)/shard_map/ppermute | solution.py:216
  123.3 23.8 %collective-permute-start.23 = (bf16[1368,128]{1,0:T(8,128)(2,1)S(1)}, bf16[1368,128]{1,0:T(8,128)(2,1)S(1)}, u32[]{:S(2)}, u32[]{:S(2)}) collective-permute-start(bf16[1368,128]{1,0:T(8,128)(2,1)S(1)} %get-tuple-element.25), channel_id=1, source_target_pairs={{8,8},{12,9},{10,10},{14,11},{9,12},{13,13},{11,14},{15,15},{16,16... | collective-permute-start | bytes 1050632 | tf_op jit(solution)/shard_map/ppermute | solution.py:216
  124.0 23.1 %collective-permute-start.21 = (bf16[1368,128]{1,0:T(8,128)(2,1)S(1)}, bf16[1368,128]{1,0:T(8,128)(2,1)S(1)}, u32[]{:S(2)}, u32[]{:S(2)}) collective-permute-start(bf16[1368,128]{1,0:T(8,128)(2,1)S(1)} %get-tuple-element.26), channel_id=1, source_target_pairs={{16,0},{20,1},{18,2},{22,3},{17,4},{21,5},{19,6},{23,7},{8,24},{12... | collective-permute-start | bytes 1050632 | tf_op jit(solution)/shard_map/ppermute | solution.py:216
  125.3 21.8 %collective-permute-start.20 = (bf16[1368,128]{1,0:T(8,128)(2,1)S(1)}, bf16[1368,128]{1,0:T(8,128)(2,1)S(1)}, u32[]{:S(2)}, u32[]{:S(2)}) collective-permute-start(bf16[1368,128]{1,0:T(8,128)(2,1)S(1)} %get-tuple-element.27), channel_id=1, source_target_pairs={{16,8},{20,9},{18,10},{22,11},{17,12},{21,13},{19,14},{23,15},{8,1... | collective-permute-start | bytes 1050632 | tf_op jit(solution)/shard_map/ppermute | solution.py:216
  (15 other events, 79.6 us)

commit v4 on v3

--- a/solution.py
+++ b/solution.py
@@ -17,7 +17,6 @@
 LEARN_RATE = 0.5
 
 AXES = ("shard", "tensor")
-VMEM_MIB = 32
 ORDER = (0, 2, 3, 1)
 
 
@@ -62,20 +61,23 @@
     return 1.0 / norm, shift / norm
 
 
-def lay_out(parts, wide):
+def lay_out(parts, wide, chunks=None):
     at = 0
     for part in parts:
-        count, _, lanes = part.shape
-        for i in range(count):
+        lanes = part.shape[2]
+        for i in range(part.shape[0]) if chunks is None else chunks:
             wide[:, at : at + lanes] = part[i]
             at += lanes
 
 
-def gram_kernel(*refs):
-    *parts, out, wide = refs
-    lay_out(parts, wide)
-    for at, size in row_tiles(out.shape[0], 352):
-        out[at : at + size, :] = dot_nt(wide[at : at + size, :], wide[...])
+def gram_kernel(samples, *refs):
+    *parts, gram, taken, wide = refs
+    rows = taken.shape[1] // len(parts)
+    for i, part in enumerate(parts):
+        taken[:, i * rows : (i + 1) * rows] = part[samples]
+    lay_out(parts, wide, range(samples))
+    for at, size in row_tiles(gram.shape[0], 352):
+        gram[at : at + size, :] = dot_nt(wide[at : at + size, :], wide[...])
 
 
 def factor_gram(wide, base, gram, scale):
@@ -87,47 +89,56 @@
             tile = tile + base[at : at + size, :]
         tile = tile * scale
         gram[at : at + size, :] = tile.astype(jnp.bfloat16)
-        row = lax.broadcasted_iota(jnp.int32, tile.shape, 0) + at
-        column = lax.broadcasted_iota(jnp.int32, tile.shape, 1)
-        trace = trace + jnp.sum(jnp.where(row == column, tile, 0.0))
+        near = at // 128 * 128
+        square = tile[:, near : at + size]
+        row = lax.broadcasted_iota(jnp.int32, square.shape, 0) + (at - near)
+        column = lax.broadcasted_iota(jnp.int32, square.shape, 1)
+        trace = trace + jnp.sum(jnp.where(row == column, square, 0.0))
         squares = squares + jnp.sum(tile * tile)
     return trace, squares
 
 
-def pick_kernel(upper, index, tokens, outer, inside):
+def pick_kernel(upper, index, tokens, grad_rows, outer, inside):
     batches, _, count = tokens.shape
     picks = index.shape[1]
+
+    def put(block, i, value):
+        @pl.when(upper[0] == block)
+        def _():
+            outer[i] = value
+
+        @pl.when(upper[0] != block)
+        def _():
+            inside[i] = value
+
     for i in range(batches):
         row = lax.broadcasted_iota(jnp.int32, (count, picks), 0)
         hot = (row == index[i : i + 1, :]).astype(jnp.float32).astype(jnp.bfloat16)
         chosen = dot_nn(tokens[i], hot)
         for block in range(2):
-            part = chosen[block * ABLK : (block + 1) * ABLK].astype(jnp.bfloat16)
-
-            @pl.when(upper[0] == block)
-            def _():
-                outer[i] = part
-
-            @pl.when(upper[0] != block)
-            def _():
-                inside[i] = part
+            put(block, i, chosen[block * ABLK : (block + 1) * ABLK].astype(jnp.bfloat16))
+    rows = grad_rows[...].astype(jnp.float32)
+    for block in range(2):
+        put(block, batches, rows[block * ABLK : (block + 1) * ABLK].astype(jnp.bfloat16))
 
 
 def grad_kernel(scale, rows, high, m, where, *refs):
-    *q_parts, w_mine, w_other, left, wide, gram, poly, all_rows = refs
+    *q_parts, poly, wide, gram = refs
     width = gram.shape[0]
-    half = w_mine.shape[1]
+    half = poly.shape[0]
     lay_out(q_parts, wide)
     trace, squares = factor_gram(wide, None, gram, scale)
     norm, shift = damping_terms(trace, squares, width)
     rounds = half // rows
-    at = lax.broadcasted_iota(jnp.int32, (width, width), 0)
+    at = lax.broadcasted_iota(jnp.int32, (width, 128), 0)
     piece = at // rows
     arrival, other = piece % rounds, piece // rounds
-    turn = arrival % high
-    position = sum(jnp.where(turn == i, ORDER[i], 0) for i in range(high))
-    shard = mirrored(position, where[0]) * m + 2 * (arrival // high) + (other ^ where[1])
-    place = shard * rows + at % rows
+    late, pair = arrival // (rounds // 2), arrival % (rounds // 2)
+    turn = 2 * late + pair % 2
+    position = sum(jnp.where(turn == i, p, 0) for i, p in enumerate(ORDER))
+    low = 2 * (pair // 2) + (other ^ where[1])
+    shard = mirrored(position, where[0]) * m + low
+    place = (shard * rows + at % rows)[:, :1]
     hot = (place == lax.broadcasted_iota(jnp.int32, (width, width), 1)).astype(jnp.float32)
     hot = hot.astype(jnp.bfloat16)
     own = hot[:half]
@@ -138,21 +149,28 @@
     y3 = norm * dot_nn(y2_low, gram[...]) + shift * y2
     total = (4.0 * y2 - 6.0 * y1 - y3).astype(jnp.bfloat16)
     poly[...] = dot_nt(total, hot).astype(jnp.bfloat16)
-    all_rows[:, :half] = w_mine[...]
-    all_rows[:, half:] = w_other[...]
-    for at, size in row_tiles(left.shape[0], 352):
+
+
+def act_kernel(scale, samples, base, poly, taken, *refs):
+    *parts, update, inner, all_rows, left, wide, gram, first, second = refs
+    width = gram.shape[0]
+    half = update.shape[1]
+    on_time = taken.shape[1] // 2
+    for i in range(2):
+        all_rows[:, i * half : i * half + on_time] = taken[:, i * on_time : (i + 1) * on_time]
+        late = parts[i * len(parts) // 2 : (i + 1) * len(parts) // 2]
+        rows = (half - on_time) // len(late)
+        for k, part in enumerate(late):
+            at = i * half + on_time + k * rows
+            all_rows[:, at : at + rows] = part[samples][:, :rows]
+    tiles = row_tiles(width, 352)
+    for at, size in tiles:
         mixed = dot_nt(all_rows[at : at + size, :], poly[...])
-        mixed = mixed + 4.0 * w_mine[at : at + size, :].astype(jnp.float32)
+        mixed = mixed + 4.0 * all_rows[at : at + size, :half].astype(jnp.float32)
         left[at : at + size, :] = mixed.astype(jnp.bfloat16)
-
-
-def act_kernel(scale, parts, base, left, w_mine, *refs):
-    *refs, update, inner, wide, gram, first, second = refs
-    lay_out(refs, wide)
-    width = gram.shape[0]
+    lay_out(parts, wide, range(samples))
     trace, squares = factor_gram(wide, base, gram, scale)
     norm, shift = damping_terms(trace, squares, width)
-    tiles = row_tiles(width, 352)
     for at, size in tiles:
         rows = left[at : at + size, :].astype(jnp.float32)
         step = norm * dot_nn(gram[at : at + size, :], left[...]) + shift * rows
@@ -168,12 +186,12 @@
         rows = left[at : at + size, :].astype(jnp.float32)
         step = norm * dot_nn(gram[at : at + size, :], second[...])
         done = step + shift * first[at : at + size, :] + 4.0 * rows
-        total = total + jnp.sum(done * w_mine[at : at + size, :].astype(jnp.float32))
+        total = total + jnp.sum(done * all_rows[at : at + size, :half].astype(jnp.float32))
         update[at : at + size, :] = done.astype(jnp.bfloat16)
     inner[...] = jnp.full(inner.shape, total, jnp.float32)
 
 
-def call(kernel, out_shape, scratch, operands, flops, scalars=0):
+def call(kernel, out_shape, scratch, operands, flops, vmem_mib, scalars=0):
     vmem = pl.BlockSpec(memory_space=pltpu.VMEM)
     smem = pl.BlockSpec(memory_space=pltpu.SMEM)
     moved = sum(x.size * x.dtype.itemsize for x in operands)
@@ -183,7 +201,7 @@
         in_specs=[smem] * scalars + [vmem] * (len(operands) - scalars),
         out_specs=jax.tree.map(lambda _: vmem, out_shape),
         scratch_shapes=[pltpu.VMEM(shape, dtype) for shape, dtype in scratch],
-        compiler_params=pltpu.CompilerParams(vmem_limit_bytes=VMEM_MIB * 2**20),
+        compiler_params=pltpu.CompilerParams(vmem_limit_bytes=vmem_mib * 2**20),
         cost_estimate=pl.CostEstimate(flops=flops, bytes_accessed=moved, transcendentals=0),
     )(*operands)
 
@@ -246,76 +264,85 @@
     my_idx = lax.dynamic_index_in_dim(sample_idx, col // 2, 0, keepdims=False)
     q = pick_transposed(tokens_t, my_idx)
     q_own = [send(q, home(p)) for p in range(rounds)]
-    q_same = jnp.stack(q_own)
-    q_parts = [q_same, over_core(q_same)]
-
     bf16, f32 = jnp.bfloat16, jnp.float32
+    assert rows == picks or n > 8
+    grad_t = grad_weight.T
+    if rows < picks:
+        grad_t = jnp.pad(grad_t, ((0, 0), (0, picks - rows)))
     outer, inside = call(
         pick_kernel,
-        (jax.ShapeDtypeStruct((batches, ABLK, picks), bf16),) * 2,
+        (jax.ShapeDtypeStruct((batches + 1, ABLK, picks), bf16),) * 2,
         [],
-        [upper.astype(jnp.int32).reshape(1), sample_idx, jnp.swapaxes(hidden_acts, 1, 2)],
+        [upper.astype(jnp.int32).reshape(1), sample_idx, jnp.swapaxes(hidden_acts, 1, 2), grad_t],
         2 * batches * picks * hidden * hidden_acts.shape[1],
+        vmem_mib=12,
         scalars=1,
     )
-    late = [p for p in range(rounds) if p % high == 2]
-    early = [p for p in range(rounds) if p % high != 2]
-    outer, inside = after((outer, inside), q_own)
-    z_early = [send(outer if outer_round(p) else inside, home(p)) for p in early]
-
-    grad_t = after(grad_weight.T, z_early)
-    first = jnp.where(upper, ABLK, 0)
-    w_outer = lax.dynamic_slice_in_dim(grad_t, first, ABLK, 0)
-    w_inside = lax.dynamic_slice_in_dim(grad_t, ABLK - first, ABLK, 0)
-    w_own = [send(w_outer if outer_round(p) else w_inside, home(p)) for p in range(rounds)]
-    w_mine = jnp.concatenate(w_own, axis=1)
-    w_other = over_core(w_mine)
-
-    inside = after(inside, w_own)
-    z_late = [send(inside, home(p)) for p in late]
-
-    for d in range(1, nt // 2):
-        q_far = send(q_same, lambda h, l, y, c, d=d: (h, l, y ^ d, c))
-        q_parts += [q_far, over_core(after(q_far, w_own))]
+    late = [p for p in range(rounds) if p % high >= 2]
+    early = [p for p in range(rounds) if p % high < 2]
+    facing = lambda parts: [x for p, x in enumerate(parts) if p % high < 2]
+    q_same = after(jnp.stack(q_own), [outer, inside])
+    q_far = [
+        send(q_same, lambda h, l, y, c, d=d: (h, l, y ^ d, c)) for d in range(1, nt // 2)
+    ]
+    turn = lambda p, pair: send(pair[0] if outer_round(p) else pair[1], home(p))
+    on_time = [turn(p, (outer, inside)) for p in early]
+
+    pair = after((outer, inside), on_time)
+    tardy = [turn(p, pair) for p in late]
+    on_time_other = [over_core(x) for x in on_time]
+    q_parts = [q_same] + q_far
+    q_parts = q_parts + [over_core(x) for x in q_parts]
 
     count = batches * picks * n
     scale = 1.0 / count
     half = rounds * rows
     where = jnp.stack([mine_j & 1, core]).astype(jnp.int32)
-    left = call(
+    poly = call(
         functools.partial(grad_kernel, scale, rows, high, m),
-        jax.ShapeDtypeStruct((ABLK, half), bf16),
-        [((DOUT, count), bf16), ((DOUT, DOUT), bf16), ((half, DOUT), bf16), ((ABLK, DOUT), bf16)],
-        [where, *q_parts, w_mine, w_other],
-        2 * DOUT * (DOUT * count + 4 * half * DOUT + ABLK * half),
+        jax.ShapeDtypeStruct((half, DOUT), bf16),
+        [((DOUT, count), bf16), ((DOUT, DOUT), bf16)],
+        [where, *q_parts],
+        2 * DOUT * (DOUT * count + 4 * half * DOUT),
+        vmem_mib=28 if n == 8 else 46,
         scalars=1,
     )
-
-    z_first = z_early + [over_core(z) for z in z_early]
-    z_second = z_late + [over_core(z) for z in z_late]
-    base = call(
-        gram_kernel,
-        jax.ShapeDtypeStruct((ABLK, ABLK), f32),
-        [((ABLK, count * len(early) // rounds), bf16)],
-        z_first,
-        2 * ABLK * ABLK * count * len(early) // rounds,
-    )
-
+    share = len(early) / rounds
+    base, taken = call(
+        functools.partial(gram_kernel, batches),
+        (
+            jax.ShapeDtypeStruct((ABLK, ABLK), f32),
+            jax.ShapeDtypeStruct((ABLK, 2 * len(early) * picks), bf16),
+        ),
+        [((ABLK, int(count * share)), bf16)],
+        on_time + on_time_other,
+        int(2 * ABLK * ABLK * count * share),
+        vmem_mib=12 if n == 8 else 40,
+    )
+    if rows < picks:
+        taken = taken.reshape(ABLK, -1, picks)[:, :, :rows].reshape(ABLK, -1)
+
+    tardy = after(tardy, [poly, base] + tardy)
+    tardy = tardy + [over_core(x) for x in tardy]
     update, inner = call(
-        functools.partial(act_kernel, scale, len(z_second)),
+        functools.partial(act_kernel, scale, batches),
         (jax.ShapeDtypeStruct((ABLK, half), bf16), jax.ShapeDtypeStruct((8, 128), f32)),
         [
-            ((ABLK, count * len(late) // rounds), bf16),
+            ((ABLK, DOUT), bf16),
+            ((ABLK, half), bf16),
+            ((ABLK, count - int(count * share)), bf16),
             ((ABLK, ABLK), bf16),
             ((ABLK, half), f32),
             ((ABLK, half), bf16),
         ],
-        [base, left, w_mine] + z_second,
-        2 * ABLK * ABLK * (count * len(late) // rounds + 3 * half),
+        [base, poly, taken] + tardy,
+        int(2 * ABLK * (ABLK * (count * (1 - share) + 3 * half) + half * DOUT)),
+        vmem_mib=28 if n == 8 else 46,
     )
 
     back = [
-        send(update[:, p * rows : (p + 1) * rows], home(p), back=True) for p in range(rounds)
+        send(update[:, a * rows : (a + 1) * rows], home(p), back=True)
+        for p, a in sorted((p, a) for a, p in enumerate(early + late))
     ]
     mine = jnp.where(at_home, inner[:1], 0.0)
     heard = lax.all_to_all(jnp.broadcast_to(mine[None], (n * nt, 1, 128)), AXES, 0, 0)

time: 151 us -> 126 us (0.83)
  starting transfers between devices: 61.2 us -> 31.7 us
  waiting for transfers between devices: 15.9 us -> 23 us
  local copies, waits for them, and re-layouts: 11.7 us -> 8.17 us
    ppermute x24 -> x19, starting transfers between devices: 61.2 us -> 31.7 us  [send(): return lax.ppermute(value, AXES, pairs)]
    ppermute x24 -> x19, waiting for transfers between devices: 15.9 us -> 23 us  [send(): return lax.ppermute(value, AXES, pairs)]
    unnamed x33 -> x20, local copies, waits for them, and re-layouts: 9.85 us -> 6.41 us
  transfers between devices with their start and end apart: 24 -> 19, of which waited for: 3 -> 5; matrix products, arithmetic and copies ran while one was open for 1% -> 1% of each run, Pallas kernels for 16% -> 17%
where the time goes in v4:
time: 126 us; the launch traced here: 125 us
  Pallas kernels  35.2 us (28%)
  starting transfers between devices  31.7 us (25%)
  waiting for transfers between devices  23 us (18%)
  blocking collectives  22.1 us (18%)
  local copies, waits for them, and re-layouts  8.17 us (6%)
  other arithmetic  3.43 us (3%)
    pallas_call x4, Pallas kernels, call(): pl.pallas_call(kernel, out_shape=out_shape, in_specs=[smem] * scalars + [...  35.2 us
    ppermute x19, starting transfers between devices, send(): return lax.ppermute(value, AXES, pairs)  31.7 us
    ppermute x19, waiting for transfers between devices, send(): return lax.ppermute(value, AXES, pairs)  23 us
    all_to_all x1, blocking collectives, per_device(): lax.all_to_all(jnp.broadcast_to(mine[None], (n * nt, 1, 128)), AXES, 0, 0)  22.1 us
    unnamed x20, local copies, waits for them, and re-layouts  6.41 us
  transfers between devices with their start and end apart: 19, of which 5 were waited for; matrix products, arithmetic and copies ran while one was open for 1% of the time, Pallas kernels for 17%

profile of v4, /device:TPU:0, one launch (start us, length us, event | category | flops | bytes accessed | tf_op | source)
XLA Modules:
  0.0 125.0 jit_solution(10168275589774736777)
XLA Ops:
  2.9 6.0 %collective-permute-start.6 = (bf16[1024,128]{1,0:T(8,128)(2,1)S(1)}, bf16[1024,128]{1,0:T(8,128)(2,1)S(1)}, u32[]{:S(2)}, u32[]{:S(2)}) collective-permute-start(bf16[1024,128]{1,0:T(8,128)(2,1)S(1)} %convolution_convert_fusion), channel_id=1, source_target_pairs={{0,16},{1,20},{2,18},{3,22},{4,17},{5,21},{6,19},{7,23},{24,8},{25... | collective-permute-start | bytes 786440 | tf_op jit(solution)/shard_map/ppermute | solution.py:234
  9.6 3.1 %collective-permute-start.4 = (bf16[1024,128]{1,0:T(8,128)(2,1)S(1)}, bf16[1024,128]{1,0:T(8,128)(2,1)S(1)}, u32[]{:S(2)}, u32[]{:S(2)}) collective-permute-start(bf16[1024,128]{1,0:T(8,128)(2,1)S(1)} %convolution_convert_fusion), channel_id=1, source_target_pairs={{0,8},{1,12},{2,10},{3,14},{4,9},{5,13},{6,11},{7,15},{24,16},{25,... | collective-permute-start | bytes 786440 | tf_op jit(solution)/shard_map/ppermute | solution.py:234
  12.7 1.8 %copy-done.1 = bf16[2,256,2736]{1,2,0:T(8,128)(2,1)S(1)} copy-done((bf16[2,256,2736]{1,2,0:T(8,128)(2,1)S(1)}, bf16[2,256,2736]{1,2,0:T(8,128)(2,1)}, u32[]{:S(2)}) %copy-start.1) | copy-done | bytes 2801688
  14.5 1.1 copy-done.2
  16.3 2.1 %shard_map.77 = (bf16[3,1368,128]{2,1,0:T(8,128)(2,1)S(1)}, bf16[3,1368,128]{2,1,0:T(8,128)(2,1)S(1)}) custom-call(s32[1]{0:T(128)} %bitcast.1.upper, s32[2,128]{1,0:T(2,128)S(1)} %copy-done.3, bf16[2,2736,256]{2,1,0:T(8,128)(2,1)S(1)} %bitcast.34, bf16[2736,128]{1,0:T(8,128)(2,1)S(1)} %bitcast.35), custom_call_target="tpu_custom_call" | custom-call | flops 358612992 | bytes 3503108 | tf_op jit(solution)/shard_map/pallas_call | solution.py:198
  18.4 2.3 %collective-permute-start = (bf16[3,1368,128]{2,1,0:T(8,128)(2,1)S(1)}, bf16[3,1368,128]{2,1,0:T(8,128)(2,1)}, u32[]{:S(2)}, u32[]{:S(2)}) collective-permute-start(bf16[3,1368,128]{2,1,0:T(8,128)(2,1)S(1)} %get-tuple-element.19), channel_id=1, source_target_pairs={{0,8},{1,12},{2,10},{3,14},{4,9},{5,13},{6,11},{7,15},{24,16},{25,... | collective-permute-start | bytes 3151880 | tf_op jit(solution)/shard_map/ppermute | solution.py:234
  20.7 1.6 %collective-permute-start.1 = (bf16[3,1368,128]{2,1,0:T(8,128)(2,1)S(1)}, bf16[3,1368,128]{2,1,0:T(8,128)(2,1)}, u32[]{:S(2)}, u32[]{:S(2)}) collective-permute-start(bf16[3,1368,128]{2,1,0:T(8,128)(2,1)S(1)} %get-tuple-element.18), channel_id=1, source_target_pairs={{8,16},{9,20},{10,18},{11,22},{12,17},{13,21},{14,19},{15,23},{16,... | collective-permute-start | bytes 3151880 | tf_op jit(solution)/shard_map/ppermute | solution.py:234
  23.2 1.2 pad_maximum_fusion.refs_0_
  24.4 1.6 %collective-permute-start.8 = (bf16[4,1024,128]{2,1,0:T(8,128)(2,1)S(1)}, bf16[4,1024,128]{2,1,0:T(8,128)(2,1)}, u32[]{:S(2)}, u32[]{:S(2)}) collective-permute-start(bf16[4,1024,128]{2,1,0:T(8,128)(2,1)S(1)} %pad_maximum_fusion.refs_0_), channel_id=1, source_target_pairs={{0,2},{1,3},{2,0},{3,1},{4,6},{5,7},{6,4},{7,5},{8,10},{9,11},{10,... | collective-permute-start | bytes 3145736 | tf_op jit(solution)/shard_map/ppermute | solution.py:234
  26.0 15.5 %collective-permute-done.refs_0_ = bf16[3,1368,128]{2,1,0:T(8,128)(2,1)} collective-permute-done((bf16[3,1368,128]{2,1,0:T(8,128)(2,1)S(1)}, bf16[3,1368,128]{2,1,0:T(8,128)(2,1)}, u32[]{:S(2)}, u32[]{:S(2)}) %collective-permute-start) | collective-permute-done | bytes 1050656 | tf_op jit(solution)/shard_map/ppermute | solution.py:234
  41.5 3.6 %collective-permute-start.2 = (bf16[3,1368,128]{2,1,0:T(8,128)(2,1)}, bf16[3,1368,128]{2,1,0:T(8,128)(2,1)}, u32[]{:S(2)}, u32[]{:S(2)}) collective-permute-start(bf16[3,1368,128]{2,1,0:T(8,128)(2,1)} %collective-permute-done.refs_0_), channel_id=1, source_target_pairs={{0,1},{1,0},{2,3},{3,2},{4,5},{5,4},{6,7},{7,6},{8,9},{9,8},{10,11... | collective-permute-start | bytes 3151880 | tf_op jit(solution)/shard_map/ppermute | solution.py:234
  45.6 2.5 %collective-permute-done.8.refs_1_ = bf16[4,1024,128]{2,1,0:T(8,128)(2,1)} collective-permute-done((bf16[4,1024,128]{2,1,0:T(8,128)(2,1)S(1)}, bf16[4,1024,128]{2,1,0:T(8,128)(2,1)}, u32[]{:S(2)}, u32[]{:S(2)}) %collective-permute-start.8) | collective-permute-done | bytes 1048608 | tf_op jit(solution)/shard_map/ppermute | solution.py:234
  48.1 2.4 %collective-permute-start.10 = (bf16[4,1024,128]{2,1,0:T(8,128)(2,1)}, bf16[4,1024,128]{2,1,0:T(8,128)(2,1)}, u32[]{:S(2)}, u32[]{:S(2)}) collective-permute-start(bf16[4,1024,128]{2,1,0:T(8,128)(2,1)} %collective-permute-done.8.refs_1_), channel_id=1, source_target_pairs={{0,1},{1,0},{2,3},{3,2},{4,5},{5,4},{6,7},{7,6},{8,9},{9,8},{10,11... | collective-permute-start | bytes 3145736 | tf_op jit(solution)/shard_map/ppermute | solution.py:234
  50.5 4.0 %collective-permute-start.11 = (bf16[3,1368,128]{2,1,0:T(8,128)(2,1)}, bf16[3,1368,128]{2,1,0:T(8,128)(2,1)S(1)}, u32[]{:S(2)}, u32[]{:S(2)}) collective-permute-start(bf16[3,1368,128]{2,1,0:T(8,128)(2,1)} %copy-done.4), channel_id=1, source_target_pairs={{0,16},{1,20},{2,18},{3,22},{4,17},{5,21},{6,19},{7,23},{24,8},{25... | collective-permute-start | bytes 3151880 | tf_op jit(solution)/shard_map/ppermute | solution.py:234
  55.5 7.0 %shard_map.78 = (f32[1368,1368]{1,0:T(8,128)S(1)}, bf16[1368,512]{1,0:T(8,128)(2,1)S(1)}) custom-call(bf16[3,1368,128]{2,1,0:T(8,128)(2,1)} %collective-permute-done.refs_0_, bf16[3,1368,128]{2,1,0:T(8,128)(2,1)} %collective-permute-done.1.refs_1_, bf16[3,1368,128]{2,1,0:T(8,128)(2,1)} %collective-permute-done.2.refs_2_, ...), custom_call_target="tpu_custom_call" | custom-call | flops 3832676352 | bytes 4202496 | tf_op jit(solution)/shard_map/pallas_call | solution.py:198
  62.5 12.1 %shard_map.79.poly = bf16[512,1024]{1,0:T(8,128)(2,1)S(1)} custom-call(s32[2]{0:T(128)S(1)} %pad_add_fusion.where, bf16[4,1024,128]{2,1,0:T(8,128)(2,1)S(1)} %pad_maximum_fusion.refs_0_, bf16[4,1024,128]{2,1,0:T(8,128)(2,1)} %collective-permute-done.8.refs_1_, bf16[4,1024,128]{2,1,0:T(8,128)(2,1)} %collective-permute-done.9.refs_2_, ...), custom_call_target="tpu_custom_call" | custom-call | flops 8589934592 | bytes 4194312 | tf_op jit(solution)/shard_map/pallas_call | solution.py:198
  74.7 1.4 %collective-permute-done.11.refs_0_ = bf16[3,1368,128]{2,1,0:T(8,128)(2,1)S(1)} collective-permute-done((bf16[3,1368,128]{2,1,0:T(8,128)(2,1)}, bf16[3,1368,128]{2,1,0:T(8,128)(2,1)S(1)}, u32[]{:S(2)}, u32[]{:S(2)}) %collective-permute-start.11) | collective-permute-done | bytes 1050656 | tf_op jit(solution)/shard_map/ppermute | solution.py:234
  76.6 2.2 %collective-permute-done.13.refs_2_ = bf16[3,1368,128]{2,1,0:T(8,128)(2,1)S(1)} collective-permute-done((bf16[3,1368,128]{2,1,0:T(8,128)(2,1)S(1)}, bf16[3,1368,128]{2,1,0:T(8,128)(2,1)S(1)}, u32[]{:S(2)}, u32[]{:S(2)}) %collective-permute-start.13) | collective-permute-done | bytes 1050656 | tf_op jit(solution)/shard_map/ppermute | solution.py:234
  78.7 1.5 %collective-permute-done.14.refs_3_ = bf16[3,1368,128]{2,1,0:T(8,128)(2,1)S(1)} collective-permute-done((bf16[3,1368,128]{2,1,0:T(8,128)(2,1)S(1)}, bf16[3,1368,128]{2,1,0:T(8,128)(2,1)S(1)}, u32[]{:S(2)}, u32[]{:S(2)}) %collective-permute-start.14) | collective-permute-done | bytes 1050656 | tf_op jit(solution)/shard_map/ppermute | solution.py:234
  80.2 14.0 %shard_map.80 = (bf16[1368,512]{1,0:T(8,128)(2,1)S(1)}, f32[8,128]{1,0:T(8,128)S(1)}) custom-call(f32[1368,1368]{1,0:T(8,128)S(1)} %get-tuple-element.15.base, bf16[512,1024]{1,0:T(8,128)(2,1)S(1)} %shard_map.79.poly, bf16[1368,512]{1,0:T(8,128)(2,1)S(1)} %get-tuple-element.17.taken, bf16[3,1368,128]{2,1,0:T(8,128)(2,1)S(1)} %collective-permute-done.11.refs_0_, ...), custom_call_target="tpu_custom_call" | custom-call | flops 11016142848 | bytes 14137600 | tf_op jit(solution)/shard_map/pallas_call | solution.py:198
  95.1 1.3 %collective-permute-start.17 = (bf16[1368,128]{1,0:T(8,128)(2,1)}, bf16[1368,128]{1,0:T(8,128)(2,1)S(1)}, u32[]{:S(2)}, u32[]{:S(2)}) collective-permute-start(bf16[1368,128]{1,0:T(8,128)(2,1)} %get-tuple-element.28), channel_id=1, source_target_pairs={{8,0},{12,1},{10,2},{14,3},{9,4},{13,5},{11,6},{15,7},{16,24},{20,... | collective-permute-start | bytes 1050632 | tf_op jit(solution)/shard_map/ppermute | solution.py:234
  97.1 1.3 %collective-permute-start.16 = (bf16[1368,128]{1,0:T(8,128)(2,1)S(1)}, bf16[1368,128]{1,0:T(8,128)(2,1)S(1)}, u32[]{:S(2)}, u32[]{:S(2)}) collective-permute-start(bf16[1368,128]{1,0:T(8,128)(2,1)S(1)} %get-tuple-element.30), channel_id=1, source_target_pairs={{16,0},{20,1},{18,2},{22,3},{17,4},{21,5},{19,6},{23,7},{8,24},{12... | collective-permute-start | bytes 1050632 | tf_op jit(solution)/shard_map/ppermute | solution.py:234
  99.2 22.1 %all_to_all.5 = f32[32,1,128]{2,1,0:T(1,128)S(1)} all-to-all(f32[32,1,128]{2,1,0:T(1,128)S(1)} %broadcast_in_dim.15), channel_id=1, replica_groups=mesh['shard'=8,'tensor'=4] {'shard','tensor'}, dimensions={0} | all-to-all | bytes 32768 | tf_op jit(solution)/shard_map/all_to_all | solution.py:348
  123.1 1.9 %fusion.1 = (f32[128,2736]{0,1:T(8,128)}, f32[128,2736]{0,1:T(8,128)}) fusion(f32[128,2736]{0,1:T(8,128)S(1)} %copy-done.5, f32[1368,128]{1,0:T(8,128)S(1)} %get-tuple-element.27, f32[1368,128]{1,0:T(8,128)S(1)} %get-tuple-element.26, f32[]{:T(128)} %bitcast.15, f32[128,2736]{0,1:T(8,128)S(1)} %copy-done.6), kind=kLoop, calls=%fused_computation.3 | loop fusion | flops 2101248 | bytes 7004164 | tf_op jit(solution)/shard_map/transpose | solution.py:359
  (49 shorter events, 10.6 us)
Async XLA Ops:
  0.6 1.2 copy-start
  2.2 18.4 %collective-permute-start.7 = (bf16[1024,128]{1,0:T(8,128)(2,1)S(1)}, bf16[1024,128]{1,0:T(8,128)(2,1)S(1)}, u32[]{:S(2)}, u32[]{:S(2)}) collective-permute-start(bf16[1024,128]{1,0:T(8,128)(2,1)S(1)} %convolution_convert_fusion), channel_id=1, source_target_pairs={{8,8},{9,12},{10,10},{11,14},{12,9},{13,13},{14,11},{15,15},{16,16... | collective-permute-start | bytes 786440 | tf_op jit(solution)/shard_map/ppermute | solution.py:234
  2.9 19.4 %collective-permute-start.6 = (bf16[1024,128]{1,0:T(8,128)(2,1)S(1)}, bf16[1024,128]{1,0:T(8,128)(2,1)S(1)}, u32[]{:S(2)}, u32[]{:S(2)}) collective-permute-start(bf16[1024,128]{1,0:T(8,128)(2,1)S(1)} %convolution_convert_fusion), channel_id=1, source_target_pairs={{0,16},{1,20},{2,18},{3,22},{4,17},{5,21},{6,19},{7,23},{24,8},{25... | collective-permute-start | bytes 786440 | tf_op jit(solution)/shard_map/ppermute | solution.py:234
  8.9 13.4 %collective-permute-start.5 = (bf16[1024,128]{1,0:T(8,128)(2,1)S(1)}, bf16[1024,128]{1,0:T(8,128)(2,1)S(1)}, u32[]{:S(2)}, u32[]{:S(2)}) collective-permute-start(bf16[1024,128]{1,0:T(8,128)(2,1)S(1)} %convolution_convert_fusion), channel_id=1, source_target_pairs={{8,16},{9,20},{10,18},{11,22},{12,17},{13,21},{14,19},{15,23},{16,... | collective-permute-start | bytes 786440 | tf_op jit(solution)/shard_map/ppermute | solution.py:234
  9.6 12.7 %collective-permute-start.4 = (bf16[1024,128]{1,0:T(8,128)(2,1)S(1)}, bf16[1024,128]{1,0:T(8,128)(2,1)S(1)}, u32[]{:S(2)}, u32[]{:S(2)}) collective-permute-start(bf16[1024,128]{1,0:T(8,128)(2,1)S(1)} %convolution_convert_fusion), channel_id=1, source_target_pairs={{0,8},{1,12},{2,10},{3,14},{4,9},{5,13},{6,11},{7,15},{24,16},{25,... | collective-permute-start | bytes 786440 | tf_op jit(solution)/shard_map/ppermute | solution.py:234
  12.7 1.8 %copy-start.1 = (bf16[2,256,2736]{1,2,0:T(8,128)(2,1)S(1)}, bf16[2,256,2736]{1,2,0:T(8,128)(2,1)}, u32[]{:S(2)}) copy-start(bf16[2,256,2736]{1,2,0:T(8,128)(2,1)} %param.6) | copy-start | bytes 8404996
  18.4 29.7 %copy-start.4 = (bf16[3,1368,128]{2,1,0:T(8,128)(2,1)}, bf16[3,1368,128]{2,1,0:T(8,128)(2,1)S(1)}, u32[]{:S(2)}) copy-start(bf16[3,1368,128]{2,1,0:T(8,128)(2,1)S(1)} %get-tuple-element.18) | copy-start | bytes 3151876
  18.4 23.1 %collective-permute-start = (bf16[3,1368,128]{2,1,0:T(8,128)(2,1)S(1)}, bf16[3,1368,128]{2,1,0:T(8,128)(2,1)}, u32[]{:S(2)}, u32[]{:S(2)}) collective-permute-start(bf16[3,1368,128]{2,1,0:T(8,128)(2,1)S(1)} %get-tuple-element.19), channel_id=1, source_target_pairs={{0,8},{1,12},{2,10},{3,14},{4,9},{5,13},{6,11},{7,15},{24,16},{25,... | collective-permute-start | bytes 3151880 | tf_op jit(solution)/shard_map/ppermute | solution.py:234
  20.7 24.4 %collective-permute-start.1 = (bf16[3,1368,128]{2,1,0:T(8,128)(2,1)S(1)}, bf16[3,1368,128]{2,1,0:T(8,128)(2,1)}, u32[]{:S(2)}, u32[]{:S(2)}) collective-permute-start(bf16[3,1368,128]{2,1,0:T(8,128)(2,1)S(1)} %get-tuple-element.18), channel_id=1, source_target_pairs={{8,16},{9,20},{10,18},{11,22},{12,17},{13,21},{14,19},{15,23},{16,... | collective-permute-start | bytes 3151880 | tf_op jit(solution)/shard_map/ppermute | solution.py:234
  24.4 23.6 %collective-permute-start.8 = (bf16[4,1024,128]{2,1,0:T(8,128)(2,1)S(1)}, bf16[4,1024,128]{2,1,0:T(8,128)(2,1)}, u32[]{:S(2)}, u32[]{:S(2)}) collective-permute-start(bf16[4,1024,128]{2,1,0:T(8,128)(2,1)S(1)} %pad_maximum_fusion.refs_0_), channel_id=1, source_target_pairs={{0,2},{1,3},{2,0},{3,1},{4,6},{5,7},{6,4},{7,5},{8,10},{9,11},{10,... | collective-permute-start | bytes 3145736 | tf_op jit(solution)/shard_map/ppermute | solution.py:234
  41.5 13.1 %collective-permute-start.2 = (bf16[3,1368,128]{2,1,0:T(8,128)(2,1)}, bf16[3,1368,128]{2,1,0:T(8,128)(2,1)}, u32[]{:S(2)}, u32[]{:S(2)}) collective-permute-start(bf16[3,1368,128]{2,1,0:T(8,128)(2,1)} %collective-permute-done.refs_0_), channel_id=1, source_target_pairs={{0,1},{1,0},{2,3},{3,2},{4,5},{5,4},{6,7},{7,6},{8,9},{9,8},{10,11... | collective-permute-start | bytes 3151880 | tf_op jit(solution)/shard_map/ppermute | solution.py:234
  45.1 10.4 %collective-permute-start.3 = (bf16[3,1368,128]{2,1,0:T(8,128)(2,1)}, bf16[3,1368,128]{2,1,0:T(8,128)(2,1)}, u32[]{:S(2)}, u32[]{:S(2)}) collective-permute-start(bf16[3,1368,128]{2,1,0:T(8,128)(2,1)} %collective-permute-done.1.refs_1_), channel_id=1, source_target_pairs={{0,1},{1,0},{2,3},{3,2},{4,5},{5,4},{6,7},{7,6},{8,9},{9,8},{10,11... | collective-permute-start | bytes 3151880 | tf_op jit(solution)/shard_map/ppermute | solution.py:234
  45.1 17.4 %collective-permute-start.9 = (bf16[4,1024,128]{2,1,0:T(8,128)(2,1)S(1)}, bf16[4,1024,128]{2,1,0:T(8,128)(2,1)}, u32[]{:S(2)}, u32[]{:S(2)}) collective-permute-start(bf16[4,1024,128]{2,1,0:T(8,128)(2,1)S(1)} %pad_maximum_fusion.refs_0_), channel_id=1, source_target_pairs={{0,1},{1,0},{2,3},{3,2},{4,5},{5,4},{6,7},{7,6},{8,9},{9,8},{10,11... | collective-permute-start | bytes 3145736 | tf_op jit(solution)/shard_map/ppermute | solution.py:234
  48.1 14.4 %collective-permute-start.10 = (bf16[4,1024,128]{2,1,0:T(8,128)(2,1)}, bf16[4,1024,128]{2,1,0:T(8,128)(2,1)}, u32[]{:S(2)}, u32[]{:S(2)}) collective-permute-start(bf16[4,1024,128]{2,1,0:T(8,128)(2,1)} %collective-permute-done.8.refs_1_), channel_id=1, source_target_pairs={{0,1},{1,0},{2,3},{3,2},{4,5},{5,4},{6,7},{7,6},{8,9},{9,8},{10,11... | collective-permute-start | bytes 3145736 | tf_op jit(solution)/shard_map/ppermute | solution.py:234
  50.5 25.5 %collective-permute-start.11 = (bf16[3,1368,128]{2,1,0:T(8,128)(2,1)}, bf16[3,1368,128]{2,1,0:T(8,128)(2,1)S(1)}, u32[]{:S(2)}, u32[]{:S(2)}) collective-permute-start(bf16[3,1368,128]{2,1,0:T(8,128)(2,1)} %copy-done.4), channel_id=1, source_target_pairs={{0,16},{1,20},{2,18},{3,22},{4,17},{5,21},{6,19},{7,23},{24,8},{25... | collective-permute-start | bytes 3151880 | tf_op jit(solution)/shard_map/ppermute | solution.py:234
  54.6 21.5 %collective-permute-start.12 = (bf16[3,1368,128]{2,1,0:T(8,128)(2,1)S(1)}, bf16[3,1368,128]{2,1,0:T(8,128)(2,1)S(1)}, u32[]{:S(2)}, u32[]{:S(2)}) collective-permute-start(bf16[3,1368,128]{2,1,0:T(8,128)(2,1)S(1)} %get-tuple-element.19), channel_id=1, source_target_pairs={{8,8},{9,12},{10,10},{11,14},{12,9},{13,13},{14,11},{15,15},{16,16... | collective-permute-start | bytes 3151880 | tf_op jit(solution)/shard_map/ppermute | solution.py:234
  76.0 2.7 %collective-permute-start.13 = (bf16[3,1368,128]{2,1,0:T(8,128)(2,1)S(1)}, bf16[3,1368,128]{2,1,0:T(8,128)(2,1)S(1)}, u32[]{:S(2)}, u32[]{:S(2)}) collective-permute-start(bf16[3,1368,128]{2,1,0:T(8,128)(2,1)S(1)} %collective-permute-done.11.refs_0_), channel_id=1, source_target_pairs={{0,1},{1,0},{2,3},{3,2},{4,5},{5,4},{6,7},{7,6},{8,9},{9,8},{10,11... | collective-permute-start | bytes 3151880 | tf_op jit(solution)/shard_map/ppermute | solution.py:234
  76.0 4.2 %collective-permute-start.14 = (bf16[3,1368,128]{2,1,0:T(8,128)(2,1)S(1)}, bf16[3,1368,128]{2,1,0:T(8,128)(2,1)S(1)}, u32[]{:S(2)}, u32[]{:S(2)}) collective-permute-start(bf16[3,1368,128]{2,1,0:T(8,128)(2,1)S(1)} %collective-permute-done.12.refs_1_), channel_id=1, source_target_pairs={{0,1},{1,0},{2,3},{3,2},{4,5},{5,4},{6,7},{7,6},{8,9},{9,8},{10,11... | collective-permute-start | bytes 3151880 | tf_op jit(solution)/shard_map/ppermute | solution.py:234
  95.1 26.2 %collective-permute-start.17 = (bf16[1368,128]{1,0:T(8,128)(2,1)}, bf16[1368,128]{1,0:T(8,128)(2,1)S(1)}, u32[]{:S(2)}, u32[]{:S(2)}) collective-permute-start(bf16[1368,128]{1,0:T(8,128)(2,1)} %get-tuple-element.28), channel_id=1, source_target_pairs={{8,0},{12,1},{10,2},{14,3},{9,4},{13,5},{11,6},{15,7},{16,24},{20,... | collective-permute-start | bytes 1050632 | tf_op jit(solution)/shard_map/ppermute | solution.py:234
  96.4 24.9 %collective-permute-start.18 = (bf16[1368,128]{1,0:T(8,128)(2,1)S(1)}, bf16[1368,128]{1,0:T(8,128)(2,1)S(1)}, u32[]{:S(2)}, u32[]{:S(2)}) collective-permute-start(bf16[1368,128]{1,0:T(8,128)(2,1)S(1)} %get-tuple-element.29), channel_id=1, source_target_pairs={{8,8},{12,9},{10,10},{14,11},{9,12},{13,13},{11,14},{15,15},{16,16... | collective-permute-start | bytes 1050632 | tf_op jit(solution)/shard_map/ppermute | solution.py:234
  97.1 24.3 %collective-permute-start.16 = (bf16[1368,128]{1,0:T(8,128)(2,1)S(1)}, bf16[1368,128]{1,0:T(8,128)(2,1)S(1)}, u32[]{:S(2)}, u32[]{:S(2)}) collective-permute-start(bf16[1368,128]{1,0:T(8,128)(2,1)S(1)} %get-tuple-element.30), channel_id=1, source_target_pairs={{16,0},{20,1},{18,2},{22,3},{17,4},{21,5},{19,6},{23,7},{8,24},{12... | collective-permute-start | bytes 1050632 | tf_op jit(solution)/shard_map/ppermute | solution.py:234
  98.4 23.0 %collective-permute-start.15 = (bf16[1368,128]{1,0:T(8,128)(2,1)S(1)}, bf16[1368,128]{1,0:T(8,128)(2,1)S(1)}, u32[]{:S(2)}, u32[]{:S(2)}) collective-permute-start(bf16[1368,128]{1,0:T(8,128)(2,1)S(1)} %get-tuple-element.31), channel_id=1, source_target_pairs={{16,8},{20,9},{18,10},{22,11},{17,12},{21,13},{19,14},{23,15},{8,1... | collective-permute-start | bytes 1050632 | tf_op jit(solution)/shard_map/ppermute | solution.py:234
  121.3 1.4 %copy-start.5 = (f32[128,2736]{0,1:T(8,128)S(1)}, f32[128,2736]{0,1:T(8,128)}, u32[]{:S(2)}) copy-start(f32[128,2736]{0,1:T(8,128)} %param.11) | copy-start | bytes 4202500
  121.3 1.8 %copy-start.6 = (f32[128,2736]{0,1:T(8,128)S(1)}, f32[128,2736]{0,1:T(8,128)}, u32[]{:S(2)}) copy-start(f32[128,2736]{0,1:T(8,128)} %param.10) | copy-start | bytes 4202500
  (5 other events, 4.1 us)

commit v5 on v4

--- a/solution.py
+++ b/solution.py
@@ -151,10 +151,11 @@
     poly[...] = dot_nt(total, hot).astype(jnp.bfloat16)
 
 
-def act_kernel(scale, samples, base, poly, taken, *refs):
-    *parts, update, inner, all_rows, left, wide, gram, first, second = refs
-    width = gram.shape[0]
-    half = update.shape[1]
+def act_kernel(scale, samples, update_rows, base, poly, taken, *refs):
+    *refs, inner, all_rows, left, wide, gram, first, second = refs
+    width, half = left.shape
+    outs = half // update_rows
+    parts, update = refs[:-outs], refs[-outs:]
     on_time = taken.shape[1] // 2
     for i in range(2):
         all_rows[:, i * half : i * half + on_time] = taken[:, i * on_time : (i + 1) * on_time]
@@ -187,7 +188,8 @@
         step = norm * dot_nn(gram[at : at + size, :], second[...])
         done = step + shift * first[at : at + size, :] + 4.0 * rows
         total = total + jnp.sum(done * all_rows[at : at + size, :half].astype(jnp.float32))
-        update[at : at + size, :] = done.astype(jnp.bfloat16)
+        for k, out in enumerate(update):
+            out[at : at + size, :] = done[:, k * update_rows : (k + 1) * update_rows].astype(jnp.bfloat16)
     inner[...] = jnp.full(inner.shape, total, jnp.float32)
 
 
@@ -288,7 +290,7 @@
     turn = lambda p, pair: send(pair[0] if outer_round(p) else pair[1], home(p))
     on_time = [turn(p, (outer, inside)) for p in early]
 
-    pair = after((outer, inside), on_time)
+    pair = after((outer, inside), [q_same])
     tardy = [turn(p, pair) for p in late]
     on_time_other = [over_core(x) for x in on_time]
     q_parts = [q_same] + q_far
@@ -324,9 +326,11 @@
 
     tardy = after(tardy, [poly, base] + tardy)
     tardy = tardy + [over_core(x) for x in tardy]
-    update, inner = call(
-        functools.partial(act_kernel, scale, batches),
-        (jax.ShapeDtypeStruct((ABLK, half), bf16), jax.ShapeDtypeStruct((8, 128), f32)),
+    piece = rows if rows % 128 == 0 else half
+    *update, inner = call(
+        functools.partial(act_kernel, scale, batches, piece),
+        (jax.ShapeDtypeStruct((ABLK, piece), bf16),) * (half // piece)
+        + (jax.ShapeDtypeStruct((8, 128), f32),),
         [
             ((ABLK, DOUT), bf16),
             ((ABLK, half), bf16),
@@ -341,7 +345,7 @@
     )
 
     back = [
-        send(update[:, a * rows : (a + 1) * rows], home(p), back=True)
+        send(update[a * rows // piece][:, a * rows % piece :][:, :rows], home(p), back=True)
         for p, a in sorted((p, a) for a, p in enumerate(early + late))
     ]
     mine = jnp.where(at_home, inner[:1], 0.0)

time: 126 us -> 122 us (0.968)
  blocking collectives: 22.1 us -> 19.7 us
  local copies, waits for them, and re-layouts: 8.17 us -> 6.17 us
    all_to_all x1, blocking collectives: 22.1 us -> 19.7 us  [per_device(): lax.all_to_all(jnp.broadcast_to(mine[None], (n * nt, 1, 128)), AXES, 0, 0)]
where the time goes in v5:
time: 122 us
  Pallas kernels  35.2 us (29%)
  starting transfers between devices  31.7 us (26%)
  waiting for transfers between devices  23 us (19%)
  blocking collectives  19.7 us (16%)
  local copies, waits for them, and re-layouts  6.17 us (5%)
  other arithmetic  4.5 us (4%)
    pallas_call x4, Pallas kernels, call(): pl.pallas_call(kernel, out_shape=out_shape, in_specs=[smem] * scalars + [...  35.2 us
    ppermute x19, starting transfers between devices, send(): return lax.ppermute(value, AXES, pairs)  31.7 us
    ppermute x19, waiting for transfers between devices, send(): return lax.ppermute(value, AXES, pairs)  23 us
    all_to_all x1, blocking collectives, per_device(): lax.all_to_all(jnp.broadcast_to(mine[None], (n * nt, 1, 128)), AXES, 0, 0)  19.7 us
    unnamed x20, local copies, waits for them, and re-layouts  5.39 us
  transfers between devices with their start and end apart: 19, of which 5 were waited for; matrix products, arithmetic and copies ran while one was open for 1% of the time, Pallas kernels for 17%

profile of v5, /device:TPU:0, one launch (start us, length us, event | category | flops | bytes accessed | tf_op | source)
XLA Modules:
  0.0 121.7 jit_solution(10493815344283208390)
XLA Ops:
  2.9 6.0 %collective-permute-start.6 = (bf16[1024,128]{1,0:T(8,128)(2,1)S(1)}, bf16[1024,128]{1,0:T(8,128)(2,1)S(1)}, u32[]{:S(2)}, u32[]{:S(2)}) collective-permute-start(bf16[1024,128]{1,0:T(8,128)(2,1)S(1)} %convolution_convert_fusion), channel_id=1, source_target_pairs={{0,16},{1,20},{2,18},{3,22},{4,17},{5,21},{6,19},{7,23},{24,8},{25... | collective-permute-start | bytes 786440 | tf_op jit(solution)/shard_map/ppermute | solution.py:236
  9.6 3.1 %collective-permute-start.4 = (bf16[1024,128]{1,0:T(8,128)(2,1)S(1)}, bf16[1024,128]{1,0:T(8,128)(2,1)S(1)}, u32[]{:S(2)}, u32[]{:S(2)}) collective-permute-start(bf16[1024,128]{1,0:T(8,128)(2,1)S(1)} %convolution_convert_fusion), channel_id=1, source_target_pairs={{0,8},{1,12},{2,10},{3,14},{4,9},{5,13},{6,11},{7,15},{24,16},{25,... | collective-permute-start | bytes 786440 | tf_op jit(solution)/shard_map/ppermute | solution.py:236
  12.7 1.8 %copy-done.1 = bf16[2,256,2736]{1,2,0:T(8,128)(2,1)S(1)} copy-done((bf16[2,256,2736]{1,2,0:T(8,128)(2,1)S(1)}, bf16[2,256,2736]{1,2,0:T(8,128)(2,1)}, u32[]{:S(2)}) %copy-start.1) | copy-done | bytes 2801688
  16.3 2.1 %shard_map.77 = (bf16[3,1368,128]{2,1,0:T(8,128)(2,1)S(1)}, bf16[3,1368,128]{2,1,0:T(8,128)(2,1)S(1)}) custom-call(s32[1]{0:T(128)} %bitcast.1.upper, s32[2,128]{1,0:T(2,128)S(1)} %copy-done.3, bf16[2,2736,256]{2,1,0:T(8,128)(2,1)S(1)} %bitcast.34, bf16[2736,128]{1,0:T(8,128)(2,1)S(1)} %bitcast.35), custom_call_target="tpu_custom_call" | custom-call | flops 358612992 | bytes 3503108 | tf_op jit(solution)/shard_map/pallas_call | solution.py:200
  18.4 2.3 %collective-permute-start = (bf16[3,1368,128]{2,1,0:T(8,128)(2,1)S(1)}, bf16[3,1368,128]{2,1,0:T(8,128)(2,1)}, u32[]{:S(2)}, u32[]{:S(2)}) collective-permute-start(bf16[3,1368,128]{2,1,0:T(8,128)(2,1)S(1)} %get-tuple-element.22), channel_id=1, source_target_pairs={{0,8},{1,12},{2,10},{3,14},{4,9},{5,13},{6,11},{7,15},{24,16},{25,... | collective-permute-start | bytes 3151880 | tf_op jit(solution)/shard_map/ppermute | solution.py:236
  20.7 1.6 %collective-permute-start.1 = (bf16[3,1368,128]{2,1,0:T(8,128)(2,1)S(1)}, bf16[3,1368,128]{2,1,0:T(8,128)(2,1)}, u32[]{:S(2)}, u32[]{:S(2)}) collective-permute-start(bf16[3,1368,128]{2,1,0:T(8,128)(2,1)S(1)} %get-tuple-element.21), channel_id=1, source_target_pairs={{8,16},{9,20},{10,18},{11,22},{12,17},{13,21},{14,19},{15,23},{16,... | collective-permute-start | bytes 3151880 | tf_op jit(solution)/shard_map/ppermute | solution.py:236
  23.2 1.2 %pad_maximum_fusion.refs_0_ = bf16[4,1024,128]{2,1,0:T(8,128)(2,1)S(1)} fusion(bf16[1,1024,128]{2,1,0:T(8,128)(2,1)S(1)} %bitcast.36, bf16[1,1024,128]{2,1,0:T(8,128)(2,1)} %bitcast.37, bf16[1,1024,128]{2,1,0:T(8,128)(2,1)} %bitcast.38, bf16[1,1024,128]{2,1,0:T(8,128)(2,1)} %bitcast.39), kind=kLoop, calls=%fused_computation.5 | loop fusion | flops 1572864 | bytes 2097152 | tf_op jit(solution)/shard_map/stack | solution.py:286
  24.5 1.6 %collective-permute-start.8 = (bf16[4,1024,128]{2,1,0:T(8,128)(2,1)S(1)}, bf16[4,1024,128]{2,1,0:T(8,128)(2,1)}, u32[]{:S(2)}, u32[]{:S(2)}) collective-permute-start(bf16[4,1024,128]{2,1,0:T(8,128)(2,1)S(1)} %pad_maximum_fusion.refs_0_), channel_id=1, source_target_pairs={{0,2},{1,3},{2,0},{3,1},{4,6},{5,7},{6,4},{7,5},{8,10},{9,11},{10,... | collective-permute-start | bytes 3145736 | tf_op jit(solution)/shard_map/ppermute | solution.py:236
  26.0 15.5 %collective-permute-done.refs_0_ = bf16[3,1368,128]{2,1,0:T(8,128)(2,1)} collective-permute-done((bf16[3,1368,128]{2,1,0:T(8,128)(2,1)S(1)}, bf16[3,1368,128]{2,1,0:T(8,128)(2,1)}, u32[]{:S(2)}, u32[]{:S(2)}) %collective-permute-start) | collective-permute-done | bytes 1050656 | tf_op jit(solution)/shard_map/ppermute | solution.py:236
  41.5 3.6 %collective-permute-start.2 = (bf16[3,1368,128]{2,1,0:T(8,128)(2,1)}, bf16[3,1368,128]{2,1,0:T(8,128)(2,1)}, u32[]{:S(2)}, u32[]{:S(2)}) collective-permute-start(bf16[3,1368,128]{2,1,0:T(8,128)(2,1)} %collective-permute-done.refs_0_), channel_id=1, source_target_pairs={{0,1},{1,0},{2,3},{3,2},{4,5},{5,4},{6,7},{7,6},{8,9},{9,8},{10,11... | collective-permute-start | bytes 3151880 | tf_op jit(solution)/shard_map/ppermute | solution.py:236
  45.6 2.5 %collective-permute-done.8.refs_1_ = bf16[4,1024,128]{2,1,0:T(8,128)(2,1)} collective-permute-done((bf16[4,1024,128]{2,1,0:T(8,128)(2,1)S(1)}, bf16[4,1024,128]{2,1,0:T(8,128)(2,1)}, u32[]{:S(2)}, u32[]{:S(2)}) %collective-permute-start.8) | collective-permute-done | bytes 1048608 | tf_op jit(solution)/shard_map/ppermute | solution.py:236
  48.1 2.4 %collective-permute-start.10 = (bf16[4,1024,128]{2,1,0:T(8,128)(2,1)}, bf16[4,1024,128]{2,1,0:T(8,128)(2,1)}, u32[]{:S(2)}, u32[]{:S(2)}) collective-permute-start(bf16[4,1024,128]{2,1,0:T(8,128)(2,1)} %collective-permute-done.8.refs_1_), channel_id=1, source_target_pairs={{0,1},{1,0},{2,3},{3,2},{4,5},{5,4},{6,7},{7,6},{8,9},{9,8},{10,11... | collective-permute-start | bytes 3145736 | tf_op jit(solution)/shard_map/ppermute | solution.py:236
  50.6 4.0 %collective-permute-start.11 = (bf16[3,1368,128]{2,1,0:T(8,128)(2,1)}, bf16[3,1368,128]{2,1,0:T(8,128)(2,1)S(1)}, u32[]{:S(2)}, u32[]{:S(2)}) collective-permute-start(bf16[3,1368,128]{2,1,0:T(8,128)(2,1)} %copy-done.4), channel_id=1, source_target_pairs={{0,16},{1,20},{2,18},{3,22},{4,17},{5,21},{6,19},{7,23},{24,8},{25... | collective-permute-start | bytes 3151880 | tf_op jit(solution)/shard_map/ppermute | solution.py:236
  55.5 7.0 %shard_map.78 = (f32[1368,1368]{1,0:T(8,128)S(1)}, bf16[1368,512]{1,0:T(8,128)(2,1)S(1)}) custom-call(bf16[3,1368,128]{2,1,0:T(8,128)(2,1)} %collective-permute-done.refs_0_, bf16[3,1368,128]{2,1,0:T(8,128)(2,1)} %collective-permute-done.1.refs_1_, bf16[3,1368,128]{2,1,0:T(8,128)(2,1)} %collective-permute-done.2.refs_2_, ...), custom_call_target="tpu_custom_call" | custom-call | flops 3832676352 | bytes 4202496 | tf_op jit(solution)/shard_map/pallas_call | solution.py:200
  62.6 12.1 %shard_map.79.poly = bf16[512,1024]{1,0:T(8,128)(2,1)S(1)} custom-call(s32[2]{0:T(128)S(1)} %pad_add_fusion.where, bf16[4,1024,128]{2,1,0:T(8,128)(2,1)S(1)} %pad_maximum_fusion.refs_0_, bf16[4,1024,128]{2,1,0:T(8,128)(2,1)} %collective-permute-done.8.refs_1_, bf16[4,1024,128]{2,1,0:T(8,128)(2,1)} %collective-permute-done.9.refs_2_, ...), custom_call_target="tpu_custom_call" | custom-call | flops 8589934592 | bytes 4194312 | tf_op jit(solution)/shard_map/pallas_call | solution.py:200
  74.6 1.4 %collective-permute-done.11.refs_0_ = bf16[3,1368,128]{2,1,0:T(8,128)(2,1)S(1)} collective-permute-done((bf16[3,1368,128]{2,1,0:T(8,128)(2,1)}, bf16[3,1368,128]{2,1,0:T(8,128)(2,1)S(1)}, u32[]{:S(2)}, u32[]{:S(2)}) %collective-permute-start.11) | collective-permute-done | bytes 1050656 | tf_op jit(solution)/shard_map/ppermute | solution.py:236
  76.6 2.2 %collective-permute-done.13.refs_2_ = bf16[3,1368,128]{2,1,0:T(8,128)(2,1)S(1)} collective-permute-done((bf16[3,1368,128]{2,1,0:T(8,128)(2,1)S(1)}, bf16[3,1368,128]{2,1,0:T(8,128)(2,1)S(1)}, u32[]{:S(2)}, u32[]{:S(2)}) %collective-permute-start.13) | collective-permute-done | bytes 1050656 | tf_op jit(solution)/shard_map/ppermute | solution.py:236
  78.7 1.5 %collective-permute-done.14.refs_3_ = bf16[3,1368,128]{2,1,0:T(8,128)(2,1)S(1)} collective-permute-done((bf16[3,1368,128]{2,1,0:T(8,128)(2,1)S(1)}, bf16[3,1368,128]{2,1,0:T(8,128)(2,1)S(1)}, u32[]{:S(2)}, u32[]{:S(2)}) %collective-permute-start.14) | collective-permute-done | bytes 1050656 | tf_op jit(solution)/shard_map/ppermute | solution.py:236
  80.2 14.0 %shard_map.80 = (bf16[1368,128]{1,0:T(8,128)(2,1)S(1)}, bf16[1368,128]{1,0:T(8,128)(2,1)S(1)}, bf16[1368,128]{1,0:T(8,128)(2,1)S(1)}, bf16[1368,128]{1,0:T(8,128)(2,1)S(1)}, f32[8,128]{1,0:T(8,128)S(1)}) custom-call(f32[1368,1368]{1,0:T(8,128)S(1)} %get-tuple-element.18.base, bf16[512,1024]{1,0:T(8,128)(2,1)S(1)} %shard_map.79.poly, ...), custom_call_target="tpu_custom_call" | custom-call | flops 11016142848 | bytes 14137600 | tf_op jit(solution)/shard_map/pallas_call | solution.py:200
  94.2 1.3 %collective-permute-start.16 = (bf16[1368,128]{1,0:T(8,128)(2,1)S(1)}, bf16[1368,128]{1,0:T(8,128)(2,1)S(1)}, u32[]{:S(2)}, u32[]{:S(2)}) collective-permute-start(bf16[1368,128]{1,0:T(8,128)(2,1)S(1)} %get-tuple-element.27), channel_id=1, source_target_pairs={{16,0},{20,1},{18,2},{22,3},{17,4},{21,5},{19,6},{23,7},{8,24},{12... | collective-permute-start | bytes 1050632 | tf_op jit(solution)/shard_map/ppermute | solution.py:236
  96.9 1.3 %collective-permute-start.17 = (bf16[1368,128]{1,0:T(8,128)(2,1)S(1)}, bf16[1368,128]{1,0:T(8,128)(2,1)}, u32[]{:S(2)}, u32[]{:S(2)}) collective-permute-start(bf16[1368,128]{1,0:T(8,128)(2,1)S(1)} %get-tuple-element.28), channel_id=1, source_target_pairs={{8,0},{12,1},{10,2},{14,3},{9,4},{13,5},{11,6},{15,7},{16,24},{20,... | collective-permute-start | bytes 1050632 | tf_op jit(solution)/shard_map/ppermute | solution.py:236
  98.2 19.7 %all_to_all.5 = f32[32,1,128]{2,1,0:T(1,128)S(1)} all-to-all(f32[32,1,128]{2,1,0:T(1,128)S(1)} %broadcast_in_dim.15), channel_id=1, replica_groups=mesh['shard'=8,'tensor'=4] {'shard','tensor'}, dimensions={0} | all-to-all | bytes 32768 | tf_op jit(solution)/shard_map/all_to_all | solution.py:352
  118.1 1.3 %fusion.3 = (f32[1368,128]{1,0:T(8,128)S(1)}, f32[1368,128]{1,0:T(8,128)S(1)}) fusion(bf16[1368,128]{1,0:T(8,128)(2,1)S(1)} %collective-permute-done.16, bf16[1368,128]{1,0:T(8,128)(2,1)S(1)} %collective-permute-done.15, bf16[1368,128]{1,0:T(8,128)(2,1)S(1)} %collective-permute-done.18, bf16[1368,128]{1,0:T(8,128)(2,1)} %collective-permute-done.17, pred[]{:T(512)S(6)} %ge.3), kind=kLoop, calls=%fused_computation.9 | loop fusion | flops 1400832 | bytes 2801665 | tf_op jit(solution)/shard_map/jit(_where)/select_n | solution.py:359
  119.9 1.8 %fusion.1 = (f32[128,2736]{0,1:T(8,128)}, f32[128,2736]{0,1:T(8,128)}) fusion(f32[128,2736]{0,1:T(8,128)S(1)} %copy-done.5, f32[1368,128]{1,0:T(8,128)S(1)} %get-tuple-element.33, f32[1368,128]{1,0:T(8,128)S(1)} %get-tuple-element.32, f32[]{:T(128)} %bitcast.15, f32[128,2736]{0,1:T(8,128)S(1)} %copy-done.6), kind=kLoop, calls=%fused_computation.3 | loop fusion | flops 2101248 | bytes 7004164 | tf_op jit(solution)/shard_map/transpose | solution.py:363
  (48 shorter events, 9.5 us)
Async XLA Ops:
  0.6 1.2 %copy-start = (bf16[2,256,1024]{2,1,0:T(8,128)(2,1)S(1)}, bf16[2,256,1024]{2,1,0:T(8,128)(2,1)}, u32[]{:S(2)}) copy-start(bf16[2,256,1024]{2,1,0:T(8,128)(2,1)} %param.7) | copy-start | bytes 3145732
  2.2 18.4 %collective-permute-start.7 = (bf16[1024,128]{1,0:T(8,128)(2,1)S(1)}, bf16[1024,128]{1,0:T(8,128)(2,1)S(1)}, u32[]{:S(2)}, u32[]{:S(2)}) collective-permute-start(bf16[1024,128]{1,0:T(8,128)(2,1)S(1)} %convolution_convert_fusion), channel_id=1, source_target_pairs={{8,8},{9,12},{10,10},{11,14},{12,9},{13,13},{14,11},{15,15},{16,16... | collective-permute-start | bytes 786440 | tf_op jit(solution)/shard_map/ppermute | solution.py:236
  2.9 19.4 %collective-permute-start.6 = (bf16[1024,128]{1,0:T(8,128)(2,1)S(1)}, bf16[1024,128]{1,0:T(8,128)(2,1)S(1)}, u32[]{:S(2)}, u32[]{:S(2)}) collective-permute-start(bf16[1024,128]{1,0:T(8,128)(2,1)S(1)} %convolution_convert_fusion), channel_id=1, source_target_pairs={{0,16},{1,20},{2,18},{3,22},{4,17},{5,21},{6,19},{7,23},{24,8},{25... | collective-permute-start | bytes 786440 | tf_op jit(solution)/shard_map/ppermute | solution.py:236
  8.9 13.4 %collective-permute-start.5 = (bf16[1024,128]{1,0:T(8,128)(2,1)S(1)}, bf16[1024,128]{1,0:T(8,128)(2,1)S(1)}, u32[]{:S(2)}, u32[]{:S(2)}) collective-permute-start(bf16[1024,128]{1,0:T(8,128)(2,1)S(1)} %convolution_convert_fusion), channel_id=1, source_target_pairs={{8,16},{9,20},{10,18},{11,22},{12,17},{13,21},{14,19},{15,23},{16,... | collective-permute-start | bytes 786440 | tf_op jit(solution)/shard_map/ppermute | solution.py:236
  9.6 12.8 %collective-permute-start.4 = (bf16[1024,128]{1,0:T(8,128)(2,1)S(1)}, bf16[1024,128]{1,0:T(8,128)(2,1)S(1)}, u32[]{:S(2)}, u32[]{:S(2)}) collective-permute-start(bf16[1024,128]{1,0:T(8,128)(2,1)S(1)} %convolution_convert_fusion), channel_id=1, source_target_pairs={{0,8},{1,12},{2,10},{3,14},{4,9},{5,13},{6,11},{7,15},{24,16},{25,... | collective-permute-start | bytes 786440 | tf_op jit(solution)/shard_map/ppermute | solution.py:236
  12.7 1.8 %copy-start.1 = (bf16[2,256,2736]{1,2,0:T(8,128)(2,1)S(1)}, bf16[2,256,2736]{1,2,0:T(8,128)(2,1)}, u32[]{:S(2)}) copy-start(bf16[2,256,2736]{1,2,0:T(8,128)(2,1)} %param.6) | copy-start | bytes 8404996
  18.4 29.7 %copy-start.4 = (bf16[3,1368,128]{2,1,0:T(8,128)(2,1)}, bf16[3,1368,128]{2,1,0:T(8,128)(2,1)S(1)}, u32[]{:S(2)}) copy-start(bf16[3,1368,128]{2,1,0:T(8,128)(2,1)S(1)} %get-tuple-element.21) | copy-start | bytes 3151876
  18.4 23.1 %collective-permute-start = (bf16[3,1368,128]{2,1,0:T(8,128)(2,1)S(1)}, bf16[3,1368,128]{2,1,0:T(8,128)(2,1)}, u32[]{:S(2)}, u32[]{:S(2)}) collective-permute-start(bf16[3,1368,128]{2,1,0:T(8,128)(2,1)S(1)} %get-tuple-element.22), channel_id=1, source_target_pairs={{0,8},{1,12},{2,10},{3,14},{4,9},{5,13},{6,11},{7,15},{24,16},{25,... | collective-permute-start | bytes 3151880 | tf_op jit(solution)/shard_map/ppermute | solution.py:236
  20.7 24.4 %collective-permute-start.1 = (bf16[3,1368,128]{2,1,0:T(8,128)(2,1)S(1)}, bf16[3,1368,128]{2,1,0:T(8,128)(2,1)}, u32[]{:S(2)}, u32[]{:S(2)}) collective-permute-start(bf16[3,1368,128]{2,1,0:T(8,128)(2,1)S(1)} %get-tuple-element.21), channel_id=1, source_target_pairs={{8,16},{9,20},{10,18},{11,22},{12,17},{13,21},{14,19},{15,23},{16,... | collective-permute-start | bytes 3151880 | tf_op jit(solution)/shard_map/ppermute | solution.py:236
  24.5 23.6 %collective-permute-start.8 = (bf16[4,1024,128]{2,1,0:T(8,128)(2,1)S(1)}, bf16[4,1024,128]{2,1,0:T(8,128)(2,1)}, u32[]{:S(2)}, u32[]{:S(2)}) collective-permute-start(bf16[4,1024,128]{2,1,0:T(8,128)(2,1)S(1)} %pad_maximum_fusion.refs_0_), channel_id=1, source_target_pairs={{0,2},{1,3},{2,0},{3,1},{4,6},{5,7},{6,4},{7,5},{8,10},{9,11},{10,... | collective-permute-start | bytes 3145736 | tf_op jit(solution)/shard_map/ppermute | solution.py:236
  41.5 13.1 %collective-permute-start.2 = (bf16[3,1368,128]{2,1,0:T(8,128)(2,1)}, bf16[3,1368,128]{2,1,0:T(8,128)(2,1)}, u32[]{:S(2)}, u32[]{:S(2)}) collective-permute-start(bf16[3,1368,128]{2,1,0:T(8,128)(2,1)} %collective-permute-done.refs_0_), channel_id=1, source_target_pairs={{0,1},{1,0},{2,3},{3,2},{4,5},{5,4},{6,7},{7,6},{8,9},{9,8},{10,11... | collective-permute-start | bytes 3151880 | tf_op jit(solution)/shard_map/ppermute | solution.py:236
  45.1 10.4 %collective-permute-start.3 = (bf16[3,1368,128]{2,1,0:T(8,128)(2,1)}, bf16[3,1368,128]{2,1,0:T(8,128)(2,1)}, u32[]{:S(2)}, u32[]{:S(2)}) collective-permute-start(bf16[3,1368,128]{2,1,0:T(8,128)(2,1)} %collective-permute-done.1.refs_1_), channel_id=1, source_target_pairs={{0,1},{1,0},{2,3},{3,2},{4,5},{5,4},{6,7},{7,6},{8,9},{9,8},{10,11... | collective-permute-start | bytes 3151880 | tf_op jit(solution)/shard_map/ppermute | solution.py:236
  45.1 17.4 %collective-permute-start.9 = (bf16[4,1024,128]{2,1,0:T(8,128)(2,1)S(1)}, bf16[4,1024,128]{2,1,0:T(8,128)(2,1)}, u32[]{:S(2)}, u32[]{:S(2)}) collective-permute-start(bf16[4,1024,128]{2,1,0:T(8,128)(2,1)S(1)} %pad_maximum_fusion.refs_0_), channel_id=1, source_target_pairs={{0,1},{1,0},{2,3},{3,2},{4,5},{5,4},{6,7},{7,6},{8,9},{9,8},{10,11... | collective-permute-start | bytes 3145736 | tf_op jit(solution)/shard_map/ppermute | solution.py:236
  48.1 14.4 %collective-permute-start.10 = (bf16[4,1024,128]{2,1,0:T(8,128)(2,1)}, bf16[4,1024,128]{2,1,0:T(8,128)(2,1)}, u32[]{:S(2)}, u32[]{:S(2)}) collective-permute-start(bf16[4,1024,128]{2,1,0:T(8,128)(2,1)} %collective-permute-done.8.refs_1_), channel_id=1, source_target_pairs={{0,1},{1,0},{2,3},{3,2},{4,5},{5,4},{6,7},{7,6},{8,9},{9,8},{10,11... | collective-permute-start | bytes 3145736 | tf_op jit(solution)/shard_map/ppermute | solution.py:236
  50.6 25.5 %collective-permute-start.11 = (bf16[3,1368,128]{2,1,0:T(8,128)(2,1)}, bf16[3,1368,128]{2,1,0:T(8,128)(2,1)S(1)}, u32[]{:S(2)}, u32[]{:S(2)}) collective-permute-start(bf16[3,1368,128]{2,1,0:T(8,128)(2,1)} %copy-done.4), channel_id=1, source_target_pairs={{0,16},{1,20},{2,18},{3,22},{4,17},{5,21},{6,19},{7,23},{24,8},{25... | collective-permute-start | bytes 3151880 | tf_op jit(solution)/shard_map/ppermute | solution.py:236
  54.6 21.5 %collective-permute-start.12 = (bf16[3,1368,128]{2,1,0:T(8,128)(2,1)S(1)}, bf16[3,1368,128]{2,1,0:T(8,128)(2,1)S(1)}, u32[]{:S(2)}, u32[]{:S(2)}) collective-permute-start(bf16[3,1368,128]{2,1,0:T(8,128)(2,1)S(1)} %get-tuple-element.22), channel_id=1, source_target_pairs={{8,8},{9,12},{10,10},{11,14},{12,9},{13,13},{14,11},{15,15},{16,16... | collective-permute-start | bytes 3151880 | tf_op jit(solution)/shard_map/ppermute | solution.py:236
  76.0 2.7 %collective-permute-start.13 = (bf16[3,1368,128]{2,1,0:T(8,128)(2,1)S(1)}, bf16[3,1368,128]{2,1,0:T(8,128)(2,1)S(1)}, u32[]{:S(2)}, u32[]{:S(2)}) collective-permute-start(bf16[3,1368,128]{2,1,0:T(8,128)(2,1)S(1)} %collective-permute-done.11.refs_0_), channel_id=1, source_target_pairs={{0,1},{1,0},{2,3},{3,2},{4,5},{5,4},{6,7},{7,6},{8,9},{9,8},{10,11... | collective-permute-start | bytes 3151880 | tf_op jit(solution)/shard_map/ppermute | solution.py:236
  76.0 4.2 %collective-permute-start.14 = (bf16[3,1368,128]{2,1,0:T(8,128)(2,1)S(1)}, bf16[3,1368,128]{2,1,0:T(8,128)(2,1)S(1)}, u32[]{:S(2)}, u32[]{:S(2)}) collective-permute-start(bf16[3,1368,128]{2,1,0:T(8,128)(2,1)S(1)} %collective-permute-done.12.refs_1_), channel_id=1, source_target_pairs={{0,1},{1,0},{2,3},{3,2},{4,5},{5,4},{6,7},{7,6},{8,9},{9,8},{10,11... | collective-permute-start | bytes 3151880 | tf_op jit(solution)/shard_map/ppermute | solution.py:236
  94.2 23.8 %collective-permute-start.16 = (bf16[1368,128]{1,0:T(8,128)(2,1)S(1)}, bf16[1368,128]{1,0:T(8,128)(2,1)S(1)}, u32[]{:S(2)}, u32[]{:S(2)}) collective-permute-start(bf16[1368,128]{1,0:T(8,128)(2,1)S(1)} %get-tuple-element.27), channel_id=1, source_target_pairs={{16,0},{20,1},{18,2},{22,3},{17,4},{21,5},{19,6},{23,7},{8,24},{12... | collective-permute-start | bytes 1050632 | tf_op jit(solution)/shard_map/ppermute | solution.py:236
  95.5 22.6 %collective-permute-start.15 = (bf16[1368,128]{1,0:T(8,128)(2,1)S(1)}, bf16[1368,128]{1,0:T(8,128)(2,1)S(1)}, u32[]{:S(2)}, u32[]{:S(2)}) collective-permute-start(bf16[1368,128]{1,0:T(8,128)(2,1)S(1)} %get-tuple-element.26), channel_id=1, source_target_pairs={{16,8},{20,9},{18,10},{22,11},{17,12},{21,13},{19,14},{23,15},{8,1... | collective-permute-start | bytes 1050632 | tf_op jit(solution)/shard_map/ppermute | solution.py:236
  96.2 21.9 %collective-permute-start.18 = (bf16[1368,128]{1,0:T(8,128)(2,1)S(1)}, bf16[1368,128]{1,0:T(8,128)(2,1)S(1)}, u32[]{:S(2)}, u32[]{:S(2)}) collective-permute-start(bf16[1368,128]{1,0:T(8,128)(2,1)S(1)} %get-tuple-element.29), channel_id=1, source_target_pairs={{8,8},{12,9},{10,10},{14,11},{9,12},{13,13},{11,14},{15,15},{16,16... | collective-permute-start | bytes 1050632 | tf_op jit(solution)/shard_map/ppermute | solution.py:236
  96.9 21.2 %collective-permute-start.17 = (bf16[1368,128]{1,0:T(8,128)(2,1)S(1)}, bf16[1368,128]{1,0:T(8,128)(2,1)}, u32[]{:S(2)}, u32[]{:S(2)}) collective-permute-start(bf16[1368,128]{1,0:T(8,128)(2,1)S(1)} %get-tuple-element.28), channel_id=1, source_target_pairs={{8,0},{12,1},{10,2},{14,3},{9,4},{13,5},{11,6},{15,7},{16,24},{20,... | collective-permute-start | bytes 1050632 | tf_op jit(solution)/shard_map/ppermute | solution.py:236
  118.0 1.5 %copy-start.5 = (f32[128,2736]{0,1:T(8,128)S(1)}, f32[128,2736]{0,1:T(8,128)}, u32[]{:S(2)}) copy-start(f32[128,2736]{0,1:T(8,128)} %param.11) | copy-start | bytes 4202500
  118.0 1.9 %copy-start.6 = (f32[128,2736]{0,1:T(8,128)S(1)}, f32[128,2736]{0,1:T(8,128)}, u32[]{:S(2)}) copy-start(f32[128,2736]{0,1:T(8,128)} %param.10) | copy-start | bytes 4202500
  (5 other events, 4.2 us)

commit v6 on v5

--- a/solution.py
+++ b/solution.py
@@ -78,6 +78,13 @@
     lay_out(parts, wide, range(samples))
     for at, size in row_tiles(gram.shape[0], 352):
         gram[at : at + size, :] = dot_nt(wide[at : at + size, :], wide[...])
+
+
+def more_gram_kernel(samples, base, *refs):
+    *parts, gram, wide = refs
+    lay_out(parts, wide, range(samples))
+    for at, size in row_tiles(gram.shape[0], 352):
+        gram[at : at + size, :] = base[at : at + size, :] + dot_nt(wide[at : at + size, :], wide[...])
 
 
 def factor_gram(wide, base, gram, scale):
@@ -123,7 +130,7 @@
 
 
 def grad_kernel(scale, rows, high, m, where, *refs):
-    *q_parts, poly, wide, gram = refs
+    *q_parts, taken, poly, left, wide, gram = refs
     width = gram.shape[0]
     half = poly.shape[0]
     lay_out(q_parts, wide)
@@ -149,9 +156,16 @@
     y3 = norm * dot_nn(y2_low, gram[...]) + shift * y2
     total = (4.0 * y2 - 6.0 * y1 - y3).astype(jnp.bfloat16)
     poly[...] = dot_nt(total, hot).astype(jnp.bfloat16)
-
-
-def act_kernel(scale, samples, update_rows, base, poly, taken, *refs):
+    on_time = taken.shape[1] // 2
+    for at, size in row_tiles(left.shape[0], 352):
+        own = taken[at : at + size, :on_time]
+        mixed = dot_nt(own, poly[:, :on_time])
+        mixed = mixed + dot_nt(taken[at : at + size, on_time:], poly[:, half : half + on_time])
+        left[at : at + size, :on_time] = mixed[:, :on_time] + 4.0 * own.astype(jnp.float32)
+        left[at : at + size, on_time:] = mixed[:, on_time:]
+
+
+def act_kernel(scale, samples, update_rows, base, poly, early, taken, *refs):
     *refs, inner, all_rows, left, wide, gram, first, second = refs
     width, half = left.shape
     outs = half // update_rows
@@ -166,10 +180,13 @@
             all_rows[:, at : at + rows] = part[samples][:, :rows]
     tiles = row_tiles(width, 352)
     for at, size in tiles:
-        mixed = dot_nt(all_rows[at : at + size, :], poly[...])
-        mixed = mixed + 4.0 * all_rows[at : at + size, :half].astype(jnp.float32)
-        left[at : at + size, :] = mixed.astype(jnp.bfloat16)
-    lay_out(parts, wide, range(samples))
+        own = all_rows[at : at + size, on_time:half]
+        mixed = early[at : at + size, :] + dot_nt(own, poly[:, on_time:half])
+        mixed = mixed + dot_nt(all_rows[at : at + size, half + on_time :], poly[:, half + on_time :])
+        left[at : at + size, :on_time] = mixed[:, :on_time].astype(jnp.bfloat16)
+        mixed = mixed[:, on_time:] + 4.0 * own.astype(jnp.float32)
+        left[at : at + size, on_time:] = mixed.astype(jnp.bfloat16)
+    lay_out(parts[::2], wide, range(samples))
     trace, squares = factor_gram(wide, base, gram, scale)
     norm, shift = damping_terms(trace, squares, width)
     for at, size in tiles:
@@ -300,15 +317,6 @@
     scale = 1.0 / count
     half = rounds * rows
     where = jnp.stack([mine_j & 1, core]).astype(jnp.int32)
-    poly = call(
-        functools.partial(grad_kernel, scale, rows, high, m),
-        jax.ShapeDtypeStruct((half, DOUT), bf16),
-        [((DOUT, count), bf16), ((DOUT, DOUT), bf16)],
-        [where, *q_parts],
-        2 * DOUT * (DOUT * count + 4 * half * DOUT),
-        vmem_mib=28 if n == 8 else 46,
-        scalars=1,
-    )
     share = len(early) / rounds
     base, taken = call(
         functools.partial(gram_kernel, batches),
@@ -323,9 +331,31 @@
     )
     if rows < picks:
         taken = taken.reshape(ABLK, -1, picks)[:, :, :rows].reshape(ABLK, -1)
-
-    tardy = after(tardy, [poly, base] + tardy)
-    tardy = tardy + [over_core(x) for x in tardy]
+    poly, left_early = call(
+        functools.partial(grad_kernel, scale, rows, high, m),
+        (jax.ShapeDtypeStruct((half, DOUT), bf16), jax.ShapeDtypeStruct((ABLK, half), f32)),
+        [((DOUT, count), bf16), ((DOUT, DOUT), bf16)],
+        [where, *q_parts, taken],
+        2 * DOUT * (DOUT * count + 4 * half * DOUT + ABLK * half // 2),
+        vmem_mib=28 if n == 8 else 58,
+        scalars=1,
+    )
+
+    local = [after(x, poly) for x, p in zip(tardy, late) if p % high == 3]
+    local = [(x, over_core(x)) for x in local]
+    last = [x for x, p in zip(tardy, late) if p % high == 2]
+    last = after(last, [poly, base] + last)
+    base = after(base, last)
+    last = [(x, over_core(x)) for x in last]
+    base = call(
+        functools.partial(more_gram_kernel, batches),
+        jax.ShapeDtypeStruct((ABLK, ABLK), f32),
+        [((ABLK, count // 4), bf16)],
+        [base] + [x for x, _ in local] + [x for _, x in local],
+        2 * ABLK * ABLK * count // 4,
+        vmem_mib=12 if n == 8 else 30,
+    )
+    tardy = [pair[i] for i in range(2) for both in zip(last, local) for pair in both]
     piece = rows if rows % 128 == 0 else half
     *update, inner = call(
         functools.partial(act_kernel, scale, batches, piece),
@@ -334,13 +364,13 @@
         [
             ((ABLK, DOUT), bf16),
             ((ABLK, half), bf16),
-            ((ABLK, count - int(count * share)), bf16),
+            ((ABLK, count // 4), bf16),
             ((ABLK, ABLK), bf16),
             ((ABLK, half), f32),
             ((ABLK, half), bf16),
         ],
-        [base, poly, taken] + tardy,
-        int(2 * ABLK * (ABLK * (count * (1 - share) + 3 * half) + half * DOUT)),
+        [base, poly, left_early, taken] + tardy,
+        int(2 * ABLK * (ABLK * (count // 4 + 3 * half) + half * DOUT // 2)),
         vmem_mib=28 if n == 8 else 46,
     )
 
@@ -353,8 +383,8 @@
     total = jnp.sum(heard, axis=0)
     ratio = jnp.minimum(1.0, CLIP_LEVEL / jnp.sqrt(total[0, 0] / (DOUT * FF)))
 
-    got_outer = sum(x.astype(f32) for p, x in enumerate(back) if outer_round(p))
-    got_inside = sum(x.astype(f32) for p, x in enumerate(back) if not outer_round(p))
+    got_outer = sum(x.astype(f32) for p, x in reversed(list(enumerate(back))) if outer_round(p))
+    got_inside = sum(x.astype(f32) for p, x in reversed(list(enumerate(back))) if not outer_round(p))
     final = jnp.concatenate(
         [jnp.where(upper, got_inside, got_outer), jnp.where(upper, got_outer, got_inside)], axis=0
     )

time: 122 us -> 121 us (level)
  waiting for transfers between devices: 23 us -> 19 us
  starting transfers between devices: 31.7 us -> 34.6 us
    ppermute x19, waiting for transfers between devices: 23 us -> 19 us  [send(): return lax.ppermute(value, AXES, pairs)]
    ppermute x19, starting transfers between devices: 31.7 us -> 34.6 us  [send(): return lax.ppermute(value, AXES, pairs)]
    pallas_call x4 -> x5, Pallas kernels: 35.2 us -> 35.9 us  [call(): pl.pallas_call(kernel, out_shape=out_shape, in_specs=[smem] * scalars + [...]
  transfers between devices with their start and end apart: 19 -> 19, of which waited for: 5 -> 4; matrix products, arithmetic and copies ran while one was open for 1% -> 1% of each run, Pallas kernels for 17% -> 20%
where the time goes in v6:
time: 121 us; the launch traced here: 120 us
  Pallas kernels  35.9 us (30%)
  starting transfers between devices  34.6 us (29%)
  waiting for transfers between devices  19 us (16%)
  blocking collectives  18.9 us (16%)
  local copies, waits for them, and re-layouts  6.15 us (5%)
  other arithmetic  4.5 us (4%)
    pallas_call x5, Pallas kernels, call(): pl.pallas_call(kernel, out_shape=out_shape, in_specs=[smem] * scalars + [...  35.9 us
    ppermute x19, starting transfers between devices, send(): return lax.ppermute(value, AXES, pairs)  34.6 us
    ppermute x19, waiting for transfers between devices, send(): return lax.ppermute(value, AXES, pairs)  19 us
    all_to_all x1, blocking collectives, per_device(): lax.all_to_all(jnp.broadcast_to(mine[None], (n * nt, 1, 128)), AXES, 0, 0)  18.9 us
    unnamed x20, local copies, waits for them, and re-layouts  5.37 us
  transfers between devices with their start and end apart: 19, of which 4 were waited for; matrix products, arithmetic and copies ran while one was open for 1% of the time, Pallas kernels for 20%

profile of v6, /device:TPU:0, one launch (start us, length us, event | category | flops | bytes accessed | tf_op | source)
XLA Modules:
  0.0 120.5 jit_solution(11764918025022927128)
XLA Ops:
  2.2 4.9 %collective-permute-start.4 = (bf16[1024,128]{1,0:T(8,128)(2,1)S(1)}, bf16[1024,128]{1,0:T(8,128)(2,1)S(1)}, u32[]{:S(2)}, u32[]{:S(2)}) collective-permute-start(bf16[1024,128]{1,0:T(8,128)(2,1)S(1)} %convolution_convert_fusion), channel_id=1, source_target_pairs={{0,8},{1,12},{2,10},{3,14},{4,9},{5,13},{6,11},{7,15},{24,16},{25,... | collective-permute-start | bytes 786440 | tf_op jit(solution)/shard_map/ppermute | solution.py:253
  7.9 4.0 %collective-permute-start.6 = (bf16[1024,128]{1,0:T(8,128)(2,1)S(1)}, bf16[1024,128]{1,0:T(8,128)(2,1)S(1)}, u32[]{:S(2)}, u32[]{:S(2)}) collective-permute-start(bf16[1024,128]{1,0:T(8,128)(2,1)S(1)} %convolution_convert_fusion), channel_id=1, source_target_pairs={{0,16},{1,20},{2,18},{3,22},{4,17},{5,21},{6,19},{7,23},{24,8},{25... | collective-permute-start | bytes 786440 | tf_op jit(solution)/shard_map/ppermute | solution.py:253
  12.6 1.8 %copy-done.1 = bf16[2,256,2736]{1,2,0:T(8,128)(2,1)S(1)} copy-done((bf16[2,256,2736]{1,2,0:T(8,128)(2,1)S(1)}, bf16[2,256,2736]{1,2,0:T(8,128)(2,1)}, u32[]{:S(2)}) %copy-start.1) | copy-done | bytes 2801688
  16.1 2.1 %shard_map.77 = (bf16[3,1368,128]{2,1,0:T(8,128)(2,1)S(1)}, bf16[3,1368,128]{2,1,0:T(8,128)(2,1)S(1)}) custom-call(s32[1]{0:T(128)} %bitcast.1.upper, s32[2,128]{1,0:T(2,128)S(1)} %copy-done.3, bf16[2,2736,256]{2,1,0:T(8,128)(2,1)S(1)} %bitcast.34, bf16[2736,128]{1,0:T(8,128)(2,1)S(1)} %bitcast.35), custom_call_target="tpu_custom_call" | custom-call | flops 358612992 | bytes 3503108 | tf_op jit(solution)/shard_map/pallas_call | solution.py:217
  18.3 2.4 %collective-permute-start = (bf16[3,1368,128]{2,1,0:T(8,128)(2,1)S(1)}, bf16[3,1368,128]{2,1,0:T(8,128)(2,1)}, u32[]{:S(2)}, u32[]{:S(2)}) collective-permute-start(bf16[3,1368,128]{2,1,0:T(8,128)(2,1)S(1)} %get-tuple-element.28), channel_id=1, source_target_pairs={{0,8},{1,12},{2,10},{3,14},{4,9},{5,13},{6,11},{7,15},{24,16},{25,... | collective-permute-start | bytes 3151880 | tf_op jit(solution)/shard_map/ppermute | solution.py:253
  20.7 1.6 %collective-permute-start.1 = (bf16[3,1368,128]{2,1,0:T(8,128)(2,1)S(1)}, bf16[3,1368,128]{2,1,0:T(8,128)(2,1)}, u32[]{:S(2)}, u32[]{:S(2)}) collective-permute-start(bf16[3,1368,128]{2,1,0:T(8,128)(2,1)S(1)} %get-tuple-element.23), channel_id=1, source_target_pairs={{8,16},{9,20},{10,18},{11,22},{12,17},{13,21},{14,19},{15,23},{16,... | collective-permute-start | bytes 3151880 | tf_op jit(solution)/shard_map/ppermute | solution.py:253
  23.2 1.2 %pad_maximum_fusion.refs_0_ = bf16[4,1024,128]{2,1,0:T(8,128)(2,1)S(1)} fusion(bf16[1,1024,128]{2,1,0:T(8,128)(2,1)} %bitcast.39, bf16[1,1024,128]{2,1,0:T(8,128)(2,1)} %bitcast.38, bf16[1,1024,128]{2,1,0:T(8,128)(2,1)} %bitcast.37, bf16[1,1024,128]{2,1,0:T(8,128)(2,1)S(1)} %bitcast.36), kind=kLoop, calls=%fused_computation.5 | loop fusion | flops 1572864 | bytes 2097152 | tf_op jit(solution)/shard_map/stack | solution.py:303
  24.4 1.6 %collective-permute-start.9 = (bf16[4,1024,128]{2,1,0:T(8,128)(2,1)S(1)}, bf16[4,1024,128]{2,1,0:T(8,128)(2,1)}, u32[]{:S(2)}, u32[]{:S(2)}) collective-permute-start(bf16[4,1024,128]{2,1,0:T(8,128)(2,1)S(1)} %pad_maximum_fusion.refs_0_), channel_id=1, source_target_pairs={{0,2},{1,3},{2,0},{3,1},{4,6},{5,7},{6,4},{7,5},{8,10},{9,11},{10,... | collective-permute-start | bytes 3145736 | tf_op jit(solution)/shard_map/ppermute | solution.py:253
  26.0 14.4 %collective-permute-done.refs_0_ = bf16[3,1368,128]{2,1,0:T(8,128)(2,1)} collective-permute-done((bf16[3,1368,128]{2,1,0:T(8,128)(2,1)S(1)}, bf16[3,1368,128]{2,1,0:T(8,128)(2,1)}, u32[]{:S(2)}, u32[]{:S(2)}) %collective-permute-start) | collective-permute-done | bytes 1050656 | tf_op jit(solution)/shard_map/ppermute | solution.py:253
  40.4 4.3 %collective-permute-start.2 = (bf16[3,1368,128]{2,1,0:T(8,128)(2,1)}, bf16[3,1368,128]{2,1,0:T(8,128)(2,1)}, u32[]{:S(2)}, u32[]{:S(2)}) collective-permute-start(bf16[3,1368,128]{2,1,0:T(8,128)(2,1)} %collective-permute-done.refs_0_), channel_id=1, source_target_pairs={{0,1},{1,0},{2,3},{3,2},{4,5},{5,4},{6,7},{7,6},{8,9},{9,8},{10,11... | collective-permute-start | bytes 3151880 | tf_op jit(solution)/shard_map/ppermute | solution.py:253
  45.2 2.8 %collective-permute-done.9.refs_1_ = bf16[4,1024,128]{2,1,0:T(8,128)(2,1)} collective-permute-done((bf16[4,1024,128]{2,1,0:T(8,128)(2,1)S(1)}, bf16[4,1024,128]{2,1,0:T(8,128)(2,1)}, u32[]{:S(2)}, u32[]{:S(2)}) %collective-permute-start.9) | collective-permute-done | bytes 1048608 | tf_op jit(solution)/shard_map/ppermute | solution.py:253
  48.1 2.4 %collective-permute-start.11 = (bf16[4,1024,128]{2,1,0:T(8,128)(2,1)}, bf16[4,1024,128]{2,1,0:T(8,128)(2,1)}, u32[]{:S(2)}, u32[]{:S(2)}) collective-permute-start(bf16[4,1024,128]{2,1,0:T(8,128)(2,1)} %collective-permute-done.9.refs_1_), channel_id=1, source_target_pairs={{0,1},{1,0},{2,3},{3,2},{4,5},{5,4},{6,7},{7,6},{8,9},{9,8},{10,11... | collective-permute-start | bytes 3145736 | tf_op jit(solution)/shard_map/ppermute | solution.py:253
  51.2 5.0 %collective-permute-start.8 = (bf16[3,1368,128]{2,1,0:T(8,128)(2,1)S(1)}, bf16[3,1368,128]{2,1,0:T(8,128)(2,1)S(1)}, u32[]{:S(2)}, u32[]{:S(2)}) collective-permute-start(bf16[3,1368,128]{2,1,0:T(8,128)(2,1)S(1)} %get-tuple-element.23), channel_id=1, source_target_pairs={{0,16},{1,20},{2,18},{3,22},{4,17},{5,21},{6,19},{7,23},{24,8},{25... | collective-permute-start | bytes 3151880 | tf_op jit(solution)/shard_map/ppermute | solution.py:253
  56.3 7.0 %shard_map.78 = (f32[1368,1368]{1,0:T(8,128)S(1)}, bf16[1368,512]{1,0:T(8,128)(2,1)S(1)}) custom-call(bf16[3,1368,128]{2,1,0:T(8,128)(2,1)} %collective-permute-done.refs_0_, bf16[3,1368,128]{2,1,0:T(8,128)(2,1)} %collective-permute-done.1.refs_1_, bf16[3,1368,128]{2,1,0:T(8,128)(2,1)} %collective-permute-done.2.refs_2_, ...), custom_call_target="tpu_custom_call" | custom-call | flops 3832676352 | bytes 4202496 | tf_op jit(solution)/shard_map/pallas_call | solution.py:217
  63.3 13.0 %shard_map.79 = (bf16[512,1024]{1,0:T(8,128)(2,1)S(1)}, f32[1368,512]{1,0:T(8,128)S(1)}) custom-call(s32[2]{0:T(128)S(1)} %pad_add_fusion.where, bf16[4,1024,128]{2,1,0:T(8,128)(2,1)S(1)} %pad_maximum_fusion.refs_0_, bf16[4,1024,128]{2,1,0:T(8,128)(2,1)} %collective-permute-done.9.refs_1_, bf16[4,1024,128]{2,1,0:T(8,128)(2,1)} %collective-permute-done.10.refs_2_, ...), custom_call_target="tpu_custom_call" | custom-call | flops 9307160576 | bytes 5595144 | tf_op jit(solution)/shard_map/pallas_call | solution.py:217
  76.3 1.3 %collective-permute-start.13 = (bf16[3,1368,128]{2,1,0:T(8,128)(2,1)S(1)}, bf16[3,1368,128]{2,1,0:T(8,128)(2,1)S(1)}, u32[]{:S(2)}, u32[]{:S(2)}) collective-permute-start(bf16[3,1368,128]{2,1,0:T(8,128)(2,1)S(1)} %collective-permute-done.12.refs_0_.refs_1_), channel_id=1, source_target_pairs={{0,1},{1,0},{2,3},{3,2},{4,5},{5,4},{6,7},{7,6},{8,9},{9,8},{10,11... | collective-permute-start | bytes 3151880 | tf_op jit(solution)/shard_map/ppermute | solution.py:253
  77.6 1.5 %collective-permute-done.8.refs_0_ = bf16[3,1368,128]{2,1,0:T(8,128)(2,1)S(1)} collective-permute-done((bf16[3,1368,128]{2,1,0:T(8,128)(2,1)S(1)}, bf16[3,1368,128]{2,1,0:T(8,128)(2,1)S(1)}, u32[]{:S(2)}, u32[]{:S(2)}) %collective-permute-start.8) | collective-permute-done | bytes 1050656 | tf_op jit(solution)/shard_map/ppermute | solution.py:253
  79.9 2.4 %shard_map.80.base = f32[1368,1368]{1,0:T(8,128)S(1)} custom-call(f32[1368,1368]{1,0:T(8,128)S(1)} %get-tuple-element.27.base, bf16[3,1368,128]{2,1,0:T(8,128)(2,1)S(1)} %collective-permute-done.12.refs_0_.refs_1_, bf16[3,1368,128]{2,1,0:T(8,128)(2,1)S(1)} %collective-permute-done.13.refs_1_.refs_3_), custom_call_target="tpu_custom_call" | custom-call | flops 1916338176 | bytes 9586944 | tf_op jit(solution)/shard_map/pallas_call | solution.py:217
  82.4 11.4 %shard_map.81 = (bf16[1368,128]{1,0:T(8,128)(2,1)S(1)}, bf16[1368,128]{1,0:T(8,128)(2,1)S(1)}, bf16[1368,128]{1,0:T(8,128)(2,1)S(1)}, bf16[1368,128]{1,0:T(8,128)(2,1)S(1)}, f32[8,128]{1,0:T(8,128)S(1)}) custom-call(f32[1368,1368]{1,0:T(8,128)S(1)} %shard_map.80.base, bf16[512,1024]{1,0:T(8,128)(2,1)S(1)} %get-tuple-element.25.poly, ...), custom_call_target="tpu_custom_call" | custom-call | flops 8382578688 | bytes 16939264 | tf_op jit(solution)/shard_map/pallas_call | solution.py:217
  93.8 1.3 %collective-permute-start.15 = (bf16[1368,128]{1,0:T(8,128)(2,1)S(1)}, bf16[1368,128]{1,0:T(8,128)(2,1)S(1)}, u32[]{:S(2)}, u32[]{:S(2)}) collective-permute-start(bf16[1368,128]{1,0:T(8,128)(2,1)S(1)} %get-tuple-element.32), channel_id=1, source_target_pairs={{16,0},{20,1},{18,2},{22,3},{17,4},{21,5},{19,6},{23,7},{8,24},{12... | collective-permute-start | bytes 1050632 | tf_op jit(solution)/shard_map/ppermute | solution.py:253
  96.4 1.3 %collective-permute-start.18 = (bf16[1368,128]{1,0:T(8,128)(2,1)S(1)}, bf16[1368,128]{1,0:T(8,128)(2,1)}, u32[]{:S(2)}, u32[]{:S(2)}) collective-permute-start(bf16[1368,128]{1,0:T(8,128)(2,1)S(1)} %get-tuple-element.35), channel_id=1, source_target_pairs={{8,0},{12,1},{10,2},{14,3},{9,4},{13,5},{11,6},{15,7},{16,24},{20,... | collective-permute-start | bytes 1050632 | tf_op jit(solution)/shard_map/ppermute | solution.py:253
  97.8 18.9 %all_to_all.5 = f32[32,1,128]{2,1,0:T(1,128)S(1)} all-to-all(f32[32,1,128]{2,1,0:T(1,128)S(1)} %broadcast_in_dim.15), channel_id=1, replica_groups=mesh['shard'=8,'tensor'=4] {'shard','tensor'}, dimensions={0} | all-to-all | bytes 32768 | tf_op jit(solution)/shard_map/all_to_all | solution.py:382
  116.8 1.3 %fusion.3 = (f32[1368,128]{1,0:T(8,128)S(1)}, f32[1368,128]{1,0:T(8,128)S(1)}) fusion(bf16[1368,128]{1,0:T(8,128)(2,1)S(1)} %collective-permute-done.16, bf16[1368,128]{1,0:T(8,128)(2,1)S(1)} %collective-permute-done.15, bf16[1368,128]{1,0:T(8,128)(2,1)} %collective-permute-done.18, bf16[1368,128]{1,0:T(8,128)(2,1)S(1)} %collective-permute-done.17, pred[]{:T(512)S(6)} %ge.3), kind=kLoop, calls=%fused_computation.9 | loop fusion | flops 1400832 | bytes 2801665 | tf_op jit(solution)/shard_map/jit(_where)/select_n | solution.py:389
  118.6 1.8 %fusion.1 = (f32[128,2736]{0,1:T(8,128)}, f32[128,2736]{0,1:T(8,128)}) fusion(f32[128,2736]{0,1:T(8,128)S(1)} %copy-done.5, f32[1368,128]{1,0:T(8,128)S(1)} %get-tuple-element.39, f32[1368,128]{1,0:T(8,128)S(1)} %get-tuple-element.38, f32[]{:T(128)} %bitcast.15, f32[128,2736]{0,1:T(8,128)S(1)} %copy-done.6), kind=kLoop, calls=%fused_computation.3 | loop fusion | flops 2101248 | bytes 7004164 | tf_op jit(solution)/shard_map/transpose | solution.py:393
  (49 shorter events, 9.6 us)
Async XLA Ops:
  0.6 1.2 %copy-start = (bf16[2,256,1024]{2,1,0:T(8,128)(2,1)S(1)}, bf16[2,256,1024]{2,1,0:T(8,128)(2,1)}, u32[]{:S(2)}) copy-start(bf16[2,256,1024]{2,1,0:T(8,128)(2,1)} %param.7) | copy-start | bytes 3145732
  2.2 18.4 %collective-permute-start.4 = (bf16[1024,128]{1,0:T(8,128)(2,1)S(1)}, bf16[1024,128]{1,0:T(8,128)(2,1)S(1)}, u32[]{:S(2)}, u32[]{:S(2)}) collective-permute-start(bf16[1024,128]{1,0:T(8,128)(2,1)S(1)} %convolution_convert_fusion), channel_id=1, source_target_pairs={{0,8},{1,12},{2,10},{3,14},{4,9},{5,13},{6,11},{7,15},{24,16},{25,... | collective-permute-start | bytes 786440 | tf_op jit(solution)/shard_map/ppermute | solution.py:253
  7.2 15.1 %collective-permute-start.5 = (bf16[1024,128]{1,0:T(8,128)(2,1)S(1)}, bf16[1024,128]{1,0:T(8,128)(2,1)S(1)}, u32[]{:S(2)}, u32[]{:S(2)}) collective-permute-start(bf16[1024,128]{1,0:T(8,128)(2,1)S(1)} %convolution_convert_fusion), channel_id=1, source_target_pairs={{8,16},{9,20},{10,18},{11,22},{12,17},{13,21},{14,19},{15,23},{16,... | collective-permute-start | bytes 786440 | tf_op jit(solution)/shard_map/ppermute | solution.py:253
  7.9 14.4 %collective-permute-start.6 = (bf16[1024,128]{1,0:T(8,128)(2,1)S(1)}, bf16[1024,128]{1,0:T(8,128)(2,1)S(1)}, u32[]{:S(2)}, u32[]{:S(2)}) collective-permute-start(bf16[1024,128]{1,0:T(8,128)(2,1)S(1)} %convolution_convert_fusion), channel_id=1, source_target_pairs={{0,16},{1,20},{2,18},{3,22},{4,17},{5,21},{6,19},{7,23},{24,8},{25... | collective-permute-start | bytes 786440 | tf_op jit(solution)/shard_map/ppermute | solution.py:253
  11.9 10.4 %collective-permute-start.7 = (bf16[1024,128]{1,0:T(8,128)(2,1)S(1)}, bf16[1024,128]{1,0:T(8,128)(2,1)S(1)}, u32[]{:S(2)}, u32[]{:S(2)}) collective-permute-start(bf16[1024,128]{1,0:T(8,128)(2,1)S(1)} %convolution_convert_fusion), channel_id=1, source_target_pairs={{8,8},{9,12},{10,10},{11,14},{12,9},{13,13},{14,11},{15,15},{16,16... | collective-permute-start | bytes 786440 | tf_op jit(solution)/shard_map/ppermute | solution.py:253
  12.6 1.8 %copy-start.1 = (bf16[2,256,2736]{1,2,0:T(8,128)(2,1)S(1)}, bf16[2,256,2736]{1,2,0:T(8,128)(2,1)}, u32[]{:S(2)}) copy-start(bf16[2,256,2736]{1,2,0:T(8,128)(2,1)} %param.6) | copy-start | bytes 8404996
  18.3 29.8 %copy-start.4 = (bf16[3,1368,128]{2,1,0:T(8,128)(2,1)}, bf16[3,1368,128]{2,1,0:T(8,128)(2,1)S(1)}, u32[]{:S(2)}) copy-start(bf16[3,1368,128]{2,1,0:T(8,128)(2,1)S(1)} %get-tuple-element.28) | copy-start | bytes 3151876
  18.3 22.1 %collective-permute-start = (bf16[3,1368,128]{2,1,0:T(8,128)(2,1)S(1)}, bf16[3,1368,128]{2,1,0:T(8,128)(2,1)}, u32[]{:S(2)}, u32[]{:S(2)}) collective-permute-start(bf16[3,1368,128]{2,1,0:T(8,128)(2,1)S(1)} %get-tuple-element.28), channel_id=1, source_target_pairs={{0,8},{1,12},{2,10},{3,14},{4,9},{5,13},{6,11},{7,15},{24,16},{25,... | collective-permute-start | bytes 3151880 | tf_op jit(solution)/shard_map/ppermute | solution.py:253
  20.7 24.1 %collective-permute-start.1 = (bf16[3,1368,128]{2,1,0:T(8,128)(2,1)S(1)}, bf16[3,1368,128]{2,1,0:T(8,128)(2,1)}, u32[]{:S(2)}, u32[]{:S(2)}) collective-permute-start(bf16[3,1368,128]{2,1,0:T(8,128)(2,1)S(1)} %get-tuple-element.23), channel_id=1, source_target_pairs={{8,16},{9,20},{10,18},{11,22},{12,17},{13,21},{14,19},{15,23},{16,... | collective-permute-start | bytes 3151880 | tf_op jit(solution)/shard_map/ppermute | solution.py:253
  24.4 23.6 %collective-permute-start.9 = (bf16[4,1024,128]{2,1,0:T(8,128)(2,1)S(1)}, bf16[4,1024,128]{2,1,0:T(8,128)(2,1)}, u32[]{:S(2)}, u32[]{:S(2)}) collective-permute-start(bf16[4,1024,128]{2,1,0:T(8,128)(2,1)S(1)} %pad_maximum_fusion.refs_0_), channel_id=1, source_target_pairs={{0,2},{1,3},{2,0},{3,1},{4,6},{5,7},{6,4},{7,5},{8,10},{9,11},{10,... | collective-permute-start | bytes 3145736 | tf_op jit(solution)/shard_map/ppermute | solution.py:253
  40.4 10.8 %collective-permute-start.2 = (bf16[3,1368,128]{2,1,0:T(8,128)(2,1)}, bf16[3,1368,128]{2,1,0:T(8,128)(2,1)}, u32[]{:S(2)}, u32[]{:S(2)}) collective-permute-start(bf16[3,1368,128]{2,1,0:T(8,128)(2,1)} %collective-permute-done.refs_0_), channel_id=1, source_target_pairs={{0,1},{1,0},{2,3},{3,2},{4,5},{5,4},{6,7},{7,6},{8,9},{9,8},{10,11... | collective-permute-start | bytes 3151880 | tf_op jit(solution)/shard_map/ppermute | solution.py:253
  44.7 11.5 %collective-permute-start.3 = (bf16[3,1368,128]{2,1,0:T(8,128)(2,1)}, bf16[3,1368,128]{2,1,0:T(8,128)(2,1)}, u32[]{:S(2)}, u32[]{:S(2)}) collective-permute-start(bf16[3,1368,128]{2,1,0:T(8,128)(2,1)} %collective-permute-done.1.refs_1_), channel_id=1, source_target_pairs={{0,1},{1,0},{2,3},{3,2},{4,5},{5,4},{6,7},{7,6},{8,9},{9,8},{10,11... | collective-permute-start | bytes 3151880 | tf_op jit(solution)/shard_map/ppermute | solution.py:253
  44.7 18.6 %collective-permute-start.10 = (bf16[4,1024,128]{2,1,0:T(8,128)(2,1)S(1)}, bf16[4,1024,128]{2,1,0:T(8,128)(2,1)}, u32[]{:S(2)}, u32[]{:S(2)}) collective-permute-start(bf16[4,1024,128]{2,1,0:T(8,128)(2,1)S(1)} %pad_maximum_fusion.refs_0_), channel_id=1, source_target_pairs={{0,1},{1,0},{2,3},{3,2},{4,5},{5,4},{6,7},{7,6},{8,9},{9,8},{10,11... | collective-permute-start | bytes 3145736 | tf_op jit(solution)/shard_map/ppermute | solution.py:253
  48.1 15.2 %collective-permute-start.11 = (bf16[4,1024,128]{2,1,0:T(8,128)(2,1)}, bf16[4,1024,128]{2,1,0:T(8,128)(2,1)}, u32[]{:S(2)}, u32[]{:S(2)}) collective-permute-start(bf16[4,1024,128]{2,1,0:T(8,128)(2,1)} %collective-permute-done.9.refs_1_), channel_id=1, source_target_pairs={{0,1},{1,0},{2,3},{3,2},{4,5},{5,4},{6,7},{7,6},{8,9},{9,8},{10,11... | collective-permute-start | bytes 3145736 | tf_op jit(solution)/shard_map/ppermute | solution.py:253
  50.5 25.8 %collective-permute-start.12 = (bf16[3,1368,128]{2,1,0:T(8,128)(2,1)}, bf16[3,1368,128]{2,1,0:T(8,128)(2,1)S(1)}, u32[]{:S(2)}, u32[]{:S(2)}) collective-permute-start(bf16[3,1368,128]{2,1,0:T(8,128)(2,1)} %copy-done.4), channel_id=1, source_target_pairs={{8,8},{9,12},{10,10},{11,14},{12,9},{13,13},{14,11},{15,15},{16,16... | collective-permute-start | bytes 3151880 | tf_op jit(solution)/shard_map/ppermute | solution.py:253
  51.2 27.9 %collective-permute-start.8 = (bf16[3,1368,128]{2,1,0:T(8,128)(2,1)S(1)}, bf16[3,1368,128]{2,1,0:T(8,128)(2,1)S(1)}, u32[]{:S(2)}, u32[]{:S(2)}) collective-permute-start(bf16[3,1368,128]{2,1,0:T(8,128)(2,1)S(1)} %get-tuple-element.23), channel_id=1, source_target_pairs={{0,16},{1,20},{2,18},{3,22},{4,17},{5,21},{6,19},{7,23},{24,8},{25... | collective-permute-start | bytes 3151880 | tf_op jit(solution)/shard_map/ppermute | solution.py:253
  76.3 3.6 %collective-permute-start.13 = (bf16[3,1368,128]{2,1,0:T(8,128)(2,1)S(1)}, bf16[3,1368,128]{2,1,0:T(8,128)(2,1)S(1)}, u32[]{:S(2)}, u32[]{:S(2)}) collective-permute-start(bf16[3,1368,128]{2,1,0:T(8,128)(2,1)S(1)} %collective-permute-done.12.refs_0_.refs_1_), channel_id=1, source_target_pairs={{0,1},{1,0},{2,3},{3,2},{4,5},{5,4},{6,7},{7,6},{8,9},{9,8},{10,11... | collective-permute-start | bytes 3151880 | tf_op jit(solution)/shard_map/ppermute | solution.py:253
  79.1 3.3 %collective-permute-start.14 = (bf16[3,1368,128]{2,1,0:T(8,128)(2,1)S(1)}, bf16[3,1368,128]{2,1,0:T(8,128)(2,1)S(1)}, u32[]{:S(2)}, u32[]{:S(2)}) collective-permute-start(bf16[3,1368,128]{2,1,0:T(8,128)(2,1)S(1)} %collective-permute-done.8.refs_0_), channel_id=1, source_target_pairs={{0,1},{1,0},{2,3},{3,2},{4,5},{5,4},{6,7},{7,6},{8,9},{9,8},{10,11... | collective-permute-start | bytes 3151880 | tf_op jit(solution)/shard_map/ppermute | solution.py:253
  93.8 23.0 %collective-permute-start.15 = (bf16[1368,128]{1,0:T(8,128)(2,1)S(1)}, bf16[1368,128]{1,0:T(8,128)(2,1)S(1)}, u32[]{:S(2)}, u32[]{:S(2)}) collective-permute-start(bf16[1368,128]{1,0:T(8,128)(2,1)S(1)} %get-tuple-element.32), channel_id=1, source_target_pairs={{16,0},{20,1},{18,2},{22,3},{17,4},{21,5},{19,6},{23,7},{8,24},{12... | collective-permute-start | bytes 1050632 | tf_op jit(solution)/shard_map/ppermute | solution.py:253
  95.1 21.7 %collective-permute-start.16 = (bf16[1368,128]{1,0:T(8,128)(2,1)S(1)}, bf16[1368,128]{1,0:T(8,128)(2,1)S(1)}, u32[]{:S(2)}, u32[]{:S(2)}) collective-permute-start(bf16[1368,128]{1,0:T(8,128)(2,1)S(1)} %get-tuple-element.33), channel_id=1, source_target_pairs={{16,8},{20,9},{18,10},{22,11},{17,12},{21,13},{19,14},{23,15},{8,1... | collective-permute-start | bytes 1050632 | tf_op jit(solution)/shard_map/ppermute | solution.py:253
  95.8 21.1 %collective-permute-start.17 = (bf16[1368,128]{1,0:T(8,128)(2,1)S(1)}, bf16[1368,128]{1,0:T(8,128)(2,1)S(1)}, u32[]{:S(2)}, u32[]{:S(2)}) collective-permute-start(bf16[1368,128]{1,0:T(8,128)(2,1)S(1)} %get-tuple-element.34), channel_id=1, source_target_pairs={{8,8},{12,9},{10,10},{14,11},{9,12},{13,13},{11,14},{15,15},{16,16... | collective-permute-start | bytes 1050632 | tf_op jit(solution)/shard_map/ppermute | solution.py:253
  96.4 20.4 %collective-permute-start.18 = (bf16[1368,128]{1,0:T(8,128)(2,1)S(1)}, bf16[1368,128]{1,0:T(8,128)(2,1)}, u32[]{:S(2)}, u32[]{:S(2)}) collective-permute-start(bf16[1368,128]{1,0:T(8,128)(2,1)S(1)} %get-tuple-element.35), channel_id=1, source_target_pairs={{8,0},{12,1},{10,2},{14,3},{9,4},{13,5},{11,6},{15,7},{16,24},{20,... | collective-permute-start | bytes 1050632 | tf_op jit(solution)/shard_map/ppermute | solution.py:253
  116.8 1.5 %copy-start.5 = (f32[128,2736]{0,1:T(8,128)S(1)}, f32[128,2736]{0,1:T(8,128)}, u32[]{:S(2)}) copy-start(f32[128,2736]{0,1:T(8,128)} %param.11) | copy-start | bytes 4202500
  116.8 1.9 %copy-start.6 = (f32[128,2736]{0,1:T(8,128)S(1)}, f32[128,2736]{0,1:T(8,128)}, u32[]{:S(2)}) copy-start(f32[128,2736]{0,1:T(8,128)} %param.10) | copy-start | bytes 4202500
  (5 other events, 4.2 us)

commit v7 on v6

--- a/solution.py
+++ b/solution.py
@@ -166,7 +166,7 @@
 
 
 def act_kernel(scale, samples, update_rows, base, poly, early, taken, *refs):
-    *refs, inner, all_rows, left, wide, gram, first, second = refs
+    *refs, inner, all_rows, left, wide, gram, first, second, third = refs
     width, half = left.shape
     outs = half // update_rows
     parts, update = refs[:-outs], refs[-outs:]
@@ -192,17 +192,19 @@
     for at, size in tiles:
         rows = left[at : at + size, :].astype(jnp.float32)
         step = norm * dot_nn(gram[at : at + size, :], left[...]) + shift * rows
-        first[at : at + size, :] = 4.0 * rows - step
-    second[...] = first[...].astype(jnp.bfloat16)
+        step = 4.0 * rows - step
+        first[at : at + size, :] = step
+        second[at : at + size, :] = step.astype(jnp.bfloat16)
     total = 0.0
     for at, size in tiles:
         rows = left[at : at + size, :].astype(jnp.float32)
         step = norm * dot_nn(gram[at : at + size, :], second[...])
-        first[at : at + size, :] = step + shift * first[at : at + size, :] - 6.0 * rows
-    second[...] = first[...].astype(jnp.bfloat16)
+        step = step + shift * first[at : at + size, :] - 6.0 * rows
+        first[at : at + size, :] = step
+        third[at : at + size, :] = step.astype(jnp.bfloat16)
     for at, size in tiles:
         rows = left[at : at + size, :].astype(jnp.float32)
-        step = norm * dot_nn(gram[at : at + size, :], second[...])
+        step = norm * dot_nn(gram[at : at + size, :], third[...])
         done = step + shift * first[at : at + size, :] + 4.0 * rows
         total = total + jnp.sum(done * all_rows[at : at + size, :half].astype(jnp.float32))
         for k, out in enumerate(update):
@@ -368,6 +370,7 @@
             ((ABLK, ABLK), bf16),
             ((ABLK, half), f32),
             ((ABLK, half), bf16),
+            ((ABLK, half), bf16),
         ],
         [base, poly, left_early, taken] + tardy,
         int(2 * ABLK * (ABLK * (count // 4 + 3 * half) + half * DOUT // 2)),

time: 121 us -> 121 us (level)
  no operation moved by 1% of the time
where the time goes in v7:
time: 121 us; the launch traced here: 120 us
  Pallas kernels  35.9 us (30%)
  starting transfers between devices  34.6 us (29%)
  waiting for transfers between devices  19 us (16%)
  blocking collectives  18.9 us (16%)
  local copies, waits for them, and re-layouts  6.15 us (5%)
  other arithmetic  4.5 us (4%)
    pallas_call x5, Pallas kernels, call(): pl.pallas_call(kernel, out_shape=out_shape, in_specs=[smem] * scalars + [...  35.9 us
    ppermute x19, starting transfers between devices, send(): return lax.ppermute(value, AXES, pairs)  34.6 us
    ppermute x19, waiting for transfers between devices, send(): return lax.ppermute(value, AXES, pairs)  19 us
    all_to_all x1, blocking collectives, per_device(): lax.all_to_all(jnp.broadcast_to(mine[None], (n * nt, 1, 128)), AXES, 0, 0)  18.9 us
    unnamed x20, local copies, waits for them, and re-layouts  5.37 us
  transfers between devices with their start and end apart: 19, of which 4 were waited for; matrix products, arithmetic and copies ran while one was open for 1% of the time, Pallas kernels for 20%

profile of v7, /device:TPU:0, one launch (start us, length us, event | category | flops | bytes accessed | tf_op | source)
XLA Modules:
  0.0 120.5 jit_solution(11764918025022927128)
XLA Ops:
  2.2 4.9 %collective-permute-start.4 = (bf16[1024,128]{1,0:T(8,128)(2,1)S(1)}, bf16[1024,128]{1,0:T(8,128)(2,1)S(1)}, u32[]{:S(2)}, u32[]{:S(2)}) collective-permute-start(bf16[1024,128]{1,0:T(8,128)(2,1)S(1)} %convolution_convert_fusion), channel_id=1, source_target_pairs={{0,8},{1,12},{2,10},{3,14},{4,9},{5,13},{6,11},{7,15},{24,16},{25,... | collective-permute-start | bytes 786440 | tf_op jit(solution)/shard_map/ppermute | solution.py:255
  7.9 4.0 %collective-permute-start.6 = (bf16[1024,128]{1,0:T(8,128)(2,1)S(1)}, bf16[1024,128]{1,0:T(8,128)(2,1)S(1)}, u32[]{:S(2)}, u32[]{:S(2)}) collective-permute-start(bf16[1024,128]{1,0:T(8,128)(2,1)S(1)} %convolution_convert_fusion), channel_id=1, source_target_pairs={{0,16},{1,20},{2,18},{3,22},{4,17},{5,21},{6,19},{7,23},{24,8},{25... | collective-permute-start | bytes 786440 | tf_op jit(solution)/shard_map/ppermute | solution.py:255
  12.6 1.8 %copy-done.1 = bf16[2,256,2736]{1,2,0:T(8,128)(2,1)S(1)} copy-done((bf16[2,256,2736]{1,2,0:T(8,128)(2,1)S(1)}, bf16[2,256,2736]{1,2,0:T(8,128)(2,1)}, u32[]{:S(2)}) %copy-start.1) | copy-done | bytes 2801688
  16.1 2.1 %shard_map.77 = (bf16[3,1368,128]{2,1,0:T(8,128)(2,1)S(1)}, bf16[3,1368,128]{2,1,0:T(8,128)(2,1)S(1)}) custom-call(s32[1]{0:T(128)} %bitcast.1.upper, s32[2,128]{1,0:T(2,128)S(1)} %copy-done.3, bf16[2,2736,256]{2,1,0:T(8,128)(2,1)S(1)} %bitcast.34, bf16[2736,128]{1,0:T(8,128)(2,1)S(1)} %bitcast.35), custom_call_target="tpu_custom_call" | custom-call | flops 358612992 | bytes 3503108 | tf_op jit(solution)/shard_map/pallas_call | solution.py:219
  18.3 2.4 %collective-permute-start = (bf16[3,1368,128]{2,1,0:T(8,128)(2,1)S(1)}, bf16[3,1368,128]{2,1,0:T(8,128)(2,1)}, u32[]{:S(2)}, u32[]{:S(2)}) collective-permute-start(bf16[3,1368,128]{2,1,0:T(8,128)(2,1)S(1)} %get-tuple-element.28), channel_id=1, source_target_pairs={{0,8},{1,12},{2,10},{3,14},{4,9},{5,13},{6,11},{7,15},{24,16},{25,... | collective-permute-start | bytes 3151880 | tf_op jit(solution)/shard_map/ppermute | solution.py:255
  20.7 1.6 %collective-permute-start.1 = (bf16[3,1368,128]{2,1,0:T(8,128)(2,1)S(1)}, bf16[3,1368,128]{2,1,0:T(8,128)(2,1)}, u32[]{:S(2)}, u32[]{:S(2)}) collective-permute-start(bf16[3,1368,128]{2,1,0:T(8,128)(2,1)S(1)} %get-tuple-element.23), channel_id=1, source_target_pairs={{8,16},{9,20},{10,18},{11,22},{12,17},{13,21},{14,19},{15,23},{16,... | collective-permute-start | bytes 3151880 | tf_op jit(solution)/shard_map/ppermute | solution.py:255
  23.2 1.2 %pad_maximum_fusion.refs_0_ = bf16[4,1024,128]{2,1,0:T(8,128)(2,1)S(1)} fusion(bf16[1,1024,128]{2,1,0:T(8,128)(2,1)} %bitcast.39, bf16[1,1024,128]{2,1,0:T(8,128)(2,1)} %bitcast.38, bf16[1,1024,128]{2,1,0:T(8,128)(2,1)} %bitcast.37, bf16[1,1024,128]{2,1,0:T(8,128)(2,1)S(1)} %bitcast.36), kind=kLoop, calls=%fused_computation.5 | loop fusion | flops 1572864 | bytes 2097152 | tf_op jit(solution)/shard_map/stack | solution.py:305
  24.4 1.6 %collective-permute-start.9 = (bf16[4,1024,128]{2,1,0:T(8,128)(2,1)S(1)}, bf16[4,1024,128]{2,1,0:T(8,128)(2,1)}, u32[]{:S(2)}, u32[]{:S(2)}) collective-permute-start(bf16[4,1024,128]{2,1,0:T(8,128)(2,1)S(1)} %pad_maximum_fusion.refs_0_), channel_id=1, source_target_pairs={{0,2},{1,3},{2,0},{3,1},{4,6},{5,7},{6,4},{7,5},{8,10},{9,11},{10,... | collective-permute-start | bytes 3145736 | tf_op jit(solution)/shard_map/ppermute | solution.py:255
  26.0 14.4 %collective-permute-done.refs_0_ = bf16[3,1368,128]{2,1,0:T(8,128)(2,1)} collective-permute-done((bf16[3,1368,128]{2,1,0:T(8,128)(2,1)S(1)}, bf16[3,1368,128]{2,1,0:T(8,128)(2,1)}, u32[]{:S(2)}, u32[]{:S(2)}) %collective-permute-start) | collective-permute-done | bytes 1050656 | tf_op jit(solution)/shard_map/ppermute | solution.py:255
  40.4 4.3 %collective-permute-start.2 = (bf16[3,1368,128]{2,1,0:T(8,128)(2,1)}, bf16[3,1368,128]{2,1,0:T(8,128)(2,1)}, u32[]{:S(2)}, u32[]{:S(2)}) collective-permute-start(bf16[3,1368,128]{2,1,0:T(8,128)(2,1)} %collective-permute-done.refs_0_), channel_id=1, source_target_pairs={{0,1},{1,0},{2,3},{3,2},{4,5},{5,4},{6,7},{7,6},{8,9},{9,8},{10,11... | collective-permute-start | bytes 3151880 | tf_op jit(solution)/shard_map/ppermute | solution.py:255
  45.2 2.8 %collective-permute-done.9.refs_1_ = bf16[4,1024,128]{2,1,0:T(8,128)(2,1)} collective-permute-done((bf16[4,1024,128]{2,1,0:T(8,128)(2,1)S(1)}, bf16[4,1024,128]{2,1,0:T(8,128)(2,1)}, u32[]{:S(2)}, u32[]{:S(2)}) %collective-permute-start.9) | collective-permute-done | bytes 1048608 | tf_op jit(solution)/shard_map/ppermute | solution.py:255
  48.1 2.4 %collective-permute-start.11 = (bf16[4,1024,128]{2,1,0:T(8,128)(2,1)}, bf16[4,1024,128]{2,1,0:T(8,128)(2,1)}, u32[]{:S(2)}, u32[]{:S(2)}) collective-permute-start(bf16[4,1024,128]{2,1,0:T(8,128)(2,1)} %collective-permute-done.9.refs_1_), channel_id=1, source_target_pairs={{0,1},{1,0},{2,3},{3,2},{4,5},{5,4},{6,7},{7,6},{8,9},{9,8},{10,11... | collective-permute-start | bytes 3145736 | tf_op jit(solution)/shard_map/ppermute | solution.py:255
  51.2 5.0 %collective-permute-start.8 = (bf16[3,1368,128]{2,1,0:T(8,128)(2,1)S(1)}, bf16[3,1368,128]{2,1,0:T(8,128)(2,1)S(1)}, u32[]{:S(2)}, u32[]{:S(2)}) collective-permute-start(bf16[3,1368,128]{2,1,0:T(8,128)(2,1)S(1)} %get-tuple-element.23), channel_id=1, source_target_pairs={{0,16},{1,20},{2,18},{3,22},{4,17},{5,21},{6,19},{7,23},{24,8},{25... | collective-permute-start | bytes 3151880 | tf_op jit(solution)/shard_map/ppermute | solution.py:255
  56.3 7.0 %shard_map.78 = (f32[1368,1368]{1,0:T(8,128)S(1)}, bf16[1368,512]{1,0:T(8,128)(2,1)S(1)}) custom-call(bf16[3,1368,128]{2,1,0:T(8,128)(2,1)} %collective-permute-done.refs_0_, bf16[3,1368,128]{2,1,0:T(8,128)(2,1)} %collective-permute-done.1.refs_1_, bf16[3,1368,128]{2,1,0:T(8,128)(2,1)} %collective-permute-done.2.refs_2_, ...), custom_call_target="tpu_custom_call" | custom-call | flops 3832676352 | bytes 4202496 | tf_op jit(solution)/shard_map/pallas_call | solution.py:219
  63.3 13.0 %shard_map.79 = (bf16[512,1024]{1,0:T(8,128)(2,1)S(1)}, f32[1368,512]{1,0:T(8,128)S(1)}) custom-call(s32[2]{0:T(128)S(1)} %pad_add_fusion.where, bf16[4,1024,128]{2,1,0:T(8,128)(2,1)S(1)} %pad_maximum_fusion.refs_0_, bf16[4,1024,128]{2,1,0:T(8,128)(2,1)} %collective-permute-done.9.refs_1_, bf16[4,1024,128]{2,1,0:T(8,128)(2,1)} %collective-permute-done.10.refs_2_, ...), custom_call_target="tpu_custom_call" | custom-call | flops 9307160576 | bytes 5595144 | tf_op jit(solution)/shard_map/pallas_call | solution.py:219
  76.3 1.3 %collective-permute-start.13 = (bf16[3,1368,128]{2,1,0:T(8,128)(2,1)S(1)}, bf16[3,1368,128]{2,1,0:T(8,128)(2,1)S(1)}, u32[]{:S(2)}, u32[]{:S(2)}) collective-permute-start(bf16[3,1368,128]{2,1,0:T(8,128)(2,1)S(1)} %collective-permute-done.12.refs_0_.refs_1_), channel_id=1, source_target_pairs={{0,1},{1,0},{2,3},{3,2},{4,5},{5,4},{6,7},{7,6},{8,9},{9,8},{10,11... | collective-permute-start | bytes 3151880 | tf_op jit(solution)/shard_map/ppermute | solution.py:255
  77.6 1.5 %collective-permute-done.8.refs_0_ = bf16[3,1368,128]{2,1,0:T(8,128)(2,1)S(1)} collective-permute-done((bf16[3,1368,128]{2,1,0:T(8,128)(2,1)S(1)}, bf16[3,1368,128]{2,1,0:T(8,128)(2,1)S(1)}, u32[]{:S(2)}, u32[]{:S(2)}) %collective-permute-start.8) | collective-permute-done | bytes 1050656 | tf_op jit(solution)/shard_map/ppermute | solution.py:255
  79.9 2.4 %shard_map.80.base = f32[1368,1368]{1,0:T(8,128)S(1)} custom-call(f32[1368,1368]{1,0:T(8,128)S(1)} %get-tuple-element.27.base, bf16[3,1368,128]{2,1,0:T(8,128)(2,1)S(1)} %collective-permute-done.12.refs_0_.refs_1_, bf16[3,1368,128]{2,1,0:T(8,128)(2,1)S(1)} %collective-permute-done.13.refs_1_.refs_3_), custom_call_target="tpu_custom_call" | custom-call | flops 1916338176 | bytes 9586944 | tf_op jit(solution)/shard_map/pallas_call | solution.py:219
  82.4 11.4 %shard_map.81 = (bf16[1368,128]{1,0:T(8,128)(2,1)S(1)}, bf16[1368,128]{1,0:T(8,128)(2,1)S(1)}, bf16[1368,128]{1,0:T(8,128)(2,1)S(1)}, bf16[1368,128]{1,0:T(8,128)(2,1)S(1)}, f32[8,128]{1,0:T(8,128)S(1)}) custom-call(f32[1368,1368]{1,0:T(8,128)S(1)} %shard_map.80.base, bf16[512,1024]{1,0:T(8,128)(2,1)S(1)} %get-tuple-element.25.poly, ...), custom_call_target="tpu_custom_call" | custom-call | flops 8382578688 | bytes 16939264 | tf_op jit(solution)/shard_map/pallas_call | solution.py:219
  93.8 1.3 %collective-permute-start.15 = (bf16[1368,128]{1,0:T(8,128)(2,1)S(1)}, bf16[1368,128]{1,0:T(8,128)(2,1)S(1)}, u32[]{:S(2)}, u32[]{:S(2)}) collective-permute-start(bf16[1368,128]{1,0:T(8,128)(2,1)S(1)} %get-tuple-element.32), channel_id=1, source_target_pairs={{16,0},{20,1},{18,2},{22,3},{17,4},{21,5},{19,6},{23,7},{8,24},{12... | collective-permute-start | bytes 1050632 | tf_op jit(solution)/shard_map/ppermute | solution.py:255
  96.4 1.3 %collective-permute-start.18 = (bf16[1368,128]{1,0:T(8,128)(2,1)S(1)}, bf16[1368,128]{1,0:T(8,128)(2,1)}, u32[]{:S(2)}, u32[]{:S(2)}) collective-permute-start(bf16[1368,128]{1,0:T(8,128)(2,1)S(1)} %get-tuple-element.35), channel_id=1, source_target_pairs={{8,0},{12,1},{10,2},{14,3},{9,4},{13,5},{11,6},{15,7},{16,24},{20,... | collective-permute-start | bytes 1050632 | tf_op jit(solution)/shard_map/ppermute | solution.py:255
  97.8 18.9 %all_to_all.5 = f32[32,1,128]{2,1,0:T(1,128)S(1)} all-to-all(f32[32,1,128]{2,1,0:T(1,128)S(1)} %broadcast_in_dim.15), channel_id=1, replica_groups=mesh['shard'=8,'tensor'=4] {'shard','tensor'}, dimensions={0} | all-to-all | bytes 32768 | tf_op jit(solution)/shard_map/all_to_all | solution.py:385
  116.8 1.3 %fusion.3 = (f32[1368,128]{1,0:T(8,128)S(1)}, f32[1368,128]{1,0:T(8,128)S(1)}) fusion(bf16[1368,128]{1,0:T(8,128)(2,1)S(1)} %collective-permute-done.16, bf16[1368,128]{1,0:T(8,128)(2,1)S(1)} %collective-permute-done.15, bf16[1368,128]{1,0:T(8,128)(2,1)} %collective-permute-done.18, bf16[1368,128]{1,0:T(8,128)(2,1)S(1)} %collective-permute-done.17, pred[]{:T(512)S(6)} %ge.3), kind=kLoop, calls=%fused_computation.9 | loop fusion | flops 1400832 | bytes 2801665 | tf_op jit(solution)/shard_map/jit(_where)/select_n | solution.py:392
  118.6 1.8 %fusion.1 = (f32[128,2736]{0,1:T(8,128)}, f32[128,2736]{0,1:T(8,128)}) fusion(f32[128,2736]{0,1:T(8,128)S(1)} %copy-done.5, f32[1368,128]{1,0:T(8,128)S(1)} %get-tuple-element.39, f32[1368,128]{1,0:T(8,128)S(1)} %get-tuple-element.38, f32[]{:T(128)} %bitcast.15, f32[128,2736]{0,1:T(8,128)S(1)} %copy-done.6), kind=kLoop, calls=%fused_computation.3 | loop fusion | flops 2101248 | bytes 7004164 | tf_op jit(solution)/shard_map/transpose | solution.py:396
  (49 shorter events, 9.6 us)
Async XLA Ops:
  0.6 1.2 %copy-start = (bf16[2,256,1024]{2,1,0:T(8,128)(2,1)S(1)}, bf16[2,256,1024]{2,1,0:T(8,128)(2,1)}, u32[]{:S(2)}) copy-start(bf16[2,256,1024]{2,1,0:T(8,128)(2,1)} %param.7) | copy-start | bytes 3145732
  2.2 18.4 %collective-permute-start.4 = (bf16[1024,128]{1,0:T(8,128)(2,1)S(1)}, bf16[1024,128]{1,0:T(8,128)(2,1)S(1)}, u32[]{:S(2)}, u32[]{:S(2)}) collective-permute-start(bf16[1024,128]{1,0:T(8,128)(2,1)S(1)} %convolution_convert_fusion), channel_id=1, source_target_pairs={{0,8},{1,12},{2,10},{3,14},{4,9},{5,13},{6,11},{7,15},{24,16},{25,... | collective-permute-start | bytes 786440 | tf_op jit(solution)/shard_map/ppermute | solution.py:255
  7.2 15.1 %collective-permute-start.5 = (bf16[1024,128]{1,0:T(8,128)(2,1)S(1)}, bf16[1024,128]{1,0:T(8,128)(2,1)S(1)}, u32[]{:S(2)}, u32[]{:S(2)}) collective-permute-start(bf16[1024,128]{1,0:T(8,128)(2,1)S(1)} %convolution_convert_fusion), channel_id=1, source_target_pairs={{8,16},{9,20},{10,18},{11,22},{12,17},{13,21},{14,19},{15,23},{16,... | collective-permute-start | bytes 786440 | tf_op jit(solution)/shard_map/ppermute | solution.py:255
  7.9 14.4 %collective-permute-start.6 = (bf16[1024,128]{1,0:T(8,128)(2,1)S(1)}, bf16[1024,128]{1,0:T(8,128)(2,1)S(1)}, u32[]{:S(2)}, u32[]{:S(2)}) collective-permute-start(bf16[1024,128]{1,0:T(8,128)(2,1)S(1)} %convolution_convert_fusion), channel_id=1, source_target_pairs={{0,16},{1,20},{2,18},{3,22},{4,17},{5,21},{6,19},{7,23},{24,8},{25... | collective-permute-start | bytes 786440 | tf_op jit(solution)/shard_map/ppermute | solution.py:255
  11.9 10.4 %collective-permute-start.7 = (bf16[1024,128]{1,0:T(8,128)(2,1)S(1)}, bf16[1024,128]{1,0:T(8,128)(2,1)S(1)}, u32[]{:S(2)}, u32[]{:S(2)}) collective-permute-start(bf16[1024,128]{1,0:T(8,128)(2,1)S(1)} %convolution_convert_fusion), channel_id=1, source_target_pairs={{8,8},{9,12},{10,10},{11,14},{12,9},{13,13},{14,11},{15,15},{16,16... | collective-permute-start | bytes 786440 | tf_op jit(solution)/shard_map/ppermute | solution.py:255
  12.6 1.8 %copy-start.1 = (bf16[2,256,2736]{1,2,0:T(8,128)(2,1)S(1)}, bf16[2,256,2736]{1,2,0:T(8,128)(2,1)}, u32[]{:S(2)}) copy-start(bf16[2,256,2736]{1,2,0:T(8,128)(2,1)} %param.6) | copy-start | bytes 8404996
  18.3 29.8 %copy-start.4 = (bf16[3,1368,128]{2,1,0:T(8,128)(2,1)}, bf16[3,1368,128]{2,1,0:T(8,128)(2,1)S(1)}, u32[]{:S(2)}) copy-start(bf16[3,1368,128]{2,1,0:T(8,128)(2,1)S(1)} %get-tuple-element.28) | copy-start | bytes 3151876
  18.3 22.1 %collective-permute-start = (bf16[3,1368,128]{2,1,0:T(8,128)(2,1)S(1)}, bf16[3,1368,128]{2,1,0:T(8,128)(2,1)}, u32[]{:S(2)}, u32[]{:S(2)}) collective-permute-start(bf16[3,1368,128]{2,1,0:T(8,128)(2,1)S(1)} %get-tuple-element.28), channel_id=1, source_target_pairs={{0,8},{1,12},{2,10},{3,14},{4,9},{5,13},{6,11},{7,15},{24,16},{25,... | collective-permute-start | bytes 3151880 | tf_op jit(solution)/shard_map/ppermute | solution.py:255
  20.7 24.1 %collective-permute-start.1 = (bf16[3,1368,128]{2,1,0:T(8,128)(2,1)S(1)}, bf16[3,1368,128]{2,1,0:T(8,128)(2,1)}, u32[]{:S(2)}, u32[]{:S(2)}) collective-permute-start(bf16[3,1368,128]{2,1,0:T(8,128)(2,1)S(1)} %get-tuple-element.23), channel_id=1, source_target_pairs={{8,16},{9,20},{10,18},{11,22},{12,17},{13,21},{14,19},{15,23},{16,... | collective-permute-start | bytes 3151880 | tf_op jit(solution)/shard_map/ppermute | solution.py:255
  24.4 23.6 %collective-permute-start.9 = (bf16[4,1024,128]{2,1,0:T(8,128)(2,1)S(1)}, bf16[4,1024,128]{2,1,0:T(8,128)(2,1)}, u32[]{:S(2)}, u32[]{:S(2)}) collective-permute-start(bf16[4,1024,128]{2,1,0:T(8,128)(2,1)S(1)} %pad_maximum_fusion.refs_0_), channel_id=1, source_target_pairs={{0,2},{1,3},{2,0},{3,1},{4,6},{5,7},{6,4},{7,5},{8,10},{9,11},{10,... | collective-permute-start | bytes 3145736 | tf_op jit(solution)/shard_map/ppermute | solution.py:255
  40.4 10.8 %collective-permute-start.2 = (bf16[3,1368,128]{2,1,0:T(8,128)(2,1)}, bf16[3,1368,128]{2,1,0:T(8,128)(2,1)}, u32[]{:S(2)}, u32[]{:S(2)}) collective-permute-start(bf16[3,1368,128]{2,1,0:T(8,128)(2,1)} %collective-permute-done.refs_0_), channel_id=1, source_target_pairs={{0,1},{1,0},{2,3},{3,2},{4,5},{5,4},{6,7},{7,6},{8,9},{9,8},{10,11... | collective-permute-start | bytes 3151880 | tf_op jit(solution)/shard_map/ppermute | solution.py:255
  44.7 11.5 %collective-permute-start.3 = (bf16[3,1368,128]{2,1,0:T(8,128)(2,1)}, bf16[3,1368,128]{2,1,0:T(8,128)(2,1)}, u32[]{:S(2)}, u32[]{:S(2)}) collective-permute-start(bf16[3,1368,128]{2,1,0:T(8,128)(2,1)} %collective-permute-done.1.refs_1_), channel_id=1, source_target_pairs={{0,1},{1,0},{2,3},{3,2},{4,5},{5,4},{6,7},{7,6},{8,9},{9,8},{10,11... | collective-permute-start | bytes 3151880 | tf_op jit(solution)/shard_map/ppermute | solution.py:255
  44.7 18.6 %collective-permute-start.10 = (bf16[4,1024,128]{2,1,0:T(8,128)(2,1)S(1)}, bf16[4,1024,128]{2,1,0:T(8,128)(2,1)}, u32[]{:S(2)}, u32[]{:S(2)}) collective-permute-start(bf16[4,1024,128]{2,1,0:T(8,128)(2,1)S(1)} %pad_maximum_fusion.refs_0_), channel_id=1, source_target_pairs={{0,1},{1,0},{2,3},{3,2},{4,5},{5,4},{6,7},{7,6},{8,9},{9,8},{10,11... | collective-permute-start | bytes 3145736 | tf_op jit(solution)/shard_map/ppermute | solution.py:255
  48.1 15.2 %collective-permute-start.11 = (bf16[4,1024,128]{2,1,0:T(8,128)(2,1)}, bf16[4,1024,128]{2,1,0:T(8,128)(2,1)}, u32[]{:S(2)}, u32[]{:S(2)}) collective-permute-start(bf16[4,1024,128]{2,1,0:T(8,128)(2,1)} %collective-permute-done.9.refs_1_), channel_id=1, source_target_pairs={{0,1},{1,0},{2,3},{3,2},{4,5},{5,4},{6,7},{7,6},{8,9},{9,8},{10,11... | collective-permute-start | bytes 3145736 | tf_op jit(solution)/shard_map/ppermute | solution.py:255
  50.5 25.8 %collective-permute-start.12 = (bf16[3,1368,128]{2,1,0:T(8,128)(2,1)}, bf16[3,1368,128]{2,1,0:T(8,128)(2,1)S(1)}, u32[]{:S(2)}, u32[]{:S(2)}) collective-permute-start(bf16[3,1368,128]{2,1,0:T(8,128)(2,1)} %copy-done.4), channel_id=1, source_target_pairs={{8,8},{9,12},{10,10},{11,14},{12,9},{13,13},{14,11},{15,15},{16,16... | collective-permute-start | bytes 3151880 | tf_op jit(solution)/shard_map/ppermute | solution.py:255
  51.2 27.9 %collective-permute-start.8 = (bf16[3,1368,128]{2,1,0:T(8,128)(2,1)S(1)}, bf16[3,1368,128]{2,1,0:T(8,128)(2,1)S(1)}, u32[]{:S(2)}, u32[]{:S(2)}) collective-permute-start(bf16[3,1368,128]{2,1,0:T(8,128)(2,1)S(1)} %get-tuple-element.23), channel_id=1, source_target_pairs={{0,16},{1,20},{2,18},{3,22},{4,17},{5,21},{6,19},{7,23},{24,8},{25... | collective-permute-start | bytes 3151880 | tf_op jit(solution)/shard_map/ppermute | solution.py:255
  76.3 3.6 %collective-permute-start.13 = (bf16[3,1368,128]{2,1,0:T(8,128)(2,1)S(1)}, bf16[3,1368,128]{2,1,0:T(8,128)(2,1)S(1)}, u32[]{:S(2)}, u32[]{:S(2)}) collective-permute-start(bf16[3,1368,128]{2,1,0:T(8,128)(2,1)S(1)} %collective-permute-done.12.refs_0_.refs_1_), channel_id=1, source_target_pairs={{0,1},{1,0},{2,3},{3,2},{4,5},{5,4},{6,7},{7,6},{8,9},{9,8},{10,11... | collective-permute-start | bytes 3151880 | tf_op jit(solution)/shard_map/ppermute | solution.py:255
  79.1 3.3 %collective-permute-start.14 = (bf16[3,1368,128]{2,1,0:T(8,128)(2,1)S(1)}, bf16[3,1368,128]{2,1,0:T(8,128)(2,1)S(1)}, u32[]{:S(2)}, u32[]{:S(2)}) collective-permute-start(bf16[3,1368,128]{2,1,0:T(8,128)(2,1)S(1)} %collective-permute-done.8.refs_0_), channel_id=1, source_target_pairs={{0,1},{1,0},{2,3},{3,2},{4,5},{5,4},{6,7},{7,6},{8,9},{9,8},{10,11... | collective-permute-start | bytes 3151880 | tf_op jit(solution)/shard_map/ppermute | solution.py:255
  93.8 23.0 %collective-permute-start.15 = (bf16[1368,128]{1,0:T(8,128)(2,1)S(1)}, bf16[1368,128]{1,0:T(8,128)(2,1)S(1)}, u32[]{:S(2)}, u32[]{:S(2)}) collective-permute-start(bf16[1368,128]{1,0:T(8,128)(2,1)S(1)} %get-tuple-element.32), channel_id=1, source_target_pairs={{16,0},{20,1},{18,2},{22,3},{17,4},{21,5},{19,6},{23,7},{8,24},{12... | collective-permute-start | bytes 1050632 | tf_op jit(solution)/shard_map/ppermute | solution.py:255
  95.1 21.7 %collective-permute-start.16 = (bf16[1368,128]{1,0:T(8,128)(2,1)S(1)}, bf16[1368,128]{1,0:T(8,128)(2,1)S(1)}, u32[]{:S(2)}, u32[]{:S(2)}) collective-permute-start(bf16[1368,128]{1,0:T(8,128)(2,1)S(1)} %get-tuple-element.33), channel_id=1, source_target_pairs={{16,8},{20,9},{18,10},{22,11},{17,12},{21,13},{19,14},{23,15},{8,1... | collective-permute-start | bytes 1050632 | tf_op jit(solution)/shard_map/ppermute | solution.py:255
  95.8 21.1 %collective-permute-start.17 = (bf16[1368,128]{1,0:T(8,128)(2,1)S(1)}, bf16[1368,128]{1,0:T(8,128)(2,1)S(1)}, u32[]{:S(2)}, u32[]{:S(2)}) collective-permute-start(bf16[1368,128]{1,0:T(8,128)(2,1)S(1)} %get-tuple-element.34), channel_id=1, source_target_pairs={{8,8},{12,9},{10,10},{14,11},{9,12},{13,13},{11,14},{15,15},{16,16... | collective-permute-start | bytes 1050632 | tf_op jit(solution)/shard_map/ppermute | solution.py:255
  96.4 20.4 %collective-permute-start.18 = (bf16[1368,128]{1,0:T(8,128)(2,1)S(1)}, bf16[1368,128]{1,0:T(8,128)(2,1)}, u32[]{:S(2)}, u32[]{:S(2)}) collective-permute-start(bf16[1368,128]{1,0:T(8,128)(2,1)S(1)} %get-tuple-element.35), channel_id=1, source_target_pairs={{8,0},{12,1},{10,2},{14,3},{9,4},{13,5},{11,6},{15,7},{16,24},{20,... | collective-permute-start | bytes 1050632 | tf_op jit(solution)/shard_map/ppermute | solution.py:255
  116.8 1.5 %copy-start.5 = (f32[128,2736]{0,1:T(8,128)S(1)}, f32[128,2736]{0,1:T(8,128)}, u32[]{:S(2)}) copy-start(f32[128,2736]{0,1:T(8,128)} %param.11) | copy-start | bytes 4202500
  116.8 1.9 %copy-start.6 = (f32[128,2736]{0,1:T(8,128)S(1)}, f32[128,2736]{0,1:T(8,128)}, u32[]{:S(2)}) copy-start(f32[128,2736]{0,1:T(8,128)} %param.10) | copy-start | bytes 4202500
  (5 other events, 4.2 us)
